TPU v7x, 128 devices: a whole 4x4x4 slice. The times are simulated.
128 devices in a mesh: dp: 8 (over z, core), patch: 16 (over x, y).
Axes of the slice: x: 4, y: 4, z: 4, core: 2. Of those that a mesh axis runs over, the one named last changes fastest.
Arguments:
- patches: bfloat16 [32768, 1024], P(('dp', 'patch')), parts along dimension 0, may hold values from -20 to 20
- cls_in: float32 [8, 1024], P('dp'), parts along dimension 0, may hold values from -64 to 64
- w_attn: bfloat16 [3, 1024, 1024], replicated, may hold values from -1 to 1
- w_out: bfloat16 [1024, 1024], replicated, may hold values from -0.1875 to 0.1875
- w_class: bfloat16 [2, 4, 1024, 1024], replicated, may hold values from -1 to 1
Outputs:
- updated: bfloat16 [32768, 1024], P(('dp', 'patch')), parts along dimension 0
- cls_out: float32 [8, 1024], P('dp'), parts along dimension 0
There are 8 independent parts, one for each index of `dp`. A program takes and returns all parts, laid end to end along the dimension named above; an argument that names none is the same for every part. Nothing has to cross between parts.
All inputs are finite; a program needn't handle non-finite values.
Results may differ from a plain program's by a relative error of at most 0.015.
Values may be sent and summed in bfloat16 or wider, within the bound.
No kernel may reach another device: no remote copies, remote signals or barrier semaphores. Data moves between devices by JAX's collectives and lax.ppermute only.
A program may use at most 128 MiB of HBM per device.

v0:
```python
import jax
import jax.numpy as jnp
from jax import lax
from jax.sharding import PartitionSpec as P

HEADS = 16
HEAD_DIM = 64
CA_LAYERS = 2


def attend_local(query_all, key_all, value_all):
    row_count = query_all.shape[0]
    head_count = query_all.shape[1] // HEAD_DIM
    query_heads = query_all.reshape(row_count, head_count, HEAD_DIM)
    key_heads = key_all.reshape(row_count, head_count, HEAD_DIM)
    value_heads = value_all.reshape(row_count, head_count, HEAD_DIM)
    block_rows = 1024
    block_count = row_count // block_rows

    def one_block(block_index):
        chosen = lax.dynamic_slice_in_dim(query_heads, block_index * block_rows, block_rows, 0)
        scores = jnp.einsum("qhd,khd->hqk", chosen, key_heads, preferred_element_type=jnp.float32)
        row_max = jnp.max(scores, axis=-1, keepdims=True)
        exp_terms = jnp.exp(scores - row_max)
        row_total = jnp.sum(exp_terms, axis=-1, keepdims=True)
        probs = exp_terms.astype(jnp.bfloat16)
        outputs = jnp.einsum("hqk,khd->qhd", probs, value_heads, preferred_element_type=jnp.float32)
        return (outputs / jnp.transpose(row_total, (1, 0, 2))).astype(jnp.bfloat16)

    blocks_out = lax.map(one_block, jnp.arange(block_count, dtype=jnp.int32))
    return blocks_out.reshape(row_count, head_count * HEAD_DIM)


def per_device(patches, cls_in, w_attn, w_out, w_class):
    queries = (jnp.dot(patches, w_attn[0], preferred_element_type=jnp.float32) * 0.125).astype(
        jnp.bfloat16
    )
    key_rows = jnp.dot(patches, w_attn[1], preferred_element_type=jnp.float32).astype(jnp.bfloat16)
    value_rows = jnp.dot(patches, w_attn[2], preferred_element_type=jnp.float32).astype(
        jnp.bfloat16
    )
    query_all, key_all, value_all = (
        lax.all_to_all(queries, "patch", split_axis=1, concat_axis=0, tiled=True),
        lax.all_to_all(key_rows, "patch", split_axis=1, concat_axis=0, tiled=True),
        lax.all_to_all(value_rows, "patch", split_axis=1, concat_axis=0, tiled=True),
    )
    attended = attend_local(query_all, key_all, value_all)
    returned = lax.all_to_all(attended, "patch", split_axis=0, concat_axis=1, tiled=True)
    updated = (
        patches.astype(jnp.float32) + jnp.dot(returned, w_out, preferred_element_type=jnp.float32)
    ).astype(jnp.bfloat16)
    local_rows = patches.shape[0]
    cls_token = cls_in
    for class_index in range(CA_LAYERS):
        cls_bf16 = cls_token.astype(jnp.bfloat16)
        class_keys = jnp.dot(
            updated, w_class[class_index, 1], preferred_element_type=jnp.float32
        ).astype(jnp.bfloat16)
        class_values = jnp.dot(
            updated, w_class[class_index, 2], preferred_element_type=jnp.float32
        ).astype(jnp.bfloat16)
        class_query = (
            jnp.dot(cls_bf16, w_class[class_index, 0], preferred_element_type=jnp.float32) * 0.125
        ).astype(jnp.bfloat16)
        self_key = jnp.dot(
            cls_bf16, w_class[class_index, 1], preferred_element_type=jnp.float32
        ).reshape(HEADS, HEAD_DIM)
        self_value = jnp.dot(
            cls_bf16, w_class[class_index, 2], preferred_element_type=jnp.float32
        ).reshape(HEADS, HEAD_DIM)
        query_heads = class_query.reshape(HEADS, HEAD_DIM)
        scores = jnp.einsum(
            "hd,khd->hk",
            query_heads,
            class_keys.reshape(local_rows, HEADS, HEAD_DIM),
            preferred_element_type=jnp.float32,
        )
        value_heads = class_values.astype(jnp.float32).reshape(local_rows, HEADS, HEAD_DIM)
        local_max = jnp.max(scores, axis=1)
        row_max = lax.pmax(local_max, "patch")
        exp_terms = jnp.exp(scores - row_max[:, None])
        partial_val = jnp.einsum(
            "hk,khd->hd", exp_terms, value_heads, precision=lax.Precision.HIGHEST
        )
        row_total, weighted = lax.psum((jnp.sum(exp_terms, axis=1), partial_val), "patch")
        self_score = jnp.sum(query_heads.astype(jnp.float32) * self_key, axis=-1)
        joint_max = jnp.maximum(row_max, self_score)
        patch_scale = jnp.exp(row_max - joint_max)
        self_term = jnp.exp(self_score - joint_max)
        denominator = row_total * patch_scale + self_term
        numerator = weighted * patch_scale[:, None] + self_term[:, None] * self_value
        class_attn = (
            (numerator / denominator[:, None]).reshape(1, HEADS * HEAD_DIM).astype(jnp.bfloat16)
        )
        cls_token = cls_token + jnp.dot(
            class_attn, w_class[class_index, 3], preferred_element_type=jnp.float32
        )
    return (updated, cls_token)


def solution(mesh):
    placed = (P(("dp", "patch"), None), P("dp", None), P(), P(), P())
    return jax.shard_map(
        per_device,
        mesh=mesh,
        in_specs=placed,
        out_specs=(P(("dp", "patch"), None), P("dp", None)),
        check_vma=False,
    )
```

profile of v0, /device:TPU:0, one launch (start us, length us, event | category | flops | bytes accessed | tf_op | source)
XLA Modules:
  0.0 376.1 jit_solution(4068203428260734063)
XLA Ops:
  0.6 2.6 fusion.77
  4.3 7.1 %all-to-all-start = ((bf16[256,16,64]{0,2,1:T(8,128)(2,1)}), bf16[256,16,64]{0,2,1:T(8,128)(2,1)S(1)}, u32[]{:S(2)}, u32[]{:S(2)}) async-start(bf16[256,16,64]{0,2,1:T(8,128)(2,1)} %bitcast.9), calls=%async_computation | async-start | bytes 1048576 | tf_op jit(solution)/shard_map/all_to_all | solution.py:43
  11.4 3.1 fusion.58
  14.5 2.1 copy.44
  16.6 6.3 %all-to-all-done = bf16[256,16,64]{0,2,1:T(8,128)(2,1)S(1)} async-done(((bf16[256,16,64]{0,2,1:T(8,128)(2,1)}), bf16[256,16,64]{0,2,1:T(8,128)(2,1)S(1)}, u32[]{:S(2)}, u32[]{:S(2)}) %all-to-all-start) | async-done | bytes 524320 | tf_op jit(solution)/shard_map/all_to_all | solution.py:43
  22.9 3.6 all-to-all-start.1
  26.5 3.3 fusion.61
  29.7 2.0 copy.46
  31.8 6.1 %fusion.125 = (bf16[1,1,1024,1024]{3,2,1,0:T(8,128)(2,1)}, bf16[1,1,1024,1024]{3,2,1,0:T(8,128)(2,1)}, bf16[1,1,1024,1024]{3,2,1,0:T(8,128)(2,1)}, bf16[1,1,1024,1024]{3,2,1,0:T(8,128)(2,1)}) fusion(bf16[2,4,1024,1024]{3,2,1,0:T(8,128)(2,1)} %param.11), kind=kLoop, calls=%fused_computation.108 | loop fusion | bytes 16777216 | tf_op jit(solution)/shard_map/slice | solution.py:57
  37.9 4.0 %copy.70 = bf16[1,1,1024,1024]{2,3,1,0:T(8,128)(2,1)} copy(bf16[1,1,1024,1024]{3,2,1,0:T(8,128)(2,1)} %get-tuple-element.61) | data formatting | bytes 4194304
  41.9 7.2 %all-to-all-start.2 = ((bf16[256,16,64]{0,2,1:T(8,128)(2,1)}), bf16[256,16,64]{0,2,1:T(8,128)(2,1)}, u32[]{:S(2)}, u32[]{:S(2)}) async-start(bf16[256,16,64]{0,2,1:T(8,128)(2,1)} %bitcast.220), calls=%async_computation.2 | async-start | bytes 1048576 | tf_op jit(solution)/shard_map/all_to_all | solution.py:45
  49.1 2.1 fusion.40
  53.4 2.1 reshape.134
  56.6 1.3 reshape.135
  57.8 1.4 all-to-all-done.2
  59.2 2.1 copy.47
  62.7 110.5 %while.10 = (s32[]{:T(128)}, bf16[4,1024,1,64]{1,3,2,0:T(8,128)(2,1)}, s32[4]{0:T(128)S(1)}, bf16[4096,1,64]{0,2,1:T(8,128)(2,1)}, bf16[4096,1,64]{0,2,1:T(8,128...) while((s32[]{:T(128)}, ...), condition=%wide.region_3.4_spmd, body=%wide.region_0.3_spmd.sunk | while | flops 1094842368 | bytes 51663520 | solution.py:30
  64.1 9.0 %fusion.156 = (f32[1024]{0:T(1024)S(1)}, f32[1024,4096]{1,0:T(8,128)}) fusion(bf16[4096,1,64]{0,2,1:T(8,128)(2,1)S(1)} %get-tuple-element.132, bf16[4096,1,64]{0,2,1:T(8,128)(2,1)} %get-tuple-element.131, s32[]{:T(128)S(6)} %select_n.4), kind=kOutput, calls=%fused_computation.107.clone.1 | convolution fusion | flops 541064192 | bytes 17436676 | tf_op jit(solution)/shard_map/while/body/eval_jaxpr/qhd,khd->hqk/dot_general | solution.py:22
  73.0 8.1 %fusion.157 = f32[1024]{0:T(1024)S(1)} fusion(f32[1024,4096]{1,0:T(8,128)} %get-tuple-element.106, f32[1024]{0:T(1024)S(1)} %get-tuple-element.107), kind=kLoop, calls=%fused_computation.1.clone.1 | loop fusion | flops 8387584 | bytes 16785408 | tf_op jit(solution)/shard_map/while/body/eval_jaxpr/reduce_sum | solution.py:25
  81.1 9.2 %fusion.158 = bf16[4,1024,1,64]{1,3,2,0:T(8,128)(2,1)} fusion(bf16[4,1024,1,64]{1,3,2,0:T(8,128)(2,1)} %get-tuple-element.119, s32[]{:T(128)} %get-tuple-element.118, f32[1024,4096]{1,0:T(8,128)} %get-tuple-element.106, f32[1024]{0:T(1024)S(1)} %get-tuple-element.107, bf16[4096,1,64]{0,2,1:T(8,128)(2,1)S(1)} %get-tuple-element.133, f32[1024]{0:T(1024)S(1)} %fusion.157), kind=kOutput, calls=%fused_computation.9.clone.1 | convolution fusion | flops 545390592 | bytes 17441280 | tf_op jit(solution)/shard_map/while/body/eval_jaxpr/hqk,khd->qhd/dot_general | solution.py:27
  91.7 9.0 %fusion.156 = (f32[1024]{0:T(1024)S(1)}, f32[1024,4096]{1,0:T(8,128)}) fusion(bf16[4096,1,64]{0,2,1:T(8,128)(2,1)S(1)} %get-tuple-element.132, bf16[4096,1,64]{0,2,1:T(8,128)(2,1)} %get-tuple-element.131, s32[]{:T(128)S(6)} %select_n.4), kind=kOutput, calls=%fused_computation.107.clone.1 | convolution fusion | flops 541064192 | bytes 17436676 | tf_op jit(solution)/shard_map/while/body/eval_jaxpr/qhd,khd->hqk/dot_general | solution.py:22
  100.7 8.1 %fusion.157 = f32[1024]{0:T(1024)S(1)} fusion(f32[1024,4096]{1,0:T(8,128)} %get-tuple-element.106, f32[1024]{0:T(1024)S(1)} %get-tuple-element.107), kind=kLoop, calls=%fused_computation.1.clone.1 | loop fusion | flops 8387584 | bytes 16785408 | tf_op jit(solution)/shard_map/while/body/eval_jaxpr/reduce_sum | solution.py:25
  108.8 9.2 %fusion.158 = bf16[4,1024,1,64]{1,3,2,0:T(8,128)(2,1)} fusion(bf16[4,1024,1,64]{1,3,2,0:T(8,128)(2,1)} %get-tuple-element.119, s32[]{:T(128)} %get-tuple-element.118, f32[1024,4096]{1,0:T(8,128)} %get-tuple-element.106, f32[1024]{0:T(1024)S(1)} %get-tuple-element.107, bf16[4096,1,64]{0,2,1:T(8,128)(2,1)S(1)} %get-tuple-element.133, f32[1024]{0:T(1024)S(1)} %fusion.157), kind=kOutput, calls=%fused_computation.9.clone.1 | convolution fusion | flops 545390592 | bytes 17441280 | tf_op jit(solution)/shard_map/while/body/eval_jaxpr/hqk,khd->qhd/dot_general | solution.py:27
  119.3 9.0 %fusion.156 = (f32[1024]{0:T(1024)S(1)}, f32[1024,4096]{1,0:T(8,128)}) fusion(bf16[4096,1,64]{0,2,1:T(8,128)(2,1)S(1)} %get-tuple-element.132, bf16[4096,1,64]{0,2,1:T(8,128)(2,1)} %get-tuple-element.131, s32[]{:T(128)S(6)} %select_n.4), kind=kOutput, calls=%fused_computation.107.clone.1 | convolution fusion | flops 541064192 | bytes 17436676 | tf_op jit(solution)/shard_map/while/body/eval_jaxpr/qhd,khd->hqk/dot_general | solution.py:22
  128.3 8.1 %fusion.157 = f32[1024]{0:T(1024)S(1)} fusion(f32[1024,4096]{1,0:T(8,128)} %get-tuple-element.106, f32[1024]{0:T(1024)S(1)} %get-tuple-element.107), kind=kLoop, calls=%fused_computation.1.clone.1 | loop fusion | flops 8387584 | bytes 16785408 | tf_op jit(solution)/shard_map/while/body/eval_jaxpr/reduce_sum | solution.py:25
  136.4 9.2 %fusion.158 = bf16[4,1024,1,64]{1,3,2,0:T(8,128)(2,1)} fusion(bf16[4,1024,1,64]{1,3,2,0:T(8,128)(2,1)} %get-tuple-element.119, s32[]{:T(128)} %get-tuple-element.118, f32[1024,4096]{1,0:T(8,128)} %get-tuple-element.106, f32[1024]{0:T(1024)S(1)} %get-tuple-element.107, bf16[4096,1,64]{0,2,1:T(8,128)(2,1)S(1)} %get-tuple-element.133, f32[1024]{0:T(1024)S(1)} %fusion.157), kind=kOutput, calls=%fused_computation.9.clone.1 | convolution fusion | flops 545390592 | bytes 17441280 | tf_op jit(solution)/shard_map/while/body/eval_jaxpr/hqk,khd->qhd/dot_general | solution.py:27
  146.9 9.0 %fusion.156 = (f32[1024]{0:T(1024)S(1)}, f32[1024,4096]{1,0:T(8,128)}) fusion(bf16[4096,1,64]{0,2,1:T(8,128)(2,1)S(1)} %get-tuple-element.132, bf16[4096,1,64]{0,2,1:T(8,128)(2,1)} %get-tuple-element.131, s32[]{:T(128)S(6)} %select_n.4), kind=kOutput, calls=%fused_computation.107.clone.1 | convolution fusion | flops 541064192 | bytes 17436676 | tf_op jit(solution)/shard_map/while/body/eval_jaxpr/qhd,khd->hqk/dot_general | solution.py:22
  155.9 8.1 %fusion.157 = f32[1024]{0:T(1024)S(1)} fusion(f32[1024,4096]{1,0:T(8,128)} %get-tuple-element.106, f32[1024]{0:T(1024)S(1)} %get-tuple-element.107), kind=kLoop, calls=%fused_computation.1.clone.1 | loop fusion | flops 8387584 | bytes 16785408 | tf_op jit(solution)/shard_map/while/body/eval_jaxpr/reduce_sum | solution.py:25
  164.0 9.2 %fusion.158 = bf16[4,1024,1,64]{1,3,2,0:T(8,128)(2,1)} fusion(bf16[4,1024,1,64]{1,3,2,0:T(8,128)(2,1)} %get-tuple-element.119, s32[]{:T(128)} %get-tuple-element.118, f32[1024,4096]{1,0:T(8,128)} %get-tuple-element.106, f32[1024]{0:T(1024)S(1)} %get-tuple-element.107, bf16[4096,1,64]{0,2,1:T(8,128)(2,1)S(1)} %get-tuple-element.133, f32[1024]{0:T(1024)S(1)} %fusion.157), kind=kOutput, calls=%fused_computation.9.clone.1 | convolution fusion | flops 545390592 | bytes 17441280 | tf_op jit(solution)/shard_map/while/body/eval_jaxpr/hqk,khd->qhd/dot_general | solution.py:27
  173.2 1.4 copy.48
  175.9 5.8 %all-to-all-start.3 = ((bf16[16,256,64]{1,2,0:T(8,128)(2,1)}), bf16[16,256,64]{1,2,0:T(8,128)(2,1)S(1)}, u32[]{:S(2)}, u32[]{:S(2)}) async-start(bf16[16,256,64]{1,2,0:T(8,128)(2,1)} %copy.49), calls=%async_computation.3 | async-start | bytes 1048576 | tf_op jit(solution)/shard_map/all_to_all | solution.py:48
  181.9 4.0 %copy.71 = bf16[1,1,1024,1024]{2,3,1,0:T(8,128)(2,1)} copy(bf16[1,1,1024,1024]{3,2,1,0:T(8,128)(2,1)} %get-tuple-element.60) | data formatting | bytes 4194304
  185.8 4.0 %copy.72 = bf16[1,1,1024,1024]{2,3,1,0:T(8,128)(2,1)} copy(bf16[1,1,1024,1024]{3,2,1,0:T(8,128)(2,1)} %get-tuple-element.59) | data formatting | bytes 4194304
  189.8 4.0 %copy.73 = bf16[1,1,1024,1024]{2,3,1,0:T(8,128)(2,1)} copy(bf16[1,1,1024,1024]{3,2,1,0:T(8,128)(2,1)} %get-tuple-element.62) | data formatting | bytes 4194304
  193.8 2.5 fusion.101
  197.2 2.5 fusion.64
  199.7 3.1 fusion.67
  202.8 3.1 fusion.70
  206.5 2.5 fusion.73
  209.0 40.7 %pmax.14 = f32[16]{0:T(128)S(1)} all-reduce(f32[16]{0:T(128)S(1)} %bitcast_reduce_fusion.1), channel_id=1, replica_groups=mesh['dp'=8,'patch'=16] {'patch'}, use_global_device_ids=true, to_apply=%region_5.6 | all-reduce | flops 16 | bytes 128 | tf_op jit(solution)/shard_map/pmax | solution.py:80
  250.9 1.5 fusion.90
  252.5 36.4 %all-reduce.1 = (f32[16,64]{1,0:T(8,128)S(1)}, f32[16]{0:T(128)S(1)}) all-reduce(f32[16,64]{1,0:T(8,128)S(1)} %bitcast.232, f32[16]{0:T(128)S(1)} %get-tuple-element.65), channel_id=1, replica_groups=mesh['dp'=8,'patch'=16] {'patch'}, use_global_device_ids=true, to_apply=%region_6.7 | all-reduce | flops 1040 | bytes 8320 | tf_op jit(solution)/shard_map/psum | solution.py:85
  289.1 2.1 fusion.80
  291.2 2.0 fusion.36
  295.8 37.4 %pmax.15 = f32[16]{0:T(128)S(1)} all-reduce(f32[16]{0:T(128)S(1)} %bitcast_reduce_fusion), channel_id=1, replica_groups=mesh['dp'=8,'patch'=16] {'patch'}, use_global_device_ids=true, to_apply=%region_11.12 | all-reduce | flops 16 | bytes 128 | tf_op jit(solution)/shard_map/pmax | solution.py:80
  333.7 2.5 fusion.96
  336.8 36.5 %all-reduce = (f32[16,64]{1,0:T(8,128)S(1)}, f32[16]{0:T(128)S(1)}) all-reduce(f32[16,64]{1,0:T(8,128)S(1)} %bitcast.233, f32[16]{0:T(128)S(1)} %get-tuple-element.63), channel_id=1, replica_groups=mesh['dp'=8,'patch'=16] {'patch'}, use_global_device_ids=true, to_apply=%region_12.13 | all-reduce | flops 1040 | bytes 8320 | tf_op jit(solution)/shard_map/psum | solution.py:85
  373.5 2.6 fusion.83
  (58 shorter events, 16.2 us)
Async XLA Ops:
  0.6 195.8 %copy-start = (bf16[1024,1024]{1,0:T(8,128)(2,1)S(1)}, bf16[1024,1024]{1,0:T(8,128)(2,1)}, u32[]{:S(2)}) copy-start(bf16[1024,1024]{1,0:T(8,128)(2,1)} %param.10) | copy-start | bytes 6291460
  3.3 8.1 %copy-start.3 = (bf16[256,1024]{1,0:T(8,128)(2,1)S(1)}, bf16[256,1024]{1,0:T(8,128)(2,1)}, u32[]{:S(2)}) copy-start(bf16[256,1024]{1,0:T(8,128)(2,1)} %param.7) | copy-start | bytes 1572868
  4.3 18.6 %all-to-all-start = ((bf16[256,16,64]{0,2,1:T(8,128)(2,1)}), bf16[256,16,64]{0,2,1:T(8,128)(2,1)S(1)}, u32[]{:S(2)}, u32[]{:S(2)}) async-start(bf16[256,16,64]{0,2,1:T(8,128)(2,1)} %bitcast.9), calls=%async_computation | async-start | bytes 1048576 | tf_op jit(solution)/shard_map/all_to_all | solution.py:43
  22.9 19.0 %all-to-all-start.1 = ((bf16[256,16,64]{0,2,1:T(8,128)(2,1)}), bf16[256,16,64]{0,2,1:T(8,128)(2,1)S(1)}, u32[]{:S(2)}, u32[]{:S(2)}) async-start(bf16[256,16,64]{0,2,1:T(8,128)(2,1)} %bitcast.221), calls=%async_computation.1 | async-start | bytes 1048576 | tf_op jit(solution)/shard_map/all_to_all | solution.py:44
  37.9 11.2 %copy-start.7 = (f32[1,1024]{1,0:T(1,128)S(1)}, f32[1,1024]{1,0:T(1,128)}, u32[]{:S(2)}) copy-start(f32[1,1024]{1,0:T(1,128)} %param.8) | copy-start | bytes 12292
  41.9 17.4 %all-to-all-start.2 = ((bf16[256,16,64]{0,2,1:T(8,128)(2,1)}), bf16[256,16,64]{0,2,1:T(8,128)(2,1)}, u32[]{:S(2)}, u32[]{:S(2)}) async-start(bf16[256,16,64]{0,2,1:T(8,128)(2,1)} %bitcast.220), calls=%async_computation.2 | async-start | bytes 1048576 | tf_op jit(solution)/shard_map/all_to_all | solution.py:45
  49.1 2.2 copy-start.2
  175.9 20.5 %all-to-all-start.3 = ((bf16[16,256,64]{1,2,0:T(8,128)(2,1)}), bf16[16,256,64]{1,2,0:T(8,128)(2,1)S(1)}, u32[]{:S(2)}, u32[]{:S(2)}) async-start(bf16[16,256,64]{1,2,0:T(8,128)(2,1)} %copy.49), calls=%async_computation.3 | async-start | bytes 1048576 | tf_op jit(solution)/shard_map/all_to_all | solution.py:48
  193.7 2.7 copy-start.4
  197.1 5.7 %copy-start.5 = (bf16[256,1024]{1,0:T(8,128)(2,1)}, bf16[256,1024]{1,0:T(8,128)(2,1)S(1)}, u32[]{:S(2)}) copy-start(bf16[256,1024]{1,0:T(8,128)(2,1)S(1)} %fusion.76) | copy-start | bytes 1572868
  206.4 43.4 %copy-start.6 = (bf16[256,1024]{1,0:T(8,128)(2,1)S(1)}, bf16[256,1024]{1,0:T(8,128)(2,1)}, u32[]{:S(2)}) copy-start(bf16[256,1024]{1,0:T(8,128)(2,1)} %fusion.67) | copy-start | bytes 1572868
  289.1 4.1 %copy-start.1 = (bf16[1,1,1024,1024]{2,3,1,0:T(8,128)(2,1)S(1)}, bf16[1,1,1024,1024]{2,3,1,0:T(8,128)(2,1)}, u32[]{:S(2)}) copy-start(bf16[1,1,1024,1024]{2,3,1,0:T(8,128)(2,1)} %copy.72) | copy-start | bytes 6291460
where the time goes:
time: 378 us; the launch traced here: 376 us
  blocking collectives  151 us (40%)
  matrix products  112 us (30%)
  local copies, waits for them, and re-layouts  44.8 us (12%)
  other arithmetic  33.4 us (9%)
  starting transfers between devices  23.7 us (6%)
  waiting for transfers between devices  7.72 us (2%)
    pmax x2, blocking collectives, per_device(): row_max = lax.pmax(local_max, 'patch')  78.2 us
    psum x2, blocking collectives, per_device(): lax.psum((jnp.sum(exp_terms, axis=1), partial_val), 'patch')  72.9 us
    dot_general x4, matrix products, one_block(): jnp.einsum('hqk,khd->qhd', probs, value_heads, preferred_element_type=jnp...  36.7 us
    dot_general x4, matrix products, one_block(): jnp.einsum('qhd,khd->hqk', chosen, key_heads, preferred_element_type=jnp....  36 us
    reduce_sum x4, other arithmetic, one_block(): row_total = jnp.sum(exp_terms, axis=-1, keepdims=True)  32.4 us
    unnamed x20, local copies, waits for them, and re-layouts  16 us
  transfers between devices with their start and end apart: 4, of which 2 were waited for; matrix products, arithmetic and copies ran while one was open for 12% of the time, Pallas kernels for 0%

commit v1 on v0

v1 whole, which is shorter than its diff:
```python
import functools

import jax
import jax.numpy as jnp
from jax import lax
from jax.experimental import pallas as pl
from jax.experimental.pallas import tpu as pltpu
from jax.sharding import PartitionSpec as P

HEADS = 16
HEAD_DIM = 64
D = 1024
ROWS = 256
PATCHES = 4096
LOG2E = 1.4426950408889634
BF16 = jnp.bfloat16
F32 = jnp.float32
NN = (((1,), (0,)), ((), ()))
NT = (((1,), (1,)), ((), ()))
TN = (((0,), (0,)), ((), ()))
VMEM_LIMIT = 60 * 2**20


def dot(a, b, dims=NN):
    return lax.dot_general(a, b, dims, preferred_element_type=F32)


def whole(shape):
    return pl.BlockSpec(shape, lambda *_: (0,) * len(shape))


def class_weight(layer, kind):
    return pl.BlockSpec((1, 1, D, D), lambda *_: (layer, kind, 0, 0))


def head_mask():
    row = lax.broadcasted_iota(jnp.int32, (HEADS, D), 0)
    lane = lax.broadcasted_iota(jnp.int32, (HEADS, D), 1)
    return lane // HEAD_DIM == row


def split_rows(value):
    high = value.astype(BF16)
    low = (value - high.astype(F32)).astype(BF16)
    return jnp.concatenate([high, low], axis=0)


def fold_halves(value):
    return value[:HEADS] + value[HEADS:]


def spread(column, mask):
    return jnp.sum(jnp.where(mask, column, 0.0), axis=0, keepdims=True)


def to_tile(row):
    return jnp.concatenate([row[:, 128 * j : 128 * (j + 1)] for j in range(8)], axis=0)


def to_row(tile):
    return jnp.concatenate([tile[j : j + 1, :] for j in range(8)], axis=1)


def project_kernel(x_ref, w_ref, out_ref):
    heads_here = out_ref.shape[0]
    x = x_ref[...]
    for kind in range(3):
        y = dot(x, w_ref[kind])
        if kind == 0:
            y = y * (0.125 * LOG2E)
        yt = y.T.astype(BF16)
        for h in range(heads_here):
            out_ref[h, kind * HEAD_DIM : (kind + 1) * HEAD_DIM, :] = yt[
                h * HEAD_DIM : (h + 1) * HEAD_DIM
            ]


def project(patches, w_attn):
    steps = 4
    cols = D // steps
    return pl.pallas_call(
        project_kernel,
        grid=(steps,),
        out_shape=jax.ShapeDtypeStruct((HEADS, 3 * HEAD_DIM, ROWS), BF16),
        in_specs=[
            whole((ROWS, D)),
            pl.BlockSpec((3, D, cols), lambda i: (0, 0, i)),
        ],
        out_specs=pl.BlockSpec((HEADS // steps, 3 * HEAD_DIM, ROWS), lambda i: (i, 0, 0)),
        compiler_params=pltpu.CompilerParams(vmem_limit_bytes=VMEM_LIMIT),
        cost_estimate=pl.CostEstimate(
            flops=2 * ROWS * D * 3 * D, bytes_accessed=8 * 2**20, transcendentals=0
        ),
        name="project",
    )(patches, w_attn)


def attend_kernel(qkv_ref, out_ref, k_s, v_s, s_s, m_s):
    step = pl.program_id(0)
    chunk = 256

    @pl.when(step == 0)
    def _():
        for j in range(HEADS):
            span = slice(j * ROWS, (j + 1) * ROWS)
            k_s[span, :] = qkv_ref[j, 64:128, :].astype(F32).T.astype(BF16)
            v_s[0:64, span] = qkv_ref[j, 128:192, :]
        v_s[64:80, :] = jnp.ones((16, PATCHES), BF16)
        m_s[...] = jnp.zeros_like(m_s)
        s_s[1] = jnp.zeros((PATCHES, ROWS), F32)

    def half(now, before):
        q_t = qkv_ref[jnp.minimum(step, HEADS - 1), 0:64, :]
        top = m_s[before]
        total = jnp.zeros((80, ROWS), F32)
        tops = []
        for c in range(PATCHES // chunk):
            span = slice(c * chunk, (c + 1) * chunk)
            scores = dot(k_s[span, :], q_t)
            s_s[now, span, :] = scores
            tops.append(jnp.max(scores, axis=0, keepdims=True))
            shifted = s_s[before, span, :] - top
            probs = jnp.exp2(shifted.astype(BF16))
            total = total + dot(v_s[:, span], probs)
        m_s[now] = functools.reduce(jnp.maximum, tops)
        out_ref[jnp.maximum(step - 1, 0)] = (total[0:64] / total[64:65]).astype(BF16)

    @pl.when(step % 2 == 0)
    def _():
        half(0, 1)

    @pl.when(step % 2 == 1)
    def _():
        half(1, 0)


def attend(qkv):
    return pl.pallas_call(
        attend_kernel,
        grid=(HEADS + 1,),
        out_shape=jax.ShapeDtypeStruct((HEADS, HEAD_DIM, ROWS), BF16),
        in_specs=[whole((HEADS, 3 * HEAD_DIM, ROWS))],
        out_specs=whole((HEADS, HEAD_DIM, ROWS)),
        scratch_shapes=[
            pltpu.VMEM((PATCHES, HEAD_DIM), BF16),
            pltpu.VMEM((80, PATCHES), BF16),
            pltpu.VMEM((2, PATCHES, ROWS), F32),
            pltpu.VMEM((2, 1, ROWS), F32),
        ],
        compiler_params=pltpu.CompilerParams(vmem_limit_bytes=VMEM_LIMIT),
        cost_estimate=pl.CostEstimate(
            flops=16 * PATCHES * PATCHES * HEAD_DIM, bytes_accessed=2**21, transcendentals=PATCHES**2
        ),
        name="attend",
    )(qkv)


def self_terms(query, cls_bf16, wk, wv, mask):
    self_key = dot(cls_bf16, wk)
    self_value = dot(cls_bf16, wv)
    product = jnp.where(mask, query * self_key, 0.0)
    score = jnp.sum(product, axis=1, keepdims=True) * LOG2E
    return to_tile(self_value), to_tile(spread(score, mask))


def class_query(cls_bf16, wq):
    return (dot(cls_bf16, wq) * 0.125).astype(BF16).astype(F32)


def ahead_kernel(cls_ref, wq_ref, wk_ref, wv_ref, t_ref, self_ref):
    mask = head_mask()
    cls_bf16 = cls_ref[...].astype(BF16)
    query = class_query(cls_bf16, wq_ref[0, 0])
    spread_query = jnp.where(mask, query, 0.0).astype(BF16)
    turned = dot(spread_query, wk_ref[0, 0], NT) * LOG2E
    t_ref[...] = split_rows(turned)
    value, score = self_terms(query, cls_bf16, wk_ref[0, 0], wv_ref[0, 0], mask)
    self_ref[0:8, :] = value
    self_ref[8:16, :] = score


def ahead(cls_in, w_class):
    return pl.pallas_call(
        ahead_kernel,
        grid=(1,),
        out_shape=(
            jax.ShapeDtypeStruct((2 * HEADS, D), BF16),
            jax.ShapeDtypeStruct((16, 128), F32),
        ),
        in_specs=[whole((1, D)), class_weight(0, 0), class_weight(0, 1), class_weight(0, 2)],
        out_specs=(whole((2 * HEADS, D)), whole((16, 128))),
        compiler_params=pltpu.CompilerParams(vmem_limit_bytes=VMEM_LIMIT),
        cost_estimate=pl.CostEstimate(flops=2**28, bytes_accessed=6 * 2**20, transcendentals=0),
        name="ahead",
    )(cls_in, w_class, w_class, w_class)


def partial_out(scores, values, mask, out_ref):
    top = jnp.max(scores, axis=1, keepdims=True)
    terms = jnp.exp2(scores - top)
    total = jnp.sum(terms, axis=1, keepdims=True)
    weighted = fold_halves(dot(split_rows(terms), values)) / total
    row = jnp.sum(jnp.where(mask, weighted, 0.0), axis=0, keepdims=True)
    tile = jnp.concatenate([to_tile(row), to_tile(spread(top + jnp.log2(total), mask))], axis=0)
    for d in range(HEADS):
        out_ref[d] = tile


def combine(parts_ref, self_ref):
    top = self_ref[8:16, :]
    for d in range(HEADS):
        top = jnp.maximum(top, parts_ref[d, 8:16, :])
    weight = jnp.exp2(self_ref[8:16, :] - top)
    total = weight
    value = weight * self_ref[0:8, :]
    for d in range(HEADS):
        weight = jnp.exp2(parts_ref[d, 8:16, :] - top)
        total = total + weight
        value = value + weight * parts_ref[d, 0:8, :]
    return to_row(value / total).astype(BF16)


def update_kernel(ret_ref, x_ref, wo_ref, t_ref, wv_ref, upd_ref, part_ref):
    mask = head_mask()
    attended = ret_ref[...].reshape(D, ROWS)
    updated = (x_ref[...].astype(F32) + dot(attended, wo_ref[...], TN)).astype(BF16)
    upd_ref[...] = updated
    scores = fold_halves(dot(t_ref[...], updated, NT))
    values = dot(updated, wv_ref[0, 0]).astype(BF16)
    partial_out(scores, values, mask, part_ref)


def update(returned, patches, w_out, turned, w_class):
    return pl.pallas_call(
        update_kernel,
        grid=(1,),
        out_shape=(
            jax.ShapeDtypeStruct((ROWS, D), BF16),
            jax.ShapeDtypeStruct((HEADS, 16, 128), F32),
        ),
        in_specs=[
            whole((HEADS, HEAD_DIM, ROWS)),
            whole((ROWS, D)),
            whole((D, D)),
            whole((2 * HEADS, D)),
            class_weight(0, 2),
        ],
        out_specs=(whole((ROWS, D)), whole((HEADS, 16, 128))),
        compiler_params=pltpu.CompilerParams(vmem_limit_bytes=VMEM_LIMIT),
        cost_estimate=pl.CostEstimate(
            flops=4 * ROWS * D * D, bytes_accessed=6 * 2**20, transcendentals=0
        ),
        name="update",
    )(returned, patches, w_out, turned, w_class)


def class_kv_kernel(upd_ref, wk_ref, wv_ref, k_ref, v_ref):
    updated = upd_ref[...]
    k_ref[...] = dot(updated, wk_ref[0, 0]).astype(BF16)
    v_ref[...] = dot(updated, wv_ref[0, 0]).astype(BF16)


def class_kv(updated, w_class):
    return pl.pallas_call(
        class_kv_kernel,
        grid=(1,),
        out_shape=(jax.ShapeDtypeStruct((ROWS, D), BF16),) * 2,
        in_specs=[whole((ROWS, D)), class_weight(1, 1), class_weight(1, 2)],
        out_specs=(whole((ROWS, D)),) * 2,
        compiler_params=pltpu.CompilerParams(vmem_limit_bytes=VMEM_LIMIT),
        cost_estimate=pl.CostEstimate(
            flops=4 * ROWS * D * D, bytes_accessed=6 * 2**20, transcendentals=0
        ),
        name="class_kv",
    )(updated, w_class, w_class)


def middle_kernel(parts_ref, self_ref, cls_ref, wo_ref, wq_ref, k_ref, v_ref, cls_out_ref, q_ref, part_ref):
    mask = head_mask()
    attn = combine(parts_ref, self_ref)
    cls_token = cls_ref[...] + dot(attn, wo_ref[0, 0])
    cls_out_ref[...] = cls_token
    query = class_query(cls_token.astype(BF16), wq_ref[0, 0])
    q_ref[...] = query
    spread_query = jnp.where(mask, query, 0.0).astype(BF16)
    scores = dot(spread_query, k_ref[...], NT) * LOG2E
    partial_out(scores, v_ref[...], mask, part_ref)


def middle(parts, self_part, cls_in, w_class, keys, values):
    return pl.pallas_call(
        middle_kernel,
        grid=(1,),
        out_shape=(
            jax.ShapeDtypeStruct((1, D), F32),
            jax.ShapeDtypeStruct((1, D), F32),
            jax.ShapeDtypeStruct((HEADS, 16, 128), F32),
        ),
        in_specs=[
            whole((HEADS, 16, 128)),
            whole((16, 128)),
            whole((1, D)),
            class_weight(0, 3),
            class_weight(1, 0),
            whole((ROWS, D)),
            whole((ROWS, D)),
        ],
        out_specs=(whole((1, D)), whole((1, D)), whole((HEADS, 16, 128))),
        compiler_params=pltpu.CompilerParams(vmem_limit_bytes=VMEM_LIMIT),
        cost_estimate=pl.CostEstimate(flops=2**28, bytes_accessed=5 * 2**20, transcendentals=0),
        name="middle",
    )(parts, self_part, cls_in, w_class, w_class, keys, values)


def self_kernel(cls_ref, q_ref, wk_ref, wv_ref, self_ref):
    cls_bf16 = cls_ref[...].astype(BF16)
    value, score = self_terms(q_ref[...], cls_bf16, wk_ref[0, 0], wv_ref[0, 0], head_mask())
    self_ref[0:8, :] = value
    self_ref[8:16, :] = score


def self_part(cls_token, query, w_class):
    return pl.pallas_call(
        self_kernel,
        grid=(1,),
        out_shape=jax.ShapeDtypeStruct((16, 128), F32),
        in_specs=[whole((1, D)), whole((1, D)), class_weight(1, 1), class_weight(1, 2)],
        out_specs=whole((16, 128)),
        compiler_params=pltpu.CompilerParams(vmem_limit_bytes=VMEM_LIMIT),
        cost_estimate=pl.CostEstimate(flops=2**27, bytes_accessed=4 * 2**20, transcendentals=0),
        name="self_part",
    )(cls_token, query, w_class, w_class)


def last_kernel(parts_ref, self_ref, cls_ref, wo_ref, out_ref):
    attn = combine(parts_ref, self_ref)
    out_ref[...] = cls_ref[...] + dot(attn, wo_ref[0, 0])


def last(parts, self_terms_1, cls_token, w_class):
    return pl.pallas_call(
        last_kernel,
        grid=(1,),
        out_shape=jax.ShapeDtypeStruct((1, D), F32),
        in_specs=[whole((HEADS, 16, 128)), whole((16, 128)), whole((1, D)), class_weight(1, 3)],
        out_specs=whole((1, D)),
        compiler_params=pltpu.CompilerParams(vmem_limit_bytes=VMEM_LIMIT),
        cost_estimate=pl.CostEstimate(flops=2**27, bytes_accessed=2 * 2**20, transcendentals=0),
        name="last",
    )(parts, self_terms_1, cls_token, w_class)


def exchange(blocks):
    return lax.all_to_all(blocks, "patch", 0, 0)


def per_device(patches, cls_in, w_attn, w_out, w_class):
    qkv = exchange(project(patches, w_attn))
    turned, self_0 = ahead(cls_in, w_class)
    returned = exchange(attend(qkv))
    updated, part_0 = update(returned, patches, w_out, turned, w_class)
    parts_0 = exchange(part_0)
    keys, values = class_kv(updated, w_class)
    cls_1, query_1, part_1 = middle(parts_0, self_0, cls_in, w_class, keys, values)
    parts_1 = exchange(part_1)
    self_1 = self_part(cls_1, query_1, w_class)
    return (updated, last(parts_1, self_1, cls_1, w_class))


def solution(mesh):
    placed = (P(("dp", "patch"), None), P("dp", None), P(), P(), P())
    return jax.shard_map(
        per_device,
        mesh=mesh,
        in_specs=placed,
        out_specs=(P(("dp", "patch"), None), P("dp", None)),
        check_vma=False,
    )
```

time: 378 us -> 108 us (0.29)
  blocking collectives: 151 us -> 29.8 us
  matrix products: 112 us -> 0 us
  Pallas kernels: 0 us -> 50.9 us
  local copies, waits for them, and re-layouts: 44.8 us -> 2.11 us
  other arithmetic: 33.4 us -> 0 us
  starting transfers between devices: 23.7 us -> 11.1 us
  waiting for transfers between devices: 7.72 us -> 13.1 us
    dot_general x28 -> x0, matrix products: 112 us -> none  [the longest x4 36.7 us: one_block(): jnp.einsum('hqk,khd->qhd', probs, value_heads, preferred_element_type=jnp...]
    pmax x2 -> x0, blocking collectives: 78.2 us -> none  [per_device(): row_max = lax.pmax(local_max, 'patch')]
    psum x2 -> x0, blocking collectives: 72.9 us -> none  [per_device(): lax.psum((jnp.sum(exp_terms, axis=1), partial_val), 'patch')]
    pallas_call x0 -> x8, Pallas kernels: none -> 50.9 us  [the longest x1 19.9 us: attend(): pl.pallas_call(attend_kernel, grid=(HEADS + 1,), out_shape=jax.ShapeDtype...]
    reduce_sum x8 -> x0, other arithmetic: 33 us -> none  [the longest x4 32.4 us: one_block(): row_total = jnp.sum(exp_terms, axis=-1, keepdims=True)]
    all_to_all x0 -> x1, blocking collectives: none -> 29.8 us  [exchange(): return lax.all_to_all(blocks, 'patch', 0, 0)]
    unnamed x20 -> x6, local copies, waits for them, and re-layouts: 16 us -> 2.11 us
    all_to_all x4 -> x3, starting transfers between devices: 23.7 us -> 11.1 us  [exchange(): return lax.all_to_all(blocks, 'patch', 0, 0)]
  transfers between devices with their start and end apart: 4 -> 3, of which waited for: 2 -> 3; matrix products, arithmetic and copies ran while one was open for 12% -> 0% of each run, Pallas kernels for 0% -> 12%
where the time goes in v1:
time: 108 us
  Pallas kernels  50.9 us (47%)
  blocking collectives  29.8 us (28%)
  waiting for transfers between devices  13.1 us (12%)
  starting transfers between devices  11.1 us (10%)
  local copies, waits for them, and re-layouts  2.11 us (2%)
    all_to_all x1, blocking collectives, exchange(): return lax.all_to_all(blocks, 'patch', 0, 0)  29.8 us
    pallas_call x1, Pallas kernels, attend(): pl.pallas_call(attend_kernel, grid=(HEADS + 1,), out_shape=jax.ShapeDtype...  19.9 us
    all_to_all x3, waiting for transfers between devices, exchange(): return lax.all_to_all(blocks, 'patch', 0, 0)  13.1 us
    all_to_all x3, starting transfers between devices, exchange(): return lax.all_to_all(blocks, 'patch', 0, 0)  11.1 us
    pallas_call x1, Pallas kernels, project(): pl.pallas_call(project_kernel, grid=(steps,), out_shape=jax.ShapeDtypeStr...  6.06 us
    pallas_call x1, Pallas kernels, ahead(): pl.pallas_call(ahead_kernel, grid=(1,), out_shape=(jax.ShapeDtypeStruct((...  4.95 us
    pallas_call x1, Pallas kernels, update(): pl.pallas_call(update_kernel, grid=(1,), out_shape=(jax.ShapeDtypeStruct(...  4.89 us
    pallas_call x1, Pallas kernels, middle(): pl.pallas_call(middle_kernel, grid=(1,), out_shape=(jax.ShapeDtypeStruct(...  4.48 us
  transfers between devices with their start and end apart: 3, of which 3 were waited for; matrix products, arithmetic and copies ran while one was open for 0% of the time, Pallas kernels for 12%

profile of v1, /device:TPU:0, one launch (start us, length us, event | category | flops | bytes accessed | tf_op | source)
XLA Modules:
  0.0 107.7 jit_solution(14353798229014717695)
XLA Ops:
  0.6 6.1 %project.1 = bf16[16,192,256]{2,1,0:T(8,128)(2,1)} custom-call(bf16[256,1024]{1,0:T(8,128)(2,1)} %x_ref.3, bf16[3,1024,1024]{2,1,0:T(8,128)(2,1)} %w_ref.1), custom_call_target="tpu_custom_call" | custom-call | flops 1610612736 | bytes 8388608 | tf_op jit(solution)/shard_map/project/pallas_call | solution.py:81
  6.7 29.8 %all_to_all.20.qkv_ref = bf16[16,192,256]{2,1,0:T(8,128)(2,1)} all-to-all(bf16[16,192,256]{2,1,0:T(8,128)(2,1)} %project.1), channel_id=1, replica_groups=mesh['dp'=8,'patch'=16] {'patch'}, dimensions={0} | all-to-all | bytes 3145728 | tf_op jit(solution)/shard_map/all_to_all | solution.py:354
  36.5 19.9 %attend.1 = bf16[16,64,256]{2,1,0:T(8,128)(2,1)} custom-call(bf16[16,192,256]{2,1,0:T(8,128)(2,1)} %all_to_all.20.qkv_ref), custom_call_target="tpu_custom_call" | custom-call | flops 17179869184 | bytes 2097152 | tf_op jit(solution)/shard_map/attend/pallas_call | solution.py:138
  56.3 3.8 %all-to-all-start.1 = ((bf16[16,64,256]{2,1,0:T(8,128)(2,1)}), bf16[16,64,256]{2,1,0:T(8,128)(2,1)S(1)}, u32[]{:S(2)}, u32[]{:S(2)}) async-start(bf16[16,64,256]{2,1,0:T(8,128)(2,1)} %attend.1), calls=%async_computation.1 | async-start | bytes 1048576 | tf_op jit(solution)/shard_map/all_to_all | solution.py:354
  60.2 5.0 %ahead.1 = (bf16[32,1024]{1,0:T(8,128)(2,1)}, f32[16,128]{1,0:T(8,128)}) custom-call(f32[1,1024]{1,0:T(1,128)} %cls_ref.3, bf16[2,4,1024,1024]{3,2,1,0:T(8,128)(2,1)} %wo_ref.5, bf16[2,4,1024,1024]{3,2,1,0:T(8,128)(2,1)} %wo_ref.5, bf16[2,4,1024,1024]{3,2,1,0:T(8,128)(2,1)} %wo_ref.5), custom_call_target="tpu_custom_call" | custom-call | flops 268435456 | bytes 6291456 | tf_op jit(solution)/shard_map/ahead/pallas_call | solution.py:183
  65.1 5.4 %all-to-all-done.1.ret_ref = bf16[16,64,256]{2,1,0:T(8,128)(2,1)S(1)} async-done(((bf16[16,64,256]{2,1,0:T(8,128)(2,1)}), bf16[16,64,256]{2,1,0:T(8,128)(2,1)S(1)}, u32[]{:S(2)}, u32[]{:S(2)}) %all-to-all-start.1) | async-done | bytes 524320 | tf_op jit(solution)/shard_map/all_to_all | solution.py:354
  70.5 0.0 copy-start
  70.5 0.8 copy-done
  71.3 4.9 %update.1 = (bf16[256,1024]{1,0:T(8,128)(2,1)}, f32[16,16,128]{2,1,0:T(8,128)}) custom-call(bf16[16,64,256]{2,1,0:T(8,128)(2,1)} %copy-done, bf16[256,1024]{1,0:T(8,128)(2,1)} %x_ref.3, bf16[1024,1024]{1,0:T(8,128)(2,1)} %wo_ref.3, bf16[32,1024]{1,0:T(8,128)(2,1)} %get-tuple-element.11.t_ref, bf16[2,4,1024,1024]{3,2,1,0:T(8,128)(2,1)} %wo_ref.5), custom_call_target="tpu_custom_call" | custom-call | flops 1073741824 | bytes 6291456 | tf_op jit(solution)/shard_map/update/pallas_call | solution.py:234
  76.2 3.5 %all-to-all-start.2 = ((f32[16,16,128]{2,1,0:T(8,128)}), f32[16,16,128]{2,1,0:T(8,128)S(1)}, u32[]{:S(2)}, u32[]{:S(2)}) async-start(f32[16,16,128]{2,1,0:T(8,128)} %get-tuple-element.13), calls=%async_computation.2 | async-start | bytes 262144 | tf_op jit(solution)/shard_map/all_to_all | solution.py:354
  79.7 4.4 %class_kv.1 = (bf16[256,1024]{1,0:T(8,128)(2,1)}, bf16[256,1024]{1,0:T(8,128)(2,1)}) custom-call(bf16[256,1024]{1,0:T(8,128)(2,1)} %get-tuple-element.9.upd_ref, bf16[2,4,1024,1024]{3,2,1,0:T(8,128)(2,1)} %wo_ref.5, bf16[2,4,1024,1024]{3,2,1,0:T(8,128)(2,1)} %wo_ref.5), custom_call_target="tpu_custom_call" | custom-call | flops 1073741824 | bytes 6291456 | tf_op jit(solution)/shard_map/class_kv/pallas_call | solution.py:264
  84.2 3.3 %all-to-all-done.2.parts_ref = f32[16,16,128]{2,1,0:T(8,128)S(1)} async-done(((f32[16,16,128]{2,1,0:T(8,128)}), f32[16,16,128]{2,1,0:T(8,128)S(1)}, u32[]{:S(2)}, u32[]{:S(2)}) %all-to-all-start.2) | async-done | bytes 131104 | tf_op jit(solution)/shard_map/all_to_all | solution.py:354
  87.5 0.0 copy-start.1
  87.5 0.7 copy-done.1
  88.2 4.5 %middle.1 = (f32[1,1024]{1,0:T(1,128)}, f32[1,1024]{1,0:T(1,128)}, f32[16,16,128]{2,1,0:T(8,128)}) custom-call(f32[16,16,128]{2,1,0:T(8,128)} %copy-done.1, f32[16,128]{1,0:T(8,128)} %get-tuple-element.14.self_ref, f32[1,1024]{1,0:T(1,128)} %cls_ref.3, bf16[2,4,1024,1024]{3,2,1,0:T(8,128)(2,1)} %wo_ref.5, bf16[2,4,1024,1024]{3,2,1,0:T(8,128)(2,1)} %wo_ref.5, ...), custom_call_target="tpu_custom_call" | custom-call | flops 268435456 | bytes 5242880 | tf_op jit(solution)/shard_map/middle/pallas_call | solution.py:291
  92.7 3.8 %all-to-all-start.3 = ((f32[16,16,128]{2,1,0:T(8,128)}), f32[16,16,128]{2,1,0:T(8,128)S(1)}, u32[]{:S(2)}, u32[]{:S(2)}) async-start(f32[16,16,128]{2,1,0:T(8,128)} %get-tuple-element.17), calls=%async_computation.3 | async-start | bytes 262144 | tf_op jit(solution)/shard_map/all_to_all | solution.py:354
  96.5 3.5 %self_part.1.self_ref = f32[16,128]{1,0:T(8,128)} custom-call(f32[1,1024]{1,0:T(1,128)} %get-tuple-element.18.cls_ref, f32[1,1024]{1,0:T(1,128)} %get-tuple-element.19.q_ref, bf16[2,4,1024,1024]{3,2,1,0:T(8,128)(2,1)} %wo_ref.5, bf16[2,4,1024,1024]{3,2,1,0:T(8,128)(2,1)} %wo_ref.5), custom_call_target="tpu_custom_call" | custom-call | flops 134217728 | bytes 4194304 | tf_op jit(solution)/shard_map/self_part/pallas_call | solution.py:323
  100.0 4.3 %all-to-all-done.3.parts_ref = f32[16,16,128]{2,1,0:T(8,128)S(1)} async-done(((f32[16,16,128]{2,1,0:T(8,128)}), f32[16,16,128]{2,1,0:T(8,128)S(1)}, u32[]{:S(2)}, u32[]{:S(2)}) %all-to-all-start.3) | async-done | bytes 131104 | tf_op jit(solution)/shard_map/all_to_all | solution.py:354
  104.3 0.0 copy-start.2
  104.3 0.6 copy-done.2
  105.0 2.7 %last.1 = f32[1,1024]{1,0:T(1,128)} custom-call(f32[16,16,128]{2,1,0:T(8,128)} %copy-done.2, f32[16,128]{1,0:T(8,128)} %self_part.1.self_ref, f32[1,1024]{1,0:T(1,128)} %get-tuple-element.18.cls_ref, bf16[2,4,1024,1024]{3,2,1,0:T(8,128)(2,1)} %wo_ref.5), custom_call_target="tpu_custom_call" | custom-call | flops 134217728 | bytes 2097152 | tf_op jit(solution)/shard_map/last/pallas_call | solution.py:341
Async XLA Ops:
  56.3 14.2 %all-to-all-start.1 = ((bf16[16,64,256]{2,1,0:T(8,128)(2,1)}), bf16[16,64,256]{2,1,0:T(8,128)(2,1)S(1)}, u32[]{:S(2)}, u32[]{:S(2)}) async-start(bf16[16,64,256]{2,1,0:T(8,128)(2,1)} %attend.1), calls=%async_computation.1 | async-start | bytes 1048576 | tf_op jit(solution)/shard_map/all_to_all | solution.py:354
  70.5 0.8 copy-start
  76.2 11.3 %all-to-all-start.2 = ((f32[16,16,128]{2,1,0:T(8,128)}), f32[16,16,128]{2,1,0:T(8,128)S(1)}, u32[]{:S(2)}, u32[]{:S(2)}) async-start(f32[16,16,128]{2,1,0:T(8,128)} %get-tuple-element.13), calls=%async_computation.2 | async-start | bytes 262144 | tf_op jit(solution)/shard_map/all_to_all | solution.py:354
  87.5 0.7 copy-start.1
  92.7 11.7 %all-to-all-start.3 = ((f32[16,16,128]{2,1,0:T(8,128)}), f32[16,16,128]{2,1,0:T(8,128)S(1)}, u32[]{:S(2)}, u32[]{:S(2)}) async-start(f32[16,16,128]{2,1,0:T(8,128)} %get-tuple-element.17), calls=%async_computation.3 | async-start | bytes 262144 | tf_op jit(solution)/shard_map/all_to_all | solution.py:354
  104.3 0.7 copy-start.2

commit v2 on v1

v2 whole, which is shorter than its diff:
```python
import functools

import jax
import jax.numpy as jnp
from jax import lax
from jax.experimental import pallas as pl
from jax.experimental.pallas import tpu as pltpu
from jax.sharding import PartitionSpec as P

HEADS = 16
HEAD_DIM = 64
D = 1024
ROWS = 256
PATCHES = 4096
LOG2E = 1.4426950408889634
BF16 = jnp.bfloat16
F32 = jnp.float32
NN = (((1,), (0,)), ((), ()))
NT = (((1,), (1,)), ((), ()))
TN = (((0,), (0,)), ((), ()))
VMEM_LIMIT = 20 * 2**20
SMALL_LIMIT = 16 * 2**20
LARGE_LIMIT = 52 * 2**20


def dot(a, b, dims=NN):
    return lax.dot_general(a, b, dims, preferred_element_type=F32)


RESIDENT = pl.BlockSpec(memory_space=pltpu.VMEM)
ANYWHERE = pl.BlockSpec(memory_space=pl.ANY)


def call(kernel, name, flops, out_shape, resident, remote=(), scratch=(), hbm_out=0):
    single = not isinstance(out_shape, tuple)
    count = 1 if single else len(out_shape)
    out_specs = (ANYWHERE,) * hbm_out + (RESIDENT,) * (count - hbm_out)
    return pl.pallas_call(
        kernel,
        out_shape=out_shape,
        in_specs=[RESIDENT] * len(resident) + [ANYWHERE] * len(remote),
        out_specs=out_specs[0] if single else out_specs,
        scratch_shapes=scratch,
        compiler_params=pltpu.CompilerParams(
            vmem_limit_bytes=LARGE_LIMIT if remote else SMALL_LIMIT
        ),
        cost_estimate=pl.CostEstimate(flops=flops, bytes_accessed=2**20, transcendentals=0),
        name=name,
    )(*resident, *remote)


SQUARE = pltpu.VMEM((D, D), BF16)


def head_mask():
    row = lax.broadcasted_iota(jnp.int32, (HEADS, D), 0)
    lane = lax.broadcasted_iota(jnp.int32, (HEADS, D), 1)
    return lane // HEAD_DIM == row


def split_rows(value):
    high = value.astype(BF16)
    low = (value - high.astype(F32)).astype(BF16)
    return jnp.concatenate([high, low], axis=0)


def fold_halves(value):
    return value[:HEADS] + value[HEADS:]


def spread(column, mask):
    return jnp.sum(jnp.where(mask, column, 0.0), axis=0, keepdims=True)


def to_tile(row):
    return jnp.concatenate([row[:, 128 * j : 128 * (j + 1)] for j in range(8)], axis=0)


def to_row(tile):
    return jnp.concatenate([tile[j : j + 1, :] for j in range(8)], axis=1)


def project_kernel(x_hbm, w_hbm, out_ref, x_s, w_s, x_sem, w_sem):
    x_copy = pltpu.make_async_copy(x_hbm, x_s, x_sem)
    copies = [pltpu.make_async_copy(w_hbm.at[k], w_s.at[k], w_sem.at[k]) for k in range(3)]
    x_copy.start()
    for copy in copies:
        copy.start()
    x_copy.wait()
    x = x_s[...]
    for kind in range(3):
        copies[kind].wait()
        y = dot(x, w_s[kind])
        if kind == 0:
            y = y * (0.125 * LOG2E)
        yt = y.astype(BF16).T
        for h in range(HEADS):
            out_ref[h, kind * HEAD_DIM : (kind + 1) * HEAD_DIM, :] = yt[
                h * HEAD_DIM : (h + 1) * HEAD_DIM
            ]


def project(patches, w_attn):
    return pl.pallas_call(
        project_kernel,
        out_shape=jax.ShapeDtypeStruct((HEADS, 3 * HEAD_DIM, ROWS), BF16),
        in_specs=[ANYWHERE] * 2,
        out_specs=RESIDENT,
        scratch_shapes=[
            pltpu.VMEM((ROWS, D), BF16),
            pltpu.VMEM((3, D, D), BF16),
            pltpu.SemaphoreType.DMA(()),
            pltpu.SemaphoreType.DMA((3,)),
        ],
        compiler_params=pltpu.CompilerParams(vmem_limit_bytes=62 * 2**20),
        cost_estimate=pl.CostEstimate(
            flops=2 * ROWS * D * 3 * D, bytes_accessed=8 * 2**20, transcendentals=0
        ),
        name="project",
    )(patches, w_attn)


CHUNK = 256
SPANS = [slice(c * CHUNK, (c + 1) * CHUNK) for c in range(PATCHES // CHUNK)]


def attend_kernel(qkv_ref, out_ref, k_s, v_s, s_s):
    for j, span in enumerate(SPANS):
        k_s[span, :] = qkv_ref[j, 64:128, :].T
        v_s[0:64, span] = qkv_ref[j, 128:192, :]
    v_s[64:80, :] = jnp.ones((16, PATCHES), BF16)

    def scores_of(q_t, span, now):
        scores = dot(k_s[span, :], q_t)
        s_s[now, span, :] = scores
        return jnp.max(scores, axis=0, keepdims=True)

    def weigh(span, before, top):
        probs = jnp.exp2((s_s[before, span, :] - top).astype(BF16))
        return dot(v_s[:, span], probs)

    def finish(block, total):
        out_ref[block] = (total[0:64] / total[64:65]).astype(BF16)

    def both(block, now, top):
        q_t = qkv_ref[block, 0:64, :]
        total = jnp.zeros((80, ROWS), F32)
        tops = []
        for span in SPANS:
            tops.append(scores_of(q_t, span, now))
            total = total + weigh(span, 1 - now, top)
        finish(block - 1, total)
        return functools.reduce(jnp.maximum, tops)

    def pair(t, top):
        top = both(2 * t + 1, 1, top)
        return both(2 * t + 2, 0, top)

    q_t = qkv_ref[0, 0:64, :]
    top = functools.reduce(jnp.maximum, [scores_of(q_t, span, 0) for span in SPANS])
    top = lax.fori_loop(0, 7, pair, top)
    top = both(15, 1, top)
    total = jnp.zeros((80, ROWS), F32)
    for span in SPANS:
        total = total + weigh(span, 1, top)
    finish(15, total)


def attend(qkv):
    return pl.pallas_call(
        attend_kernel,
        out_shape=jax.ShapeDtypeStruct((HEADS, HEAD_DIM, ROWS), BF16),
        in_specs=[RESIDENT],
        out_specs=RESIDENT,
        scratch_shapes=[
            pltpu.VMEM((PATCHES, HEAD_DIM), BF16),
            pltpu.VMEM((80, PATCHES), BF16),
            pltpu.VMEM((2, PATCHES, ROWS), F32),
        ],
        compiler_params=pltpu.CompilerParams(vmem_limit_bytes=VMEM_LIMIT),
        cost_estimate=pl.CostEstimate(
            flops=16 * PATCHES * PATCHES * HEAD_DIM, bytes_accessed=2**21, transcendentals=PATCHES**2
        ),
        name="attend",
    )(qkv)


def self_terms(query, cls_bf16, wk, wv, mask):
    self_key = dot(cls_bf16, wk)
    self_value = dot(cls_bf16, wv)
    product = jnp.where(mask, query * self_key, 0.0)
    score = jnp.sum(product, axis=1, keepdims=True) * LOG2E
    return to_tile(self_value), to_tile(spread(score, mask))


def class_query(cls_bf16, wq):
    return (dot(cls_bf16, wq) * 0.125).astype(BF16).astype(F32)


def start_copies(copies):
    copies = [pltpu.make_async_copy(*copy) for copy in copies]
    for copy in copies:
        copy.start()
    return copies


PIECES = 4
PIECE = D // PIECES


def stream(w_hbm, w_s, sems):
    cut = [slice(PIECE * p, PIECE * (p + 1)) for p in range(PIECES)]
    return start_copies([(w_hbm.at[c], w_s.at[c], sems.at[p]) for p, c in enumerate(cut)])


def dot_streamed(a, w_s, copies, turned=False):
    total = None
    for p, copy in enumerate(copies):
        cut = slice(PIECE * p, PIECE * (p + 1))
        copy.wait()
        part = dot(a[cut, :], w_s[cut, :], TN) if turned else dot(a[:, cut], w_s[cut, :])
        total = part if total is None else total + part
    return total


def ahead_kernel(cls_ref, w_hbm, t_ref, self_ref, wq_s, wk_s, wv_s, sems):
    copies = start_copies([(w_hbm.at[0, k], ref, sems.at[k]) for k, ref in enumerate((wq_s, wk_s, wv_s))])
    mask = head_mask()
    cls_bf16 = cls_ref[...].astype(BF16)
    copies[0].wait()
    query = class_query(cls_bf16, wq_s[...])
    spread_query = jnp.where(mask, query, 0.0).astype(BF16)
    copies[1].wait()
    turned = dot(spread_query, wk_s[...], NT) * LOG2E
    t_ref[...] = split_rows(turned)
    copies[2].wait()
    value, score = self_terms(query, cls_bf16, wk_s[...], wv_s[...], mask)
    self_ref[0:8, :] = value
    self_ref[8:16, :] = score


def ahead(cls_in, w_class):
    shapes = (jax.ShapeDtypeStruct((2 * HEADS, D), BF16), jax.ShapeDtypeStruct((16, 128), F32))
    scratch = (SQUARE, SQUARE, SQUARE, pltpu.SemaphoreType.DMA((3,)))
    return call(ahead_kernel, "ahead", 2**30, shapes, (cls_in,), (w_class,), scratch)


def partial_out(scores, values, mask, out_ref):
    top = jnp.max(scores, axis=1, keepdims=True)
    terms = jnp.exp2(scores - top)
    total = jnp.sum(terms, axis=1, keepdims=True)
    weighted = fold_halves(dot(split_rows(terms), values)) / total
    row = jnp.sum(jnp.where(mask, weighted, 0.0), axis=0, keepdims=True)
    tile = jnp.concatenate([to_tile(row), to_tile(spread(top + jnp.log2(total), mask))], axis=0)
    for d in range(HEADS):
        out_ref[d] = tile


def combine(parts_ref, self_ref):
    top = self_ref[8:16, :]
    for d in range(HEADS):
        top = jnp.maximum(top, parts_ref[d, 8:16, :])
    weight = jnp.exp2(self_ref[8:16, :] - top)
    total = weight
    value = weight * self_ref[0:8, :]
    for d in range(HEADS):
        weight = jnp.exp2(parts_ref[d, 8:16, :] - top)
        total = total + weight
        value = value + weight * parts_ref[d, 0:8, :]
    return to_row(value / total).astype(BF16)


def update_kernel(ret_ref, x_ref, t_ref, wo_hbm, w_hbm, upd_hbm, upd_ref, part_ref, wo_s, wv_s, sems, sem):
    wo_copies = stream(wo_hbm, wo_s, sems.at[0])
    wv_copies = stream(w_hbm.at[0, 2], wv_s, sems.at[1])
    mask = head_mask()
    attended = ret_ref[...].reshape(D, ROWS)
    added = dot_streamed(attended, wo_s, wo_copies, turned=True)
    updated = (x_ref[...].astype(F32) + added).astype(BF16)
    upd_ref[...] = updated
    (out_copy,) = start_copies([(upd_ref, upd_hbm, sem)])
    scores = fold_halves(dot(t_ref[...], updated, NT))
    for copy in wv_copies:
        copy.wait()
    values = dot(updated, wv_s[...]).astype(BF16)
    partial_out(scores, values, mask, part_ref)
    out_copy.wait()


def update(returned, patches, w_out, turned, w_class):
    shapes = (
        jax.ShapeDtypeStruct((ROWS, D), BF16),
        jax.ShapeDtypeStruct((ROWS, D), BF16),
        jax.ShapeDtypeStruct((HEADS, 16, 128), F32),
    )
    scratch = (SQUARE, SQUARE, pltpu.SemaphoreType.DMA((2, PIECES)), pltpu.SemaphoreType.DMA(()))
    args = (returned, patches, turned)
    return call(update_kernel, "update", 4 * ROWS * D * D, shapes, args, (w_out, w_class), scratch, 1)


def class_kv_kernel(upd_ref, w_hbm, k_ref, v_ref, wk_s, wv_s, sems):
    copies = start_copies([(w_hbm.at[1, 1], wk_s, sems.at[0]), (w_hbm.at[1, 2], wv_s, sems.at[1])])
    updated = upd_ref[...]
    copies[0].wait()
    k_ref[...] = dot(updated, wk_s[...]).astype(BF16)
    copies[1].wait()
    v_ref[...] = dot(updated, wv_s[...]).astype(BF16)


def class_kv(updated, w_class):
    shapes = (jax.ShapeDtypeStruct((ROWS, D), BF16),) * 2
    scratch = (SQUARE, SQUARE, pltpu.SemaphoreType.DMA((2,)))
    return call(class_kv_kernel, "class_kv", 2**31, shapes, (updated,), (w_class,), scratch)


def middle_kernel(
    parts_ref, self_ref, cls_ref, k_ref, v_ref, w_hbm, cls_out_ref, q_ref, part_ref, wo_s, wq_s, sems
):
    wo_copies = stream(w_hbm.at[0, 3], wo_s, sems.at[0])
    wq_copies = stream(w_hbm.at[1, 0], wq_s, sems.at[1])
    mask = head_mask()
    attn = combine(parts_ref, self_ref)
    cls_token = cls_ref[...] + dot_streamed(attn, wo_s, wo_copies)
    cls_out_ref[...] = cls_token
    query = (dot_streamed(cls_token.astype(BF16), wq_s, wq_copies) * 0.125).astype(BF16).astype(F32)
    q_ref[...] = query
    spread_query = jnp.where(mask, query, 0.0).astype(BF16)
    scores = dot(spread_query, k_ref[...], NT) * LOG2E
    partial_out(scores, v_ref[...], mask, part_ref)


def middle(parts, self_part, cls_in, keys, values, w_class):
    shapes = (
        jax.ShapeDtypeStruct((1, D), F32),
        jax.ShapeDtypeStruct((1, D), F32),
        jax.ShapeDtypeStruct((HEADS, 16, 128), F32),
    )
    args = (parts, self_part, cls_in, keys, values)
    scratch = (SQUARE, SQUARE, pltpu.SemaphoreType.DMA((2, PIECES)))
    return call(middle_kernel, "middle", 2**28, shapes, args, (w_class,), scratch)


def self_kernel(cls_ref, q_ref, w_hbm, self_ref, wk_s, wv_s, sems):
    copies = start_copies([(w_hbm.at[1, 1], wk_s, sems.at[0]), (w_hbm.at[1, 2], wv_s, sems.at[1])])
    cls_bf16 = cls_ref[...].astype(BF16)
    for copy in copies:
        copy.wait()
    value, score = self_terms(q_ref[...], cls_bf16, wk_s[...], wv_s[...], head_mask())
    self_ref[0:8, :] = value
    self_ref[8:16, :] = score


def self_part(cls_token, query, w_class):
    shape = jax.ShapeDtypeStruct((16, 128), F32)
    scratch = (SQUARE, SQUARE, pltpu.SemaphoreType.DMA((2,)))
    return call(self_kernel, "self_part", 2**30, shape, (cls_token, query), (w_class,), scratch)


def last_kernel(parts_ref, self_ref, cls_ref, w_hbm, out_ref, wo_s, sems):
    wo_copies = stream(w_hbm.at[1, 3], wo_s, sems)
    attn = combine(parts_ref, self_ref)
    out_ref[...] = cls_ref[...] + dot_streamed(attn, wo_s, wo_copies)


def last(parts, self_terms_1, cls_token, w_class):
    shape = jax.ShapeDtypeStruct((1, D), F32)
    scratch = (SQUARE, pltpu.SemaphoreType.DMA((PIECES,)))
    args = (parts, self_terms_1, cls_token)
    return call(last_kernel, "last", 2**27, shape, args, (w_class,), scratch)


def exchange(blocks):
    return lax.all_to_all(blocks, "patch", 0, 0)


def per_device(patches, cls_in, w_attn, w_out, w_class):
    qkv = exchange(project(patches, w_attn))
    turned, self_0 = ahead(cls_in, w_class)
    returned = exchange(attend(qkv))
    updated, updated_here, part_0 = update(returned, patches, w_out, turned, w_class)
    parts_0 = exchange(part_0)
    keys, values = class_kv(updated_here, w_class)
    cls_1, query_1, part_1 = middle(parts_0, self_0, cls_in, keys, values, w_class)
    parts_1 = exchange(part_1)
    self_1 = self_part(cls_1, query_1, w_class)
    return (updated, last(parts_1, self_1, cls_1, w_class))


def solution(mesh):
    placed = (P(("dp", "patch"), None), P("dp", None), P(), P(), P())
    return jax.shard_map(
        per_device,
        mesh=mesh,
        in_specs=placed,
        out_specs=(P(("dp", "patch"), None), P("dp", None)),
        check_vma=False,
    )
```

time: 108 us -> 102 us (0.944)
  Pallas kernels: 50.9 us -> 44 us
  waiting for transfers between devices: 13.1 us -> 16.4 us
  local copies, waits for them, and re-layouts: 2.11 us -> 0.01 us
    pallas_call x8, Pallas kernels: 50.9 us -> 44 us  [the longest x6 19.4 us: call(): pl.pallas_call(kernel, out_shape=out_shape, in_specs=[RESIDENT] * len(res...]
    all_to_all x3, waiting for transfers between devices: 13.1 us -> 16.4 us  [exchange(): return lax.all_to_all(blocks, 'patch', 0, 0)]
    unnamed x6 -> x4, local copies, waits for them, and re-layouts: 2.11 us -> 0.01 us
  transfers between devices with their start and end apart: 3 -> 3, of which waited for: 3 -> 3; matrix products, arithmetic and copies ran while one was open for 0% -> 0% of each run, Pallas kernels for 12% -> 9%
where the time goes in v2:
time: 102 us
  Pallas kernels  44 us (43%)
  blocking collectives  29.7 us (29%)
  waiting for transfers between devices  16.4 us (16%)
  starting transfers between devices  11 us (11%)
    all_to_all x1, blocking collectives, exchange(): return lax.all_to_all(blocks, 'patch', 0, 0)  29.7 us
    pallas_call x6, Pallas kernels, call(): pl.pallas_call(kernel, out_shape=out_shape, in_specs=[RESIDENT] * len(res...  19.4 us
    pallas_call x1, Pallas kernels, attend(): pl.pallas_call(attend_kernel, out_shape=jax.ShapeDtypeStruct((HEADS, HEAD...  18.7 us
    all_to_all x3, waiting for transfers between devices, exchange(): return lax.all_to_all(blocks, 'patch', 0, 0)  16.4 us
    all_to_all x3, starting transfers between devices, exchange(): return lax.all_to_all(blocks, 'patch', 0, 0)  11 us
    pallas_call x1, Pallas kernels, project(): pl.pallas_call(project_kernel, out_shape=jax.ShapeDtypeStruct((HEADS, 3 *...  5.87 us
  transfers between devices with their start and end apart: 3, of which 3 were waited for; matrix products, arithmetic and copies ran while one was open for 0% of the time, Pallas kernels for 9%

profile of v2, /device:TPU:0, one launch (start us, length us, event | category | flops | bytes accessed | tf_op | source)
XLA Modules:
  0.0 101.7 jit_solution(9146410055915257160)
XLA Ops:
  0.6 5.9 %project.1 = bf16[16,192,256]{2,1,0:T(8,128)(2,1)} custom-call(bf16[256,1024]{1,0:T(8,128)(2,1)} %x_ref.1, bf16[3,1024,1024]{2,1,0:T(8,128)(2,1)} %w_hbm.7), custom_call_target="tpu_custom_call" | custom-call | flops 1610612736 | bytes 8388608 | tf_op jit(solution)/shard_map/project/pallas_call | solution.py:104
  6.5 29.7 %all_to_all.20.qkv_ref = bf16[16,192,256]{2,1,0:T(8,128)(2,1)S(1)} all-to-all(bf16[16,192,256]{2,1,0:T(8,128)(2,1)} %project.1), channel_id=1, replica_groups=mesh['dp'=8,'patch'=16] {'patch'}, dimensions={0} | all-to-all | bytes 3145728 | tf_op jit(solution)/shard_map/all_to_all | solution.py:373
  36.2 0.0 copy-start.1
  36.2 18.7 %attend.1 = bf16[16,64,256]{2,1,0:T(8,128)(2,1)} custom-call(bf16[16,192,256]{2,1,0:T(8,128)(2,1)S(1)} %all_to_all.20.qkv_ref), custom_call_target="tpu_custom_call" | custom-call | flops 17179869184 | bytes 2097152 | tf_op jit(solution)/shard_map/attend/pallas_call | solution.py:170
  54.9 3.8 %all-to-all-start.1 = ((bf16[16,64,256]{2,1,0:T(8,128)(2,1)}), bf16[16,64,256]{2,1,0:T(8,128)(2,1)S(1)}, u32[]{:S(2)}, u32[]{:S(2)}) async-start(bf16[16,64,256]{2,1,0:T(8,128)(2,1)} %attend.1), calls=%async_computation.1 | async-start | bytes 1048576 | tf_op jit(solution)/shard_map/all_to_all | solution.py:373
  58.7 0.0 copy-done.1
  58.8 0.0 copy-start
  58.8 3.6 %ahead.1 = (bf16[32,1024]{1,0:T(8,128)(2,1)S(1)}, f32[16,128]{1,0:T(8,128)S(1)}) custom-call(f32[1,1024]{1,0:T(1,128)S(1)} %copy-done.1, bf16[2,4,1024,1024]{3,2,1,0:T(8,128)(2,1)} %w_hbm.13), custom_call_target="tpu_custom_call" | custom-call | flops 1073741824 | bytes 1048576 | tf_op jit(solution)/shard_map/ahead/pallas_call | solution.py:38
  62.4 6.7 %all-to-all-done.1.ret_ref = bf16[16,64,256]{2,1,0:T(8,128)(2,1)S(1)} async-done(((bf16[16,64,256]{2,1,0:T(8,128)(2,1)}), bf16[16,64,256]{2,1,0:T(8,128)(2,1)S(1)}, u32[]{:S(2)}, u32[]{:S(2)}) %all-to-all-start.1) | async-done | bytes 524320 | tf_op jit(solution)/shard_map/all_to_all | solution.py:373
  69.1 0.0 copy-done
  69.1 3.9 %update.1 = (bf16[256,1024]{1,0:T(8,128)(2,1)}, bf16[256,1024]{1,0:T(8,128)(2,1)S(1)}, f32[16,16,128]{2,1,0:T(8,128)}) custom-call(bf16[16,64,256]{2,1,0:T(8,128)(2,1)S(1)} %all-to-all-done.1.ret_ref, bf16[256,1024]{1,0:T(8,128)(2,1)S(1)} %copy-done, bf16[32,1024]{1,0:T(8,128)(2,1)S(1)} %get-tuple-element.12.t_ref, bf16[1024,1024]{1,0:T(8,128)(2,1)} %wo_hbm.1, ...), custom_call_target="tpu_custom_call" | custom-call | flops 1073741824 | bytes 1048576 | tf_op jit(solution)/shard_map/update/pallas_call | solution.py:38
  73.0 3.5 %all-to-all-start.2 = ((f32[16,16,128]{2,1,0:T(8,128)}), f32[16,16,128]{2,1,0:T(8,128)S(1)}, u32[]{:S(2)}, u32[]{:S(2)}) async-start(f32[16,16,128]{2,1,0:T(8,128)} %get-tuple-element.14), calls=%async_computation.2 | async-start | bytes 262144 | tf_op jit(solution)/shard_map/all_to_all | solution.py:373
  76.5 3.0 %class_kv.1 = (bf16[256,1024]{1,0:T(8,128)(2,1)S(1)}, bf16[256,1024]{1,0:T(8,128)(2,1)S(1)}) custom-call(bf16[256,1024]{1,0:T(8,128)(2,1)S(1)} %get-tuple-element.16.upd_ref, bf16[2,4,1024,1024]{3,2,1,0:T(8,128)(2,1)} %w_hbm.13), custom_call_target="tpu_custom_call" | custom-call | flops 2147483648 | bytes 1048576 | tf_op jit(solution)/shard_map/class_kv/pallas_call | solution.py:38
  79.6 4.7 %all-to-all-done.2.parts_ref = f32[16,16,128]{2,1,0:T(8,128)S(1)} async-done(((f32[16,16,128]{2,1,0:T(8,128)}), f32[16,16,128]{2,1,0:T(8,128)S(1)}, u32[]{:S(2)}, u32[]{:S(2)}) %all-to-all-start.2) | async-done | bytes 131104 | tf_op jit(solution)/shard_map/all_to_all | solution.py:373
  84.3 3.6 %middle.1 = (f32[1,1024]{1,0:T(1,128)S(1)}, f32[1,1024]{1,0:T(1,128)S(1)}, f32[16,16,128]{2,1,0:T(8,128)}) custom-call(f32[16,16,128]{2,1,0:T(8,128)S(1)} %all-to-all-done.2.parts_ref, f32[16,128]{1,0:T(8,128)S(1)} %get-tuple-element.15.self_ref, f32[1,1024]{1,0:T(1,128)S(1)} %copy-done.1, bf16[256,1024]{1,0:T(8,128)(2,1)S(1)} %get-tuple-element.17.k_ref, ...), custom_call_target="tpu_custom_call" | custom-call | flops 268435456 | bytes 1048576 | tf_op jit(solution)/shard_map/middle/pallas_call | solution.py:38
  87.9 3.6 %all-to-all-start.3 = ((f32[16,16,128]{2,1,0:T(8,128)}), f32[16,16,128]{2,1,0:T(8,128)S(1)}, u32[]{:S(2)}, u32[]{:S(2)}) async-start(f32[16,16,128]{2,1,0:T(8,128)} %get-tuple-element.19), calls=%async_computation.3 | async-start | bytes 262144 | tf_op jit(solution)/shard_map/all_to_all | solution.py:373
  91.6 2.9 %self_part.1.self_ref = f32[16,128]{1,0:T(8,128)S(1)} custom-call(f32[1,1024]{1,0:T(1,128)S(1)} %get-tuple-element.20.cls_ref, f32[1,1024]{1,0:T(1,128)S(1)} %get-tuple-element.21.q_ref, bf16[2,4,1024,1024]{3,2,1,0:T(8,128)(2,1)} %w_hbm.13), custom_call_target="tpu_custom_call" | custom-call | flops 1073741824 | bytes 1048576 | tf_op jit(solution)/shard_map/self_part/pallas_call | solution.py:38
  94.5 4.9 %all-to-all-done.3.parts_ref = f32[16,16,128]{2,1,0:T(8,128)S(1)} async-done(((f32[16,16,128]{2,1,0:T(8,128)}), f32[16,16,128]{2,1,0:T(8,128)S(1)}, u32[]{:S(2)}, u32[]{:S(2)}) %all-to-all-start.3) | async-done | bytes 131104 | tf_op jit(solution)/shard_map/all_to_all | solution.py:373
  99.4 2.3 %last.1 = f32[1,1024]{1,0:T(1,128)} custom-call(f32[16,16,128]{2,1,0:T(8,128)S(1)} %all-to-all-done.3.parts_ref, f32[16,128]{1,0:T(8,128)S(1)} %self_part.1.self_ref, f32[1,1024]{1,0:T(1,128)S(1)} %get-tuple-element.20.cls_ref, bf16[2,4,1024,1024]{3,2,1,0:T(8,128)(2,1)} %w_hbm.13), custom_call_target="tpu_custom_call" | custom-call | flops 134217728 | bytes 1048576 | tf_op jit(solution)/shard_map/last/pallas_call | solution.py:38
Async XLA Ops:
  36.2 22.6 %copy-start.1 = (f32[1,1024]{1,0:T(1,128)S(1)}, f32[1,1024]{1,0:T(1,128)}, u32[]{:S(2)}) copy-start(f32[1,1024]{1,0:T(1,128)} %cls_ref.3) | copy-start | bytes 12292
  54.9 14.2 %all-to-all-start.1 = ((bf16[16,64,256]{2,1,0:T(8,128)(2,1)}), bf16[16,64,256]{2,1,0:T(8,128)(2,1)S(1)}, u32[]{:S(2)}, u32[]{:S(2)}) async-start(bf16[16,64,256]{2,1,0:T(8,128)(2,1)} %attend.1), calls=%async_computation.1 | async-start | bytes 1048576 | tf_op jit(solution)/shard_map/all_to_all | solution.py:373
  58.8 10.4 %copy-start = (bf16[256,1024]{1,0:T(8,128)(2,1)S(1)}, bf16[256,1024]{1,0:T(8,128)(2,1)}, u32[]{:S(2)}) copy-start(bf16[256,1024]{1,0:T(8,128)(2,1)} %x_ref.1) | copy-start | bytes 1572868
  73.0 11.3 %all-to-all-start.2 = ((f32[16,16,128]{2,1,0:T(8,128)}), f32[16,16,128]{2,1,0:T(8,128)S(1)}, u32[]{:S(2)}, u32[]{:S(2)}) async-start(f32[16,16,128]{2,1,0:T(8,128)} %get-tuple-element.14), calls=%async_computation.2 | async-start | bytes 262144 | tf_op jit(solution)/shard_map/all_to_all | solution.py:373
  87.9 11.5 %all-to-all-start.3 = ((f32[16,16,128]{2,1,0:T(8,128)}), f32[16,16,128]{2,1,0:T(8,128)S(1)}, u32[]{:S(2)}, u32[]{:S(2)}) async-start(f32[16,16,128]{2,1,0:T(8,128)} %get-tuple-element.19), calls=%async_computation.3 | async-start | bytes 262144 | tf_op jit(solution)/shard_map/all_to_all | solution.py:373

commit v3 on v2

--- a/solution.py
+++ b/solution.py
@@ -18,9 +18,9 @@
 NN = (((1,), (0,)), ((), ()))
 NT = (((1,), (1,)), ((), ()))
 TN = (((0,), (0,)), ((), ()))
-VMEM_LIMIT = 20 * 2**20
-SMALL_LIMIT = 16 * 2**20
-LARGE_LIMIT = 52 * 2**20
+VMEM_LIMIT = 14 * 2**20
+SMALL_LIMIT = 8 * 2**20
+LARGE_LIMIT = 46 * 2**20
 
 
 def dot(a, b, dims=NN):
@@ -213,12 +213,12 @@
     return start_copies([(w_hbm.at[c], w_s.at[c], sems.at[p]) for p, c in enumerate(cut)])
 
 
-def dot_streamed(a, w_s, copies, turned=False):
+def dot_streamed(a, w_s, copies):
     total = None
     for p, copy in enumerate(copies):
         cut = slice(PIECE * p, PIECE * (p + 1))
         copy.wait()
-        part = dot(a[cut, :], w_s[cut, :], TN) if turned else dot(a[:, cut], w_s[cut, :])
+        part = dot(a[:, cut], w_s[cut, :])
         total = part if total is None else total + part
     return total
 
@@ -270,18 +270,15 @@
     return to_row(value / total).astype(BF16)
 
 
-def update_kernel(ret_ref, x_ref, t_ref, wo_hbm, w_hbm, upd_hbm, upd_ref, part_ref, wo_s, wv_s, sems, sem):
-    wo_copies = stream(wo_hbm, wo_s, sems.at[0])
-    wv_copies = stream(w_hbm.at[0, 2], wv_s, sems.at[1])
+def update_kernel(ret_ref, x_ref, t_ref, wo_ref, w_hbm, upd_hbm, part_ref, upd_s, wv_s, sems):
+    (weight_copy,) = start_copies([(w_hbm.at[0, 2], wv_s, sems.at[0])])
     mask = head_mask()
     attended = ret_ref[...].reshape(D, ROWS)
-    added = dot_streamed(attended, wo_s, wo_copies, turned=True)
-    updated = (x_ref[...].astype(F32) + added).astype(BF16)
-    upd_ref[...] = updated
-    (out_copy,) = start_copies([(upd_ref, upd_hbm, sem)])
+    updated = (x_ref[...].astype(F32) + dot(attended, wo_ref[...], TN)).astype(BF16)
+    upd_s[...] = updated
+    (out_copy,) = start_copies([(upd_s, upd_hbm, sems.at[1])])
     scores = fold_halves(dot(t_ref[...], updated, NT))
-    for copy in wv_copies:
-        copy.wait()
+    weight_copy.wait()
     values = dot(updated, wv_s[...]).astype(BF16)
     partial_out(scores, values, mask, part_ref)
     out_copy.wait()
@@ -290,37 +287,45 @@
 def update(returned, patches, w_out, turned, w_class):
     shapes = (
         jax.ShapeDtypeStruct((ROWS, D), BF16),
-        jax.ShapeDtypeStruct((ROWS, D), BF16),
         jax.ShapeDtypeStruct((HEADS, 16, 128), F32),
     )
-    scratch = (SQUARE, SQUARE, pltpu.SemaphoreType.DMA((2, PIECES)), pltpu.SemaphoreType.DMA(()))
-    args = (returned, patches, turned)
-    return call(update_kernel, "update", 4 * ROWS * D * D, shapes, args, (w_out, w_class), scratch, 1)
-
-
-def class_kv_kernel(upd_ref, w_hbm, k_ref, v_ref, wk_s, wv_s, sems):
-    copies = start_copies([(w_hbm.at[1, 1], wk_s, sems.at[0]), (w_hbm.at[1, 2], wv_s, sems.at[1])])
-    updated = upd_ref[...]
+    scratch = (pltpu.VMEM((ROWS, D), BF16), SQUARE, pltpu.SemaphoreType.DMA((2,)))
+    args = (returned, patches, turned, w_out)
+    return call(update_kernel, "update", 4 * ROWS * D * D, shapes, args, (w_class,), scratch, 1)
+
+
+def class_kv_kernel(upd_hbm, w_hbm, k_ref, v_ref, wo_ref, upd_s, wk_s, wv_s, sems):
+    copies = start_copies(
+        [
+            (upd_hbm, upd_s, sems.at[0]),
+            (w_hbm.at[1, 1], wk_s, sems.at[1]),
+            (w_hbm.at[1, 2], wv_s, sems.at[2]),
+            (w_hbm.at[0, 3], wo_ref, sems.at[3]),
+        ]
+    )
     copies[0].wait()
+    updated = upd_s[...]
+    copies[1].wait()
     k_ref[...] = dot(updated, wk_s[...]).astype(BF16)
-    copies[1].wait()
+    copies[2].wait()
     v_ref[...] = dot(updated, wv_s[...]).astype(BF16)
+    copies[3].wait()
 
 
 def class_kv(updated, w_class):
-    shapes = (jax.ShapeDtypeStruct((ROWS, D), BF16),) * 2
-    scratch = (SQUARE, SQUARE, pltpu.SemaphoreType.DMA((2,)))
-    return call(class_kv_kernel, "class_kv", 2**31, shapes, (updated,), (w_class,), scratch)
+    rows = jax.ShapeDtypeStruct((ROWS, D), BF16)
+    shapes = (rows, rows, jax.ShapeDtypeStruct((D, D), BF16))
+    scratch = (pltpu.VMEM((ROWS, D), BF16), SQUARE, SQUARE, pltpu.SemaphoreType.DMA((4,)))
+    return call(class_kv_kernel, "class_kv", 2**31, shapes, (), (updated, w_class), scratch)
 
 
 def middle_kernel(
-    parts_ref, self_ref, cls_ref, k_ref, v_ref, w_hbm, cls_out_ref, q_ref, part_ref, wo_s, wq_s, sems
+    parts_ref, self_ref, cls_ref, wo_ref, k_ref, v_ref, w_hbm, cls_out_ref, q_ref, part_ref, wq_s, sems
 ):
-    wo_copies = stream(w_hbm.at[0, 3], wo_s, sems.at[0])
-    wq_copies = stream(w_hbm.at[1, 0], wq_s, sems.at[1])
+    wq_copies = stream(w_hbm.at[1, 0], wq_s, sems)
     mask = head_mask()
     attn = combine(parts_ref, self_ref)
-    cls_token = cls_ref[...] + dot_streamed(attn, wo_s, wo_copies)
+    cls_token = cls_ref[...] + dot(attn, wo_ref[...])
     cls_out_ref[...] = cls_token
     query = (dot_streamed(cls_token.astype(BF16), wq_s, wq_copies) * 0.125).astype(BF16).astype(F32)
     q_ref[...] = query
@@ -329,44 +334,48 @@
     partial_out(scores, v_ref[...], mask, part_ref)
 
 
-def middle(parts, self_part, cls_in, keys, values, w_class):
+def middle(parts, self_part, cls_in, w_o, keys, values, w_class):
     shapes = (
         jax.ShapeDtypeStruct((1, D), F32),
         jax.ShapeDtypeStruct((1, D), F32),
         jax.ShapeDtypeStruct((HEADS, 16, 128), F32),
     )
-    args = (parts, self_part, cls_in, keys, values)
-    scratch = (SQUARE, SQUARE, pltpu.SemaphoreType.DMA((2, PIECES)))
+    args = (parts, self_part, cls_in, w_o, keys, values)
+    scratch = (SQUARE, pltpu.SemaphoreType.DMA((PIECES,)))
     return call(middle_kernel, "middle", 2**28, shapes, args, (w_class,), scratch)
 
 
-def self_kernel(cls_ref, q_ref, w_hbm, self_ref, wk_s, wv_s, sems):
-    copies = start_copies([(w_hbm.at[1, 1], wk_s, sems.at[0]), (w_hbm.at[1, 2], wv_s, sems.at[1])])
+def self_kernel(cls_ref, q_ref, w_hbm, self_ref, wo_ref, wk_s, wv_s, sems):
+    copies = start_copies(
+        [
+            (w_hbm.at[1, 1], wk_s, sems.at[0]),
+            (w_hbm.at[1, 2], wv_s, sems.at[1]),
+            (w_hbm.at[1, 3], wo_ref, sems.at[2]),
+        ]
+    )
     cls_bf16 = cls_ref[...].astype(BF16)
-    for copy in copies:
-        copy.wait()
+    copies[0].wait()
+    copies[1].wait()
     value, score = self_terms(q_ref[...], cls_bf16, wk_s[...], wv_s[...], head_mask())
     self_ref[0:8, :] = value
     self_ref[8:16, :] = score
+    copies[2].wait()
 
 
 def self_part(cls_token, query, w_class):
-    shape = jax.ShapeDtypeStruct((16, 128), F32)
-    scratch = (SQUARE, SQUARE, pltpu.SemaphoreType.DMA((2,)))
-    return call(self_kernel, "self_part", 2**30, shape, (cls_token, query), (w_class,), scratch)
-
-
-def last_kernel(parts_ref, self_ref, cls_ref, w_hbm, out_ref, wo_s, sems):
-    wo_copies = stream(w_hbm.at[1, 3], wo_s, sems)
+    shapes = (jax.ShapeDtypeStruct((16, 128), F32), jax.ShapeDtypeStruct((D, D), BF16))
+    scratch = (SQUARE, SQUARE, pltpu.SemaphoreType.DMA((3,)))
+    return call(self_kernel, "self_part", 2**30, shapes, (cls_token, query), (w_class,), scratch)
+
+
+def last_kernel(parts_ref, self_ref, cls_ref, wo_ref, out_ref):
     attn = combine(parts_ref, self_ref)
-    out_ref[...] = cls_ref[...] + dot_streamed(attn, wo_s, wo_copies)
-
-
-def last(parts, self_terms_1, cls_token, w_class):
+    out_ref[...] = cls_ref[...] + dot(attn, wo_ref[...])
+
+
+def last(parts, self_terms_1, cls_token, w_o):
     shape = jax.ShapeDtypeStruct((1, D), F32)
-    scratch = (SQUARE, pltpu.SemaphoreType.DMA((PIECES,)))
-    args = (parts, self_terms_1, cls_token)
-    return call(last_kernel, "last", 2**27, shape, args, (w_class,), scratch)
+    return call(last_kernel, "last", 2**27, shape, (parts, self_terms_1, cls_token, w_o))
 
 
 def exchange(blocks):
@@ -377,13 +386,13 @@
     qkv = exchange(project(patches, w_attn))
     turned, self_0 = ahead(cls_in, w_class)
     returned = exchange(attend(qkv))
-    updated, updated_here, part_0 = update(returned, patches, w_out, turned, w_class)
+    updated, part_0 = update(returned, patches, w_out, turned, w_class)
     parts_0 = exchange(part_0)
-    keys, values = class_kv(updated_here, w_class)
-    cls_1, query_1, part_1 = middle(parts_0, self_0, cls_in, keys, values, w_class)
+    keys, values, w_o_0 = class_kv(updated, w_class)
+    cls_1, query_1, part_1 = middle(parts_0, self_0, cls_in, w_o_0, keys, values, w_class)
     parts_1 = exchange(part_1)
-    self_1 = self_part(cls_1, query_1, w_class)
-    return (updated, last(parts_1, self_1, cls_1, w_class))
+    self_1, w_o_1 = self_part(cls_1, query_1, w_class)
+    return (updated, last(parts_1, self_1, cls_1, w_o_1))
 
 
 def solution(mesh):

time: 102 us -> 99.6 us (0.976)
  Pallas kernels: 44 us -> 41.5 us
  waiting for transfers between devices: 16.4 us -> 15.1 us
  local copies, waits for them, and re-layouts: 0.01 us -> 1.05 us
    pallas_call x6, Pallas kernels: 19.4 us -> 17.2 us  [call(): pl.pallas_call(kernel, out_shape=out_shape, in_specs=[RESIDENT] * len(res...]
    all_to_all x3, waiting for transfers between devices: 16.4 us -> 15.1 us  [exchange(): return lax.all_to_all(blocks, 'patch', 0, 0)]
    unnamed x4 -> x8, local copies, waits for them, and re-layouts: 0.01 us -> 1.05 us
  transfers between devices with their start and end apart: 3 -> 3, of which waited for: 3 -> 3; matrix products, arithmetic and copies ran while one was open for 0% -> 0% of each run, Pallas kernels for 9% -> 10%
where the time goes in v3:
time: 99.6 us; the launch traced here: 99.1 us
  Pallas kernels  41.5 us (42%)
  blocking collectives  29.7 us (30%)
  waiting for transfers between devices  15.1 us (15%)
  starting transfers between devices  11 us (11%)
  local copies, waits for them, and re-layouts  1.05 us (1%)
    all_to_all x1, blocking collectives, exchange(): return lax.all_to_all(blocks, 'patch', 0, 0)  29.7 us
    pallas_call x1, Pallas kernels, attend(): pl.pallas_call(attend_kernel, out_shape=jax.ShapeDtypeStruct((HEADS, HEAD...  18.4 us
    pallas_call x6, Pallas kernels, call(): pl.pallas_call(kernel, out_shape=out_shape, in_specs=[RESIDENT] * len(res...  17.2 us
    all_to_all x3, waiting for transfers between devices, exchange(): return lax.all_to_all(blocks, 'patch', 0, 0)  15.1 us
    all_to_all x3, starting transfers between devices, exchange(): return lax.all_to_all(blocks, 'patch', 0, 0)  11 us
    pallas_call x1, Pallas kernels, project(): pl.pallas_call(project_kernel, out_shape=jax.ShapeDtypeStruct((HEADS, 3 *...  5.89 us
  transfers between devices with their start and end apart: 3, of which 3 were waited for; matrix products, arithmetic and copies ran while one was open for 0% of the time, Pallas kernels for 10%

profile of v3, /device:TPU:0, one launch (start us, length us, event | category | flops | bytes accessed | tf_op | source)
XLA Modules:
  0.0 99.1 jit_solution(13109541719177528806)
XLA Ops:
  0.6 5.9 %project.1 = bf16[16,192,256]{2,1,0:T(8,128)(2,1)} custom-call(bf16[256,1024]{1,0:T(8,128)(2,1)} %x_ref.1, bf16[3,1024,1024]{2,1,0:T(8,128)(2,1)} %w_hbm.6), custom_call_target="tpu_custom_call" | custom-call | flops 1610612736 | bytes 8388608 | tf_op jit(solution)/shard_map/project/pallas_call | solution.py:104
  6.5 29.7 %all_to_all.20.qkv_ref = bf16[16,192,256]{2,1,0:T(8,128)(2,1)S(1)} all-to-all(bf16[16,192,256]{2,1,0:T(8,128)(2,1)} %project.1), channel_id=1, replica_groups=mesh['dp'=8,'patch'=16] {'patch'}, dimensions={0} | all-to-all | bytes 3145728 | tf_op jit(solution)/shard_map/all_to_all | solution.py:382
  36.2 0.0 copy-start.3
  36.2 18.4 %attend.1 = bf16[16,64,256]{2,1,0:T(8,128)(2,1)} custom-call(bf16[16,192,256]{2,1,0:T(8,128)(2,1)S(1)} %all_to_all.20.qkv_ref), custom_call_target="tpu_custom_call" | custom-call | flops 17179869184 | bytes 2097152 | tf_op jit(solution)/shard_map/attend/pallas_call | solution.py:170
  54.6 3.8 %all-to-all-start.1 = ((bf16[16,64,256]{2,1,0:T(8,128)(2,1)}), bf16[16,64,256]{2,1,0:T(8,128)(2,1)S(1)}, u32[]{:S(2)}, u32[]{:S(2)}) async-start(bf16[16,64,256]{2,1,0:T(8,128)(2,1)} %attend.1), calls=%async_computation.1 | async-start | bytes 1048576 | tf_op jit(solution)/shard_map/all_to_all | solution.py:382
  58.4 0.0 copy-done.3
  58.5 0.0 copy-start
  58.5 0.0 copy-start.1
  58.5 3.7 %ahead.1 = (bf16[32,1024]{1,0:T(8,128)(2,1)S(1)}, f32[16,128]{1,0:T(8,128)S(1)}) custom-call(f32[1,1024]{1,0:T(1,128)S(1)} %copy-done.3, bf16[2,4,1024,1024]{3,2,1,0:T(8,128)(2,1)} %w_hbm.11), custom_call_target="tpu_custom_call" | custom-call | flops 1073741824 | bytes 1048576 | tf_op jit(solution)/shard_map/ahead/pallas_call | solution.py:38
  62.2 6.6 %all-to-all-done.1.ret_ref = bf16[16,64,256]{2,1,0:T(8,128)(2,1)S(1)} async-done(((bf16[16,64,256]{2,1,0:T(8,128)(2,1)}), bf16[16,64,256]{2,1,0:T(8,128)(2,1)S(1)}, u32[]{:S(2)}, u32[]{:S(2)}) %all-to-all-start.1) | async-done | bytes 524320 | tf_op jit(solution)/shard_map/all_to_all | solution.py:382
  68.8 0.0 copy-done
  68.8 0.0 copy-done.1
  68.8 3.2 %update.1 = (bf16[256,1024]{1,0:T(8,128)(2,1)}, f32[16,16,128]{2,1,0:T(8,128)}) custom-call(bf16[16,64,256]{2,1,0:T(8,128)(2,1)S(1)} %all-to-all-done.1.ret_ref, bf16[256,1024]{1,0:T(8,128)(2,1)S(1)} %copy-done.1, bf16[32,1024]{1,0:T(8,128)(2,1)S(1)} %get-tuple-element.14.t_ref, bf16[1024,1024]{1,0:T(8,128)(2,1)S(1)} %copy-done, ...), custom_call_target="tpu_custom_call" | custom-call | flops 1073741824 | bytes 1048576 | tf_op jit(solution)/shard_map/update/pallas_call | solution.py:38
  72.0 3.5 %all-to-all-start.2 = ((f32[16,16,128]{2,1,0:T(8,128)}), f32[16,16,128]{2,1,0:T(8,128)S(1)}, u32[]{:S(2)}, u32[]{:S(2)}) async-start(f32[16,16,128]{2,1,0:T(8,128)} %get-tuple-element.16), calls=%async_computation.2 | async-start | bytes 262144 | tf_op jit(solution)/shard_map/all_to_all | solution.py:382
  75.5 0.0 copy-start.2
  75.6 1.0 %copy-done.2 = bf16[256,1024]{1,0:T(8,128)(2,1)S(1)} copy-done((bf16[256,1024]{1,0:T(8,128)(2,1)S(1)}, bf16[256,1024]{1,0:T(8,128)(2,1)}, u32[]{:S(2)}) %copy-start.2) | copy-done | bytes 524312
  76.6 3.1 %class_kv.1 = (bf16[256,1024]{1,0:T(8,128)(2,1)S(1)}, bf16[256,1024]{1,0:T(8,128)(2,1)S(1)}, bf16[1024,1024]{1,0:T(8,128)(2,1)S(1)}) custom-call(bf16[256,1024]{1,0:T(8,128)(2,1)S(1)} %copy-done.2, bf16[2,4,1024,1024]{3,2,1,0:T(8,128)(2,1)} %w_hbm.11), custom_call_target="tpu_custom_call" | custom-call | flops 2147483648 | bytes 1048576 | tf_op jit(solution)/shard_map/class_kv/pallas_call | solution.py:38
  79.7 3.6 %all-to-all-done.2.parts_ref = f32[16,16,128]{2,1,0:T(8,128)S(1)} async-done(((f32[16,16,128]{2,1,0:T(8,128)}), f32[16,16,128]{2,1,0:T(8,128)S(1)}, u32[]{:S(2)}, u32[]{:S(2)}) %all-to-all-start.2) | async-done | bytes 131104 | tf_op jit(solution)/shard_map/all_to_all | solution.py:382
  83.3 3.2 %middle.1 = (f32[1,1024]{1,0:T(1,128)S(1)}, f32[1,1024]{1,0:T(1,128)S(1)}, f32[16,16,128]{2,1,0:T(8,128)}) custom-call(f32[16,16,128]{2,1,0:T(8,128)S(1)} %all-to-all-done.2.parts_ref, f32[16,128]{1,0:T(8,128)S(1)} %get-tuple-element.17.self_ref, f32[1,1024]{1,0:T(1,128)S(1)} %copy-done.3, bf16[1024,1024]{1,0:T(8,128)(2,1)S(1)} %get-tuple-element.18.wo_ref, ...), custom_call_target="tpu_custom_call" | custom-call | flops 268435456 | bytes 1048576 | tf_op jit(solution)/shard_map/middle/pallas_call | solution.py:38
  86.5 3.6 %all-to-all-start.3 = ((f32[16,16,128]{2,1,0:T(8,128)}), f32[16,16,128]{2,1,0:T(8,128)S(1)}, u32[]{:S(2)}, u32[]{:S(2)}) async-start(f32[16,16,128]{2,1,0:T(8,128)} %get-tuple-element.21), calls=%async_computation.3 | async-start | bytes 262144 | tf_op jit(solution)/shard_map/all_to_all | solution.py:382
  90.2 2.9 %self_part.1 = (f32[16,128]{1,0:T(8,128)S(1)}, bf16[1024,1024]{1,0:T(8,128)(2,1)S(1)}) custom-call(f32[1,1024]{1,0:T(1,128)S(1)} %get-tuple-element.22.cls_ref, f32[1,1024]{1,0:T(1,128)S(1)} %get-tuple-element.23.q_ref, bf16[2,4,1024,1024]{3,2,1,0:T(8,128)(2,1)} %w_hbm.11), custom_call_target="tpu_custom_call" | custom-call | flops 1073741824 | bytes 1048576 | tf_op jit(solution)/shard_map/self_part/pallas_call | solution.py:38
  93.1 4.9 %all-to-all-done.3.parts_ref = f32[16,16,128]{2,1,0:T(8,128)S(1)} async-done(((f32[16,16,128]{2,1,0:T(8,128)}), f32[16,16,128]{2,1,0:T(8,128)S(1)}, u32[]{:S(2)}, u32[]{:S(2)}) %all-to-all-start.3) | async-done | bytes 131104 | tf_op jit(solution)/shard_map/all_to_all | solution.py:382
  98.0 1.0 %last.1 = f32[1,1024]{1,0:T(1,128)} custom-call(f32[16,16,128]{2,1,0:T(8,128)S(1)} %all-to-all-done.3.parts_ref, f32[16,128]{1,0:T(8,128)S(1)} %get-tuple-element.24.self_ref, f32[1,1024]{1,0:T(1,128)S(1)} %get-tuple-element.22.cls_ref, bf16[1024,1024]{1,0:T(8,128)(2,1)S(1)} %get-tuple-element.25.wo_ref), custom_call_target="tpu_custom_call" | custom-call | flops 134217728 | bytes 1048576 | tf_op jit(solution)/shard_map/last/pallas_call | solution.py:38
Async XLA Ops:
  36.2 22.2 %copy-start.3 = (f32[1,1024]{1,0:T(1,128)S(1)}, f32[1,1024]{1,0:T(1,128)}, u32[]{:S(2)}) copy-start(f32[1,1024]{1,0:T(1,128)} %cls_ref.3) | copy-start | bytes 12292
  54.6 14.2 %all-to-all-start.1 = ((bf16[16,64,256]{2,1,0:T(8,128)(2,1)}), bf16[16,64,256]{2,1,0:T(8,128)(2,1)S(1)}, u32[]{:S(2)}, u32[]{:S(2)}) async-start(bf16[16,64,256]{2,1,0:T(8,128)(2,1)} %attend.1), calls=%async_computation.1 | async-start | bytes 1048576 | tf_op jit(solution)/shard_map/all_to_all | solution.py:382
  58.5 10.3 %copy-start = (bf16[1024,1024]{1,0:T(8,128)(2,1)S(1)}, bf16[1024,1024]{1,0:T(8,128)(2,1)}, u32[]{:S(2)}) copy-start(bf16[1024,1024]{1,0:T(8,128)(2,1)} %wo_ref.1) | copy-start | bytes 6291460
  58.5 10.3 %copy-start.1 = (bf16[256,1024]{1,0:T(8,128)(2,1)S(1)}, bf16[256,1024]{1,0:T(8,128)(2,1)}, u32[]{:S(2)}) copy-start(bf16[256,1024]{1,0:T(8,128)(2,1)} %x_ref.1) | copy-start | bytes 1572868
  72.0 11.3 %all-to-all-start.2 = ((f32[16,16,128]{2,1,0:T(8,128)}), f32[16,16,128]{2,1,0:T(8,128)S(1)}, u32[]{:S(2)}, u32[]{:S(2)}) async-start(f32[16,16,128]{2,1,0:T(8,128)} %get-tuple-element.16), calls=%async_computation.2 | async-start | bytes 262144 | tf_op jit(solution)/shard_map/all_to_all | solution.py:382
  75.5 1.0 %copy-start.2 = (bf16[256,1024]{1,0:T(8,128)(2,1)S(1)}, bf16[256,1024]{1,0:T(8,128)(2,1)}, u32[]{:S(2)}) copy-start(bf16[256,1024]{1,0:T(8,128)(2,1)} %get-tuple-element.12.upd_hbm) | copy-start | bytes 1572868
  86.5 11.5 %all-to-all-start.3 = ((f32[16,16,128]{2,1,0:T(8,128)}), f32[16,16,128]{2,1,0:T(8,128)S(1)}, u32[]{:S(2)}, u32[]{:S(2)}) async-start(f32[16,16,128]{2,1,0:T(8,128)} %get-tuple-element.21), calls=%async_computation.3 | async-start | bytes 262144 | tf_op jit(solution)/shard_map/all_to_all | solution.py:382

commit v4 on v3

--- a/solution.py
+++ b/solution.py
@@ -80,37 +80,56 @@
     return jnp.concatenate([tile[j : j + 1, :] for j in range(8)], axis=1)
 
 
-def project_kernel(x_hbm, w_hbm, out_ref, x_s, w_s, x_sem, w_sem):
+PARTS = ((0, 0, 16), (1, 0, 16), (2, 0, 8), (2, 8, 8))
+
+
+def project_kernel(x_hbm, w_hbm, out_hbm, x_s, w_s, out_s, x_sem, in_sems, out_sems):
     x_copy = pltpu.make_async_copy(x_hbm, x_s, x_sem)
-    copies = [pltpu.make_async_copy(w_hbm.at[k], w_s.at[k], w_sem.at[k]) for k in range(3)]
     x_copy.start()
-    for copy in copies:
-        copy.start()
+    copies = []
+    for p, (kind, head, count) in enumerate(PARTS):
+        cols = slice(head * HEAD_DIM, (head + count) * HEAD_DIM)
+        copies.append(
+            pltpu.make_async_copy(w_hbm.at[kind, :, cols], w_s.at[kind, :, cols], in_sems.at[p])
+        )
+        copies[-1].start()
     x_copy.wait()
     x = x_s[...]
-    for kind in range(3):
-        copies[kind].wait()
-        y = dot(x, w_s[kind])
+    outs = []
+    for p, (kind, head, count) in enumerate(PARTS):
+        copies[p].wait()
+        y = dot(x, w_s[kind, :, head * HEAD_DIM : (head + count) * HEAD_DIM])
         if kind == 0:
             y = y * (0.125 * LOG2E)
         yt = y.astype(BF16).T
-        for h in range(HEADS):
-            out_ref[h, kind * HEAD_DIM : (kind + 1) * HEAD_DIM, :] = yt[
-                h * HEAD_DIM : (h + 1) * HEAD_DIM
-            ]
+        rows = slice(kind * HEAD_DIM, (kind + 1) * HEAD_DIM)
+        for h in range(count):
+            out_s[head + h, rows, :] = yt[h * HEAD_DIM : (h + 1) * HEAD_DIM]
+        heads = slice(head, head + count)
+        outs.append(
+            pltpu.make_async_copy(
+                out_s.at[heads, rows, :], out_hbm.at[heads, rows, :], out_sems.at[p]
+            )
+        )
+        outs[-1].start()
+    for copy in outs:
+        copy.wait()
 
 
 def project(patches, w_attn):
+    packed = (HEADS, 3 * HEAD_DIM, ROWS)
     return pl.pallas_call(
         project_kernel,
-        out_shape=jax.ShapeDtypeStruct((HEADS, 3 * HEAD_DIM, ROWS), BF16),
+        out_shape=jax.ShapeDtypeStruct(packed, BF16),
         in_specs=[ANYWHERE] * 2,
-        out_specs=RESIDENT,
+        out_specs=ANYWHERE,
         scratch_shapes=[
             pltpu.VMEM((ROWS, D), BF16),
             pltpu.VMEM((3, D, D), BF16),
+            pltpu.VMEM(packed, BF16),
             pltpu.SemaphoreType.DMA(()),
-            pltpu.SemaphoreType.DMA((3,)),
+            pltpu.SemaphoreType.DMA((len(PARTS),)),
+            pltpu.SemaphoreType.DMA((len(PARTS),)),
         ],
         compiler_params=pltpu.CompilerParams(vmem_limit_bytes=62 * 2**20),
         cost_estimate=pl.CostEstimate(
@@ -136,7 +155,7 @@
         return jnp.max(scores, axis=0, keepdims=True)
 
     def weigh(span, before, top):
-        probs = jnp.exp2((s_s[before, span, :] - top).astype(BF16))
+        probs = jnp.exp2(s_s[before, span, :] - top).astype(BF16)
         return dot(v_s[:, span], probs)
 
     def finish(block, total):

time: 99.6 us -> 98.2 us (0.986)
  Pallas kernels: 41.5 us -> 40 us
    pallas_call x1, Pallas kernels: 18.4 us -> 16.8 us  [attend(): pl.pallas_call(attend_kernel, out_shape=jax.ShapeDtypeStruct((HEADS, HEAD...]
where the time goes in v4:
time: 98.2 us; the launch traced here: 97.6 us
  Pallas kernels  40 us (41%)
  blocking collectives  29.7 us (30%)
  waiting for transfers between devices  15.1 us (15%)
  starting transfers between devices  11 us (11%)
  local copies, waits for them, and re-layouts  1.05 us (1%)
    all_to_all x1, blocking collectives, exchange(): return lax.all_to_all(blocks, 'patch', 0, 0)  29.7 us
    pallas_call x6, Pallas kernels, call(): pl.pallas_call(kernel, out_shape=out_shape, in_specs=[RESIDENT] * len(res...  17.2 us
    pallas_call x1, Pallas kernels, attend(): pl.pallas_call(attend_kernel, out_shape=jax.ShapeDtypeStruct((HEADS, HEAD...  16.8 us
    all_to_all x3, waiting for transfers between devices, exchange(): return lax.all_to_all(blocks, 'patch', 0, 0)  15.1 us
    all_to_all x3, starting transfers between devices, exchange(): return lax.all_to_all(blocks, 'patch', 0, 0)  11 us
    pallas_call x1, Pallas kernels, project(): pl.pallas_call(project_kernel, out_shape=jax.ShapeDtypeStruct(packed, BF1...  6.04 us
  transfers between devices with their start and end apart: 3, of which 3 were waited for; matrix products, arithmetic and copies ran while one was open for 0% of the time, Pallas kernels for 10%

profile of v4, /device:TPU:0, one launch (start us, length us, event | category | flops | bytes accessed | tf_op | source)
XLA Modules:
  0.0 97.6 jit_solution(14399756246042260708)
XLA Ops:
  0.6 6.0 %project.1 = bf16[16,192,256]{2,1,0:T(8,128)(2,1)} custom-call(bf16[256,1024]{1,0:T(8,128)(2,1)} %x_ref.1, bf16[3,1024,1024]{2,1,0:T(8,128)(2,1)} %w_hbm.6), custom_call_target="tpu_custom_call" | custom-call | flops 1610612736 | bytes 8388608 | tf_op jit(solution)/shard_map/project/pallas_call | solution.py:121
  6.7 29.7 %all_to_all.20.qkv_ref = bf16[16,192,256]{2,1,0:T(8,128)(2,1)S(1)} all-to-all(bf16[16,192,256]{2,1,0:T(8,128)(2,1)} %project.1), channel_id=1, replica_groups=mesh['dp'=8,'patch'=16] {'patch'}, dimensions={0} | all-to-all | bytes 3145728 | tf_op jit(solution)/shard_map/all_to_all | solution.py:401
  36.4 0.0 copy-start.3
  36.4 16.8 %attend.1 = bf16[16,64,256]{2,1,0:T(8,128)(2,1)} custom-call(bf16[16,192,256]{2,1,0:T(8,128)(2,1)S(1)} %all_to_all.20.qkv_ref), custom_call_target="tpu_custom_call" | custom-call | flops 17179869184 | bytes 2097152 | tf_op jit(solution)/shard_map/attend/pallas_call | solution.py:189
  53.2 3.9 %all-to-all-start.1 = ((bf16[16,64,256]{2,1,0:T(8,128)(2,1)}), bf16[16,64,256]{2,1,0:T(8,128)(2,1)S(1)}, u32[]{:S(2)}, u32[]{:S(2)}) async-start(bf16[16,64,256]{2,1,0:T(8,128)(2,1)} %attend.1), calls=%async_computation.1 | async-start | bytes 1048576 | tf_op jit(solution)/shard_map/all_to_all | solution.py:401
  57.1 0.0 copy-done.3
  57.1 0.0 copy-start
  57.1 0.0 copy-start.1
  57.1 3.7 %ahead.1 = (bf16[32,1024]{1,0:T(8,128)(2,1)S(1)}, f32[16,128]{1,0:T(8,128)S(1)}) custom-call(f32[1,1024]{1,0:T(1,128)S(1)} %copy-done.3, bf16[2,4,1024,1024]{3,2,1,0:T(8,128)(2,1)} %w_hbm.11), custom_call_target="tpu_custom_call" | custom-call | flops 1073741824 | bytes 1048576 | tf_op jit(solution)/shard_map/ahead/pallas_call | solution.py:38
  60.8 6.5 %all-to-all-done.1.ret_ref = bf16[16,64,256]{2,1,0:T(8,128)(2,1)S(1)} async-done(((bf16[16,64,256]{2,1,0:T(8,128)(2,1)}), bf16[16,64,256]{2,1,0:T(8,128)(2,1)S(1)}, u32[]{:S(2)}, u32[]{:S(2)}) %all-to-all-start.1) | async-done | bytes 524320 | tf_op jit(solution)/shard_map/all_to_all | solution.py:401
  67.4 0.0 copy-done
  67.4 0.0 copy-done.1
  67.4 3.2 %update.1 = (bf16[256,1024]{1,0:T(8,128)(2,1)}, f32[16,16,128]{2,1,0:T(8,128)}) custom-call(bf16[16,64,256]{2,1,0:T(8,128)(2,1)S(1)} %all-to-all-done.1.ret_ref, bf16[256,1024]{1,0:T(8,128)(2,1)S(1)} %copy-done.1, bf16[32,1024]{1,0:T(8,128)(2,1)S(1)} %get-tuple-element.14.t_ref, bf16[1024,1024]{1,0:T(8,128)(2,1)S(1)} %copy-done, ...), custom_call_target="tpu_custom_call" | custom-call | flops 1073741824 | bytes 1048576 | tf_op jit(solution)/shard_map/update/pallas_call | solution.py:38
  70.6 3.5 %all-to-all-start.2 = ((f32[16,16,128]{2,1,0:T(8,128)}), f32[16,16,128]{2,1,0:T(8,128)S(1)}, u32[]{:S(2)}, u32[]{:S(2)}) async-start(f32[16,16,128]{2,1,0:T(8,128)} %get-tuple-element.16), calls=%async_computation.2 | async-start | bytes 262144 | tf_op jit(solution)/shard_map/all_to_all | solution.py:401
  74.1 0.0 copy-start.2
  74.1 1.0 %copy-done.2 = bf16[256,1024]{1,0:T(8,128)(2,1)S(1)} copy-done((bf16[256,1024]{1,0:T(8,128)(2,1)S(1)}, bf16[256,1024]{1,0:T(8,128)(2,1)}, u32[]{:S(2)}) %copy-start.2) | copy-done | bytes 524312
  75.2 3.1 %class_kv.1 = (bf16[256,1024]{1,0:T(8,128)(2,1)S(1)}, bf16[256,1024]{1,0:T(8,128)(2,1)S(1)}, bf16[1024,1024]{1,0:T(8,128)(2,1)S(1)}) custom-call(bf16[256,1024]{1,0:T(8,128)(2,1)S(1)} %copy-done.2, bf16[2,4,1024,1024]{3,2,1,0:T(8,128)(2,1)} %w_hbm.11), custom_call_target="tpu_custom_call" | custom-call | flops 2147483648 | bytes 1048576 | tf_op jit(solution)/shard_map/class_kv/pallas_call | solution.py:38
  78.3 3.6 %all-to-all-done.2.parts_ref = f32[16,16,128]{2,1,0:T(8,128)S(1)} async-done(((f32[16,16,128]{2,1,0:T(8,128)}), f32[16,16,128]{2,1,0:T(8,128)S(1)}, u32[]{:S(2)}, u32[]{:S(2)}) %all-to-all-start.2) | async-done | bytes 131104 | tf_op jit(solution)/shard_map/all_to_all | solution.py:401
  81.9 3.2 %middle.1 = (f32[1,1024]{1,0:T(1,128)S(1)}, f32[1,1024]{1,0:T(1,128)S(1)}, f32[16,16,128]{2,1,0:T(8,128)}) custom-call(f32[16,16,128]{2,1,0:T(8,128)S(1)} %all-to-all-done.2.parts_ref, f32[16,128]{1,0:T(8,128)S(1)} %get-tuple-element.17.self_ref, f32[1,1024]{1,0:T(1,128)S(1)} %copy-done.3, bf16[1024,1024]{1,0:T(8,128)(2,1)S(1)} %get-tuple-element.18.wo_ref, ...), custom_call_target="tpu_custom_call" | custom-call | flops 268435456 | bytes 1048576 | tf_op jit(solution)/shard_map/middle/pallas_call | solution.py:38
  85.1 3.6 %all-to-all-start.3 = ((f32[16,16,128]{2,1,0:T(8,128)}), f32[16,16,128]{2,1,0:T(8,128)S(1)}, u32[]{:S(2)}, u32[]{:S(2)}) async-start(f32[16,16,128]{2,1,0:T(8,128)} %get-tuple-element.21), calls=%async_computation.3 | async-start | bytes 262144 | tf_op jit(solution)/shard_map/all_to_all | solution.py:401
  88.8 2.9 %self_part.1 = (f32[16,128]{1,0:T(8,128)S(1)}, bf16[1024,1024]{1,0:T(8,128)(2,1)S(1)}) custom-call(f32[1,1024]{1,0:T(1,128)S(1)} %get-tuple-element.22.cls_ref, f32[1,1024]{1,0:T(1,128)S(1)} %get-tuple-element.23.q_ref, bf16[2,4,1024,1024]{3,2,1,0:T(8,128)(2,1)} %w_hbm.11), custom_call_target="tpu_custom_call" | custom-call | flops 1073741824 | bytes 1048576 | tf_op jit(solution)/shard_map/self_part/pallas_call | solution.py:38
  91.7 4.9 %all-to-all-done.3.parts_ref = f32[16,16,128]{2,1,0:T(8,128)S(1)} async-done(((f32[16,16,128]{2,1,0:T(8,128)}), f32[16,16,128]{2,1,0:T(8,128)S(1)}, u32[]{:S(2)}, u32[]{:S(2)}) %all-to-all-start.3) | async-done | bytes 131104 | tf_op jit(solution)/shard_map/all_to_all | solution.py:401
  96.6 1.0 %last.1 = f32[1,1024]{1,0:T(1,128)} custom-call(f32[16,16,128]{2,1,0:T(8,128)S(1)} %all-to-all-done.3.parts_ref, f32[16,128]{1,0:T(8,128)S(1)} %get-tuple-element.24.self_ref, f32[1,1024]{1,0:T(1,128)S(1)} %get-tuple-element.22.cls_ref, bf16[1024,1024]{1,0:T(8,128)(2,1)S(1)} %get-tuple-element.25.wo_ref), custom_call_target="tpu_custom_call" | custom-call | flops 134217728 | bytes 1048576 | tf_op jit(solution)/shard_map/last/pallas_call | solution.py:38
Async XLA Ops:
  36.4 20.7 %copy-start.3 = (f32[1,1024]{1,0:T(1,128)S(1)}, f32[1,1024]{1,0:T(1,128)}, u32[]{:S(2)}) copy-start(f32[1,1024]{1,0:T(1,128)} %cls_ref.3) | copy-start | bytes 12292
  53.2 14.2 %all-to-all-start.1 = ((bf16[16,64,256]{2,1,0:T(8,128)(2,1)}), bf16[16,64,256]{2,1,0:T(8,128)(2,1)S(1)}, u32[]{:S(2)}, u32[]{:S(2)}) async-start(bf16[16,64,256]{2,1,0:T(8,128)(2,1)} %attend.1), calls=%async_computation.1 | async-start | bytes 1048576 | tf_op jit(solution)/shard_map/all_to_all | solution.py:401
  57.1 10.3 %copy-start = (bf16[1024,1024]{1,0:T(8,128)(2,1)S(1)}, bf16[1024,1024]{1,0:T(8,128)(2,1)}, u32[]{:S(2)}) copy-start(bf16[1024,1024]{1,0:T(8,128)(2,1)} %wo_ref.1) | copy-start | bytes 6291460
  57.1 10.3 %copy-start.1 = (bf16[256,1024]{1,0:T(8,128)(2,1)S(1)}, bf16[256,1024]{1,0:T(8,128)(2,1)}, u32[]{:S(2)}) copy-start(bf16[256,1024]{1,0:T(8,128)(2,1)} %x_ref.1) | copy-start | bytes 1572868
  70.6 11.3 %all-to-all-start.2 = ((f32[16,16,128]{2,1,0:T(8,128)}), f32[16,16,128]{2,1,0:T(8,128)S(1)}, u32[]{:S(2)}, u32[]{:S(2)}) async-start(f32[16,16,128]{2,1,0:T(8,128)} %get-tuple-element.16), calls=%async_computation.2 | async-start | bytes 262144 | tf_op jit(solution)/shard_map/all_to_all | solution.py:401
  74.1 1.0 %copy-start.2 = (bf16[256,1024]{1,0:T(8,128)(2,1)S(1)}, bf16[256,1024]{1,0:T(8,128)(2,1)}, u32[]{:S(2)}) copy-start(bf16[256,1024]{1,0:T(8,128)(2,1)} %get-tuple-element.12.upd_hbm) | copy-start | bytes 1572868
  85.1 11.5 %all-to-all-start.3 = ((f32[16,16,128]{2,1,0:T(8,128)}), f32[16,16,128]{2,1,0:T(8,128)S(1)}, u32[]{:S(2)}, u32[]{:S(2)}) async-start(f32[16,16,128]{2,1,0:T(8,128)} %get-tuple-element.21), calls=%async_computation.3 | async-start | bytes 262144 | tf_op jit(solution)/shard_map/all_to_all | solution.py:401

commit v5 on v3

--- a/solution.py
+++ b/solution.py
@@ -80,14 +80,11 @@
     return jnp.concatenate([tile[j : j + 1, :] for j in range(8)], axis=1)
 
 
-def project_kernel(x_hbm, w_hbm, out_ref, x_s, w_s, x_sem, w_sem):
-    x_copy = pltpu.make_async_copy(x_hbm, x_s, x_sem)
+def project_kernel(x_ref, w_hbm, out_ref, w_s, w_sem):
     copies = [pltpu.make_async_copy(w_hbm.at[k], w_s.at[k], w_sem.at[k]) for k in range(3)]
-    x_copy.start()
     for copy in copies:
         copy.start()
-    x_copy.wait()
-    x = x_s[...]
+    x = x_ref[...]
     for kind in range(3):
         copies[kind].wait()
         y = dot(x, w_s[kind])
@@ -104,15 +101,13 @@
     return pl.pallas_call(
         project_kernel,
         out_shape=jax.ShapeDtypeStruct((HEADS, 3 * HEAD_DIM, ROWS), BF16),
-        in_specs=[ANYWHERE] * 2,
+        in_specs=[RESIDENT, ANYWHERE],
         out_specs=RESIDENT,
         scratch_shapes=[
-            pltpu.VMEM((ROWS, D), BF16),
             pltpu.VMEM((3, D, D), BF16),
-            pltpu.SemaphoreType.DMA(()),
             pltpu.SemaphoreType.DMA((3,)),
         ],
-        compiler_params=pltpu.CompilerParams(vmem_limit_bytes=62 * 2**20),
+        compiler_params=pltpu.CompilerParams(vmem_limit_bytes=50 * 2**20),
         cost_estimate=pl.CostEstimate(
             flops=2 * ROWS * D * 3 * D, bytes_accessed=8 * 2**20, transcendentals=0
         ),
@@ -124,7 +119,7 @@
 SPANS = [slice(c * CHUNK, (c + 1) * CHUNK) for c in range(PATCHES // CHUNK)]
 
 
-def attend_kernel(qkv_ref, out_ref, k_s, v_s, s_s):
+def attend_kernel(qkv_ref, out_hbm, k_s, v_s, s_s, out_s, sems):
     for j, span in enumerate(SPANS):
         k_s[span, :] = qkv_ref[j, 64:128, :].T
         v_s[0:64, span] = qkv_ref[j, 128:192, :]
@@ -136,11 +131,15 @@
         return jnp.max(scores, axis=0, keepdims=True)
 
     def weigh(span, before, top):
-        probs = jnp.exp2((s_s[before, span, :] - top).astype(BF16))
+        probs = jnp.exp2(s_s[before, span, :] - top).astype(BF16)
         return dot(v_s[:, span], probs)
 
+    def leave(block):
+        return pltpu.make_async_copy(out_s.at[block], out_hbm.at[block], sems.at[block])
+
     def finish(block, total):
-        out_ref[block] = (total[0:64] / total[64:65]).astype(BF16)
+        out_s[block] = (total[0:64] / total[64:65]).astype(BF16)
+        leave(block).start()
 
     def both(block, now, top):
         q_t = qkv_ref[block, 0:64, :]
@@ -164,6 +163,8 @@
     for span in SPANS:
         total = total + weigh(span, 1, top)
     finish(15, total)
+    for block in range(HEADS):
+        leave(block).wait()
 
 
 def attend(qkv):
@@ -171,11 +172,13 @@
         attend_kernel,
         out_shape=jax.ShapeDtypeStruct((HEADS, HEAD_DIM, ROWS), BF16),
         in_specs=[RESIDENT],
-        out_specs=RESIDENT,
+        out_specs=ANYWHERE,
         scratch_shapes=[
             pltpu.VMEM((PATCHES, HEAD_DIM), BF16),
             pltpu.VMEM((80, PATCHES), BF16),
             pltpu.VMEM((2, PATCHES, ROWS), F32),
+            pltpu.VMEM((HEADS, HEAD_DIM, ROWS), BF16),
+            pltpu.SemaphoreType.DMA((HEADS,)),
         ],
         compiler_params=pltpu.CompilerParams(vmem_limit_bytes=VMEM_LIMIT),
         cost_estimate=pl.CostEstimate(

time: 99.6 us -> 96.9 us (0.973)
  Pallas kernels: 41.5 us -> 37.9 us
  local copies, waits for them, and re-layouts: 1.05 us -> 2.09 us
    pallas_call x1, Pallas kernels: 5.89 us -> 3.97 us  [project(): pl.pallas_call(project_kernel, out_shape=jax.ShapeDtypeStruct((HEADS, 3 *...]
    pallas_call x1, Pallas kernels: 18.4 us -> 16.8 us  [attend(): pl.pallas_call(attend_kernel, out_shape=jax.ShapeDtypeStruct((HEADS, HEAD...]
    unnamed x8 -> x10, local copies, waits for them, and re-layouts: 1.05 us -> 2.09 us
where the time goes in v5:
time: 96.9 us; the launch traced here: 96.4 us
  Pallas kernels  37.9 us (39%)
  blocking collectives  29.5 us (30%)
  waiting for transfers between devices  15.1 us (16%)
  starting transfers between devices  11 us (11%)
  local copies, waits for them, and re-layouts  2.09 us (2%)
    all_to_all x1, blocking collectives, exchange(): return lax.all_to_all(blocks, 'patch', 0, 0)  29.5 us
    pallas_call x6, Pallas kernels, call(): pl.pallas_call(kernel, out_shape=out_shape, in_specs=[RESIDENT] * len(res...  17.2 us
    pallas_call x1, Pallas kernels, attend(): pl.pallas_call(attend_kernel, out_shape=jax.ShapeDtypeStruct((HEADS, HEAD...  16.8 us
    all_to_all x3, waiting for transfers between devices, exchange(): return lax.all_to_all(blocks, 'patch', 0, 0)  15.1 us
    all_to_all x3, starting transfers between devices, exchange(): return lax.all_to_all(blocks, 'patch', 0, 0)  11 us
    pallas_call x1, Pallas kernels, project(): pl.pallas_call(project_kernel, out_shape=jax.ShapeDtypeStruct((HEADS, 3 *...  3.97 us
    unnamed x10, local copies, waits for them, and re-layouts  2.09 us
  transfers between devices with their start and end apart: 3, of which 3 were waited for; matrix products, arithmetic and copies ran while one was open for 0% of the time, Pallas kernels for 10%

profile of v5, /device:TPU:0, one launch (start us, length us, event | category | flops | bytes accessed | tf_op | source)
XLA Modules:
  0.0 96.4 jit_solution(15852176404259676966)
XLA Ops:
  0.6 0.0 copy-start.1
  0.6 1.0 %copy-done.1 = bf16[256,1024]{1,0:T(8,128)(2,1)S(1)} copy-done((bf16[256,1024]{1,0:T(8,128)(2,1)S(1)}, bf16[256,1024]{1,0:T(8,128)(2,1)}, u32[]{:S(2)}) %copy-start.1) | copy-done | bytes 524312
  1.7 4.0 %project.1 = bf16[16,192,256]{2,1,0:T(8,128)(2,1)S(1)} custom-call(bf16[256,1024]{1,0:T(8,128)(2,1)S(1)} %copy-done.1, bf16[3,1024,1024]{2,1,0:T(8,128)(2,1)} %w_hbm.6), custom_call_target="tpu_custom_call" | custom-call | flops 1610612736 | bytes 8388608 | tf_op jit(solution)/shard_map/project/pallas_call | solution.py:101
  5.7 29.5 %all_to_all.20.qkv_ref = bf16[16,192,256]{2,1,0:T(8,128)(2,1)S(1)} all-to-all(bf16[16,192,256]{2,1,0:T(8,128)(2,1)S(1)} %project.1), channel_id=1, replica_groups=mesh['dp'=8,'patch'=16] {'patch'}, dimensions={0} | all-to-all | bytes 3145728 | tf_op jit(solution)/shard_map/all_to_all | solution.py:385
  35.1 0.0 copy-start.4
  35.1 16.8 %attend.1 = bf16[16,64,256]{2,1,0:T(8,128)(2,1)} custom-call(bf16[16,192,256]{2,1,0:T(8,128)(2,1)S(1)} %all_to_all.20.qkv_ref), custom_call_target="tpu_custom_call" | custom-call | flops 17179869184 | bytes 2097152 | tf_op jit(solution)/shard_map/attend/pallas_call | solution.py:171
  51.9 3.9 %all-to-all-start.1 = ((bf16[16,64,256]{2,1,0:T(8,128)(2,1)}), bf16[16,64,256]{2,1,0:T(8,128)(2,1)S(1)}, u32[]{:S(2)}, u32[]{:S(2)}) async-start(bf16[16,64,256]{2,1,0:T(8,128)(2,1)} %attend.1), calls=%async_computation.1 | async-start | bytes 1048576 | tf_op jit(solution)/shard_map/all_to_all | solution.py:385
  55.8 0.0 copy-done.4
  55.8 0.0 copy-start
  55.8 0.0 copy-start.2
  55.8 3.7 %ahead.1 = (bf16[32,1024]{1,0:T(8,128)(2,1)S(1)}, f32[16,128]{1,0:T(8,128)S(1)}) custom-call(f32[1,1024]{1,0:T(1,128)S(1)} %copy-done.4, bf16[2,4,1024,1024]{3,2,1,0:T(8,128)(2,1)} %w_hbm.11), custom_call_target="tpu_custom_call" | custom-call | flops 1073741824 | bytes 1048576 | tf_op jit(solution)/shard_map/ahead/pallas_call | solution.py:38
  59.5 6.6 %all-to-all-done.1.ret_ref = bf16[16,64,256]{2,1,0:T(8,128)(2,1)S(1)} async-done(((bf16[16,64,256]{2,1,0:T(8,128)(2,1)}), bf16[16,64,256]{2,1,0:T(8,128)(2,1)S(1)}, u32[]{:S(2)}, u32[]{:S(2)}) %all-to-all-start.1) | async-done | bytes 524320 | tf_op jit(solution)/shard_map/all_to_all | solution.py:385
  66.1 0.0 copy-done
  66.1 0.0 copy-done.2
  66.1 3.2 %update.1 = (bf16[256,1024]{1,0:T(8,128)(2,1)}, f32[16,16,128]{2,1,0:T(8,128)}) custom-call(bf16[16,64,256]{2,1,0:T(8,128)(2,1)S(1)} %all-to-all-done.1.ret_ref, bf16[256,1024]{1,0:T(8,128)(2,1)S(1)} %copy-done.2, bf16[32,1024]{1,0:T(8,128)(2,1)S(1)} %get-tuple-element.14.t_ref, bf16[1024,1024]{1,0:T(8,128)(2,1)S(1)} %copy-done, ...), custom_call_target="tpu_custom_call" | custom-call | flops 1073741824 | bytes 1048576 | tf_op jit(solution)/shard_map/update/pallas_call | solution.py:38
  69.3 3.5 %all-to-all-start.2 = ((f32[16,16,128]{2,1,0:T(8,128)}), f32[16,16,128]{2,1,0:T(8,128)S(1)}, u32[]{:S(2)}, u32[]{:S(2)}) async-start(f32[16,16,128]{2,1,0:T(8,128)} %get-tuple-element.16), calls=%async_computation.2 | async-start | bytes 262144 | tf_op jit(solution)/shard_map/all_to_all | solution.py:385
  72.9 0.0 copy-start.3
  72.9 1.0 %copy-done.3 = bf16[256,1024]{1,0:T(8,128)(2,1)S(1)} copy-done((bf16[256,1024]{1,0:T(8,128)(2,1)S(1)}, bf16[256,1024]{1,0:T(8,128)(2,1)}, u32[]{:S(2)}) %copy-start.3) | copy-done | bytes 524312
  73.9 3.1 %class_kv.1 = (bf16[256,1024]{1,0:T(8,128)(2,1)S(1)}, bf16[256,1024]{1,0:T(8,128)(2,1)S(1)}, bf16[1024,1024]{1,0:T(8,128)(2,1)S(1)}) custom-call(bf16[256,1024]{1,0:T(8,128)(2,1)S(1)} %copy-done.3, bf16[2,4,1024,1024]{3,2,1,0:T(8,128)(2,1)} %w_hbm.11), custom_call_target="tpu_custom_call" | custom-call | flops 2147483648 | bytes 1048576 | tf_op jit(solution)/shard_map/class_kv/pallas_call | solution.py:38
  77.0 3.6 %all-to-all-done.2.parts_ref = f32[16,16,128]{2,1,0:T(8,128)S(1)} async-done(((f32[16,16,128]{2,1,0:T(8,128)}), f32[16,16,128]{2,1,0:T(8,128)S(1)}, u32[]{:S(2)}, u32[]{:S(2)}) %all-to-all-start.2) | async-done | bytes 131104 | tf_op jit(solution)/shard_map/all_to_all | solution.py:385
  80.6 3.2 %middle.1 = (f32[1,1024]{1,0:T(1,128)S(1)}, f32[1,1024]{1,0:T(1,128)S(1)}, f32[16,16,128]{2,1,0:T(8,128)}) custom-call(f32[16,16,128]{2,1,0:T(8,128)S(1)} %all-to-all-done.2.parts_ref, f32[16,128]{1,0:T(8,128)S(1)} %get-tuple-element.17.self_ref, f32[1,1024]{1,0:T(1,128)S(1)} %copy-done.4, bf16[1024,1024]{1,0:T(8,128)(2,1)S(1)} %get-tuple-element.18.wo_ref, ...), custom_call_target="tpu_custom_call" | custom-call | flops 268435456 | bytes 1048576 | tf_op jit(solution)/shard_map/middle/pallas_call | solution.py:38
  83.9 3.6 %all-to-all-start.3 = ((f32[16,16,128]{2,1,0:T(8,128)}), f32[16,16,128]{2,1,0:T(8,128)S(1)}, u32[]{:S(2)}, u32[]{:S(2)}) async-start(f32[16,16,128]{2,1,0:T(8,128)} %get-tuple-element.21), calls=%async_computation.3 | async-start | bytes 262144 | tf_op jit(solution)/shard_map/all_to_all | solution.py:385
  87.5 2.9 %self_part.1 = (f32[16,128]{1,0:T(8,128)S(1)}, bf16[1024,1024]{1,0:T(8,128)(2,1)S(1)}) custom-call(f32[1,1024]{1,0:T(1,128)S(1)} %get-tuple-element.22.cls_ref, f32[1,1024]{1,0:T(1,128)S(1)} %get-tuple-element.23.q_ref, bf16[2,4,1024,1024]{3,2,1,0:T(8,128)(2,1)} %w_hbm.11), custom_call_target="tpu_custom_call" | custom-call | flops 1073741824 | bytes 1048576 | tf_op jit(solution)/shard_map/self_part/pallas_call | solution.py:38
  90.4 4.9 %all-to-all-done.3.parts_ref = f32[16,16,128]{2,1,0:T(8,128)S(1)} async-done(((f32[16,16,128]{2,1,0:T(8,128)}), f32[16,16,128]{2,1,0:T(8,128)S(1)}, u32[]{:S(2)}, u32[]{:S(2)}) %all-to-all-start.3) | async-done | bytes 131104 | tf_op jit(solution)/shard_map/all_to_all | solution.py:385
  95.4 1.0 %last.1 = f32[1,1024]{1,0:T(1,128)} custom-call(f32[16,16,128]{2,1,0:T(8,128)S(1)} %all-to-all-done.3.parts_ref, f32[16,128]{1,0:T(8,128)S(1)} %get-tuple-element.24.self_ref, f32[1,1024]{1,0:T(1,128)S(1)} %get-tuple-element.22.cls_ref, bf16[1024,1024]{1,0:T(8,128)(2,1)S(1)} %get-tuple-element.25.wo_ref), custom_call_target="tpu_custom_call" | custom-call | flops 134217728 | bytes 1048576 | tf_op jit(solution)/shard_map/last/pallas_call | solution.py:38
Async XLA Ops:
  0.6 1.0 %copy-start.1 = (bf16[256,1024]{1,0:T(8,128)(2,1)S(1)}, bf16[256,1024]{1,0:T(8,128)(2,1)}, u32[]{:S(2)}) copy-start(bf16[256,1024]{1,0:T(8,128)(2,1)} %x_ref.3) | copy-start | bytes 1572868
  35.1 20.6 %copy-start.4 = (f32[1,1024]{1,0:T(1,128)S(1)}, f32[1,1024]{1,0:T(1,128)}, u32[]{:S(2)}) copy-start(f32[1,1024]{1,0:T(1,128)} %cls_ref.3) | copy-start | bytes 12292
  51.9 14.2 %all-to-all-start.1 = ((bf16[16,64,256]{2,1,0:T(8,128)(2,1)}), bf16[16,64,256]{2,1,0:T(8,128)(2,1)S(1)}, u32[]{:S(2)}, u32[]{:S(2)}) async-start(bf16[16,64,256]{2,1,0:T(8,128)(2,1)} %attend.1), calls=%async_computation.1 | async-start | bytes 1048576 | tf_op jit(solution)/shard_map/all_to_all | solution.py:385
  55.8 10.3 %copy-start = (bf16[1024,1024]{1,0:T(8,128)(2,1)S(1)}, bf16[1024,1024]{1,0:T(8,128)(2,1)}, u32[]{:S(2)}) copy-start(bf16[1024,1024]{1,0:T(8,128)(2,1)} %wo_ref.1) | copy-start | bytes 6291460
  55.8 10.3 %copy-start.2 = (bf16[256,1024]{1,0:T(8,128)(2,1)S(1)}, bf16[256,1024]{1,0:T(8,128)(2,1)}, u32[]{:S(2)}) copy-start(bf16[256,1024]{1,0:T(8,128)(2,1)} %x_ref.3) | copy-start | bytes 1572868
  69.3 11.3 %all-to-all-start.2 = ((f32[16,16,128]{2,1,0:T(8,128)}), f32[16,16,128]{2,1,0:T(8,128)S(1)}, u32[]{:S(2)}, u32[]{:S(2)}) async-start(f32[16,16,128]{2,1,0:T(8,128)} %get-tuple-element.16), calls=%async_computation.2 | async-start | bytes 262144 | tf_op jit(solution)/shard_map/all_to_all | solution.py:385
  72.9 1.0 %copy-start.3 = (bf16[256,1024]{1,0:T(8,128)(2,1)S(1)}, bf16[256,1024]{1,0:T(8,128)(2,1)}, u32[]{:S(2)}) copy-start(bf16[256,1024]{1,0:T(8,128)(2,1)} %get-tuple-element.12.upd_hbm) | copy-start | bytes 1572868
  83.9 11.5 %all-to-all-start.3 = ((f32[16,16,128]{2,1,0:T(8,128)}), f32[16,16,128]{2,1,0:T(8,128)S(1)}, u32[]{:S(2)}, u32[]{:S(2)}) async-start(f32[16,16,128]{2,1,0:T(8,128)} %get-tuple-element.21), calls=%async_computation.3 | async-start | bytes 262144 | tf_op jit(solution)/shard_map/all_to_all | solution.py:385

commit v6 on v5

--- a/solution.py
+++ b/solution.py
@@ -21,6 +21,7 @@
 VMEM_LIMIT = 14 * 2**20
 SMALL_LIMIT = 8 * 2**20
 LARGE_LIMIT = 46 * 2**20
+PROJECT_LIMIT = 50 * 2**20
 
 
 def dot(a, b, dims=NN):
@@ -80,10 +81,14 @@
     return jnp.concatenate([tile[j : j + 1, :] for j in range(8)], axis=1)
 
 
-def project_kernel(x_ref, w_hbm, out_ref, w_s, w_sem):
-    copies = [pltpu.make_async_copy(w_hbm.at[k], w_s.at[k], w_sem.at[k]) for k in range(3)]
-    for copy in copies:
-        copy.start()
+def second_core():
+    return lax.rem(lax.axis_index("dp"), 2) == 1
+
+
+def project_kernel(
+    x_ref, w_hbm, cls_hbm, class_hbm, out_ref, t_ref, self_ref, base_ref, m_hbm, w_s, m_s, cls_s, sems, sem
+):
+    copies = start_copies([(w_hbm.at[k], w_s.at[k], sems.at[k]) for k in range(3)])
     x = x_ref[...]
     for kind in range(3):
         copies[kind].wait()
@@ -96,23 +101,40 @@
                 h * HEAD_DIM : (h + 1) * HEAD_DIM
             ]
 
-
-def project(patches, w_attn):
+    @pl.when(second_core())
+    def _():
+        (copy,) = start_copies([(cls_hbm, cls_s, sem)])
+        copy.wait()
+        class_ahead(cls_s[...], class_hbm, t_ref, self_ref, base_ref, m_hbm, w_s, m_s, sems, sem)
+
+
+AHEAD_SHAPES = (
+    jax.ShapeDtypeStruct((2 * HEADS, D), BF16),
+    jax.ShapeDtypeStruct((16, 128), F32),
+    jax.ShapeDtypeStruct((1, D), F32),
+    jax.ShapeDtypeStruct((3, D, D), BF16),
+)
+
+
+def project(patches, w_attn, cls_in, w_class):
     return pl.pallas_call(
         project_kernel,
-        out_shape=jax.ShapeDtypeStruct((HEADS, 3 * HEAD_DIM, ROWS), BF16),
-        in_specs=[RESIDENT, ANYWHERE],
-        out_specs=RESIDENT,
+        out_shape=(jax.ShapeDtypeStruct((HEADS, 3 * HEAD_DIM, ROWS), BF16), *AHEAD_SHAPES),
+        in_specs=[RESIDENT, ANYWHERE, ANYWHERE, ANYWHERE],
+        out_specs=(RESIDENT, RESIDENT, RESIDENT, RESIDENT, ANYWHERE),
         scratch_shapes=[
-            pltpu.VMEM((3, D, D), BF16),
-            pltpu.SemaphoreType.DMA((3,)),
+            pltpu.VMEM((5, D, D), BF16),
+            pltpu.VMEM((D, D), BF16),
+            pltpu.VMEM((1, D), F32),
+            pltpu.SemaphoreType.DMA((5,)),
+            pltpu.SemaphoreType.DMA(()),
         ],
-        compiler_params=pltpu.CompilerParams(vmem_limit_bytes=50 * 2**20),
+        compiler_params=pltpu.CompilerParams(vmem_limit_bytes=PROJECT_LIMIT),
         cost_estimate=pl.CostEstimate(
             flops=2 * ROWS * D * 3 * D, bytes_accessed=8 * 2**20, transcendentals=0
         ),
         name="project",
-    )(patches, w_attn)
+    )(patches, w_attn, cls_in, w_class)
 
 
 CHUNK = 256
@@ -207,45 +229,66 @@
     return copies
 
 
-PIECES = 4
-PIECE = D // PIECES
-
-
-def stream(w_hbm, w_s, sems):
-    cut = [slice(PIECE * p, PIECE * (p + 1)) for p in range(PIECES)]
-    return start_copies([(w_hbm.at[c], w_s.at[c], sems.at[p]) for p, c in enumerate(cut)])
-
-
-def dot_streamed(a, w_s, copies):
-    total = None
-    for p, copy in enumerate(copies):
-        cut = slice(PIECE * p, PIECE * (p + 1))
-        copy.wait()
-        part = dot(a[:, cut], w_s[cut, :])
-        total = part if total is None else total + part
-    return total
-
-
-def ahead_kernel(cls_ref, w_hbm, t_ref, self_ref, wq_s, wk_s, wv_s, sems):
-    copies = start_copies([(w_hbm.at[0, k], ref, sems.at[k]) for k, ref in enumerate((wq_s, wk_s, wv_s))])
+def class_ahead(cls_token, w_hbm, t_ref, self_ref, base_ref, m_hbm, w_s, m_s, sems, sem):
+    sources = ((0, 0), (0, 1), (0, 2), (0, 3), (1, 0))
+    copies = start_copies([(w_hbm.at[c, k], w_s.at[n], sems.at[n]) for n, (c, k) in enumerate(sources)])
     mask = head_mask()
-    cls_bf16 = cls_ref[...].astype(BF16)
+    cls_bf16 = cls_token.astype(BF16)
     copies[0].wait()
-    query = class_query(cls_bf16, wq_s[...])
+    query = class_query(cls_bf16, w_s[0])
     spread_query = jnp.where(mask, query, 0.0).astype(BF16)
     copies[1].wait()
-    turned = dot(spread_query, wk_s[...], NT) * LOG2E
+    turned = dot(spread_query, w_s[1], NT) * LOG2E
     t_ref[...] = split_rows(turned)
     copies[2].wait()
-    value, score = self_terms(query, cls_bf16, wk_s[...], wv_s[...], mask)
+    value, score = self_terms(query, cls_bf16, w_s[1], w_s[2], mask)
     self_ref[0:8, :] = value
     self_ref[8:16, :] = score
-
-
-def ahead(cls_in, w_class):
-    shapes = (jax.ShapeDtypeStruct((2 * HEADS, D), BF16), jax.ShapeDtypeStruct((16, 128), F32))
-    scratch = (SQUARE, SQUARE, SQUARE, pltpu.SemaphoreType.DMA((3,)))
-    return call(ahead_kernel, "ahead", 2**30, shapes, (cls_in,), (w_class,), scratch)
+    copies[3].wait()
+    copies[4].wait()
+    low = (cls_token - cls_bf16.astype(F32)).astype(BF16)
+    base_ref[...] = dot(cls_bf16, w_s[4]) + dot(low, w_s[4])
+    for c in range(4):
+        rows = slice(c * 256, (c + 1) * 256)
+        m_s[rows, :] = dot(w_s[3, rows, :], w_s[4]).astype(BF16)
+    (copy,) = start_copies([(m_s, m_hbm.at[0], sem)])
+    copy.wait()
+
+
+def ahead_kernel(
+    cls_ref, t_in, self_in, base_in, w_hbm, m_in, t_ref, self_ref, base_ref, m_hbm, w_s, m_s, sems, sem
+):
+    del m_in
+    second = second_core()
+
+    @pl.when(second)
+    def _():
+        t_ref[...] = t_in[...]
+        self_ref[...] = self_in[...]
+        base_ref[...] = base_in[...]
+
+    @pl.when(jnp.logical_not(second))
+    def _():
+        class_ahead(cls_ref[...], w_hbm, t_ref, self_ref, base_ref, m_hbm, w_s, m_s, sems, sem)
+
+
+def ahead(cls_in, turned, self_0, base, m, w_class):
+    return pl.pallas_call(
+        ahead_kernel,
+        out_shape=AHEAD_SHAPES,
+        in_specs=[RESIDENT] * 4 + [ANYWHERE] * 2,
+        out_specs=(RESIDENT, RESIDENT, RESIDENT, ANYWHERE),
+        scratch_shapes=[
+            pltpu.VMEM((5, D, D), BF16),
+            SQUARE,
+            pltpu.SemaphoreType.DMA((5,)),
+            pltpu.SemaphoreType.DMA(()),
+        ],
+        input_output_aliases={5: 3},
+        compiler_params=pltpu.CompilerParams(vmem_limit_bytes=49 * 2**20),
+        cost_estimate=pl.CostEstimate(flops=2**32, bytes_accessed=2**20, transcendentals=0),
+        name="ahead",
+    )(cls_in, turned, self_0, base, w_class, m)
 
 
 def partial_out(scores, values, mask, out_ref):
@@ -297,13 +340,13 @@
     return call(update_kernel, "update", 4 * ROWS * D * D, shapes, args, (w_class,), scratch, 1)
 
 
-def class_kv_kernel(upd_hbm, w_hbm, k_ref, v_ref, wo_ref, upd_s, wk_s, wv_s, sems):
+def class_kv_kernel(upd_hbm, w_hbm, m_hbm, k_ref, v_ref, m_ref, upd_s, wk_s, wv_s, sems):
     copies = start_copies(
         [
             (upd_hbm, upd_s, sems.at[0]),
             (w_hbm.at[1, 1], wk_s, sems.at[1]),
             (w_hbm.at[1, 2], wv_s, sems.at[2]),
-            (w_hbm.at[0, 3], wo_ref, sems.at[3]),
+            (m_hbm.at[0], m_ref, sems.at[3]),
         ]
     )
     copies[0].wait()
@@ -315,60 +358,61 @@
     copies[3].wait()
 
 
-def class_kv(updated, w_class):
+def class_kv(updated, w_class, m):
     rows = jax.ShapeDtypeStruct((ROWS, D), BF16)
     shapes = (rows, rows, jax.ShapeDtypeStruct((D, D), BF16))
     scratch = (pltpu.VMEM((ROWS, D), BF16), SQUARE, SQUARE, pltpu.SemaphoreType.DMA((4,)))
-    return call(class_kv_kernel, "class_kv", 2**31, shapes, (), (updated, w_class), scratch)
-
-
-def middle_kernel(
-    parts_ref, self_ref, cls_ref, wo_ref, k_ref, v_ref, w_hbm, cls_out_ref, q_ref, part_ref, wq_s, sems
-):
-    wq_copies = stream(w_hbm.at[1, 0], wq_s, sems)
+    return call(class_kv_kernel, "class_kv", 2**31, shapes, (), (updated, w_class, m), scratch)
+
+
+def middle_kernel(parts_ref, self_ref, base_ref, m_ref, k_ref, v_ref, attn_ref, q_ref, part_ref):
     mask = head_mask()
     attn = combine(parts_ref, self_ref)
-    cls_token = cls_ref[...] + dot(attn, wo_ref[...])
-    cls_out_ref[...] = cls_token
-    query = (dot_streamed(cls_token.astype(BF16), wq_s, wq_copies) * 0.125).astype(BF16).astype(F32)
+    attn_ref[...] = attn.astype(F32)
+    query = ((base_ref[...] + dot(attn, m_ref[...])) * 0.125).astype(BF16).astype(F32)
     q_ref[...] = query
     spread_query = jnp.where(mask, query, 0.0).astype(BF16)
     scores = dot(spread_query, k_ref[...], NT) * LOG2E
     partial_out(scores, v_ref[...], mask, part_ref)
 
 
-def middle(parts, self_part, cls_in, w_o, keys, values, w_class):
+def middle(parts, self_part, base, m, keys, values):
     shapes = (
         jax.ShapeDtypeStruct((1, D), F32),
         jax.ShapeDtypeStruct((1, D), F32),
         jax.ShapeDtypeStruct((HEADS, 16, 128), F32),
     )
-    args = (parts, self_part, cls_in, w_o, keys, values)
-    scratch = (SQUARE, pltpu.SemaphoreType.DMA((PIECES,)))
-    return call(middle_kernel, "middle", 2**28, shapes, args, (w_class,), scratch)
-
-
-def self_kernel(cls_ref, q_ref, w_hbm, self_ref, wo_ref, wk_s, wv_s, sems):
+    return call(middle_kernel, "middle", 2**28, shapes, (parts, self_part, base, m, keys, values))
+
+
+def self_kernel(cls_ref, attn_ref, q_ref, w_hbm, self_ref, cls_out_ref, wo_ref, w_s, sems):
     copies = start_copies(
         [
-            (w_hbm.at[1, 1], wk_s, sems.at[0]),
-            (w_hbm.at[1, 2], wv_s, sems.at[1]),
-            (w_hbm.at[1, 3], wo_ref, sems.at[2]),
+            (w_hbm.at[0, 3], w_s.at[0], sems.at[0]),
+            (w_hbm.at[1, 1], w_s.at[1], sems.at[1]),
+            (w_hbm.at[1, 2], w_s.at[2], sems.at[2]),
+            (w_hbm.at[1, 3], wo_ref, sems.at[3]),
         ]
     )
-    cls_bf16 = cls_ref[...].astype(BF16)
     copies[0].wait()
+    cls_token = cls_ref[...] + dot(attn_ref[...].astype(BF16), w_s[0])
+    cls_out_ref[...] = cls_token
     copies[1].wait()
-    value, score = self_terms(q_ref[...], cls_bf16, wk_s[...], wv_s[...], head_mask())
+    copies[2].wait()
+    value, score = self_terms(q_ref[...], cls_token.astype(BF16), w_s[1], w_s[2], head_mask())
     self_ref[0:8, :] = value
     self_ref[8:16, :] = score
-    copies[2].wait()
-
-
-def self_part(cls_token, query, w_class):
-    shapes = (jax.ShapeDtypeStruct((16, 128), F32), jax.ShapeDtypeStruct((D, D), BF16))
-    scratch = (SQUARE, SQUARE, pltpu.SemaphoreType.DMA((3,)))
-    return call(self_kernel, "self_part", 2**30, shapes, (cls_token, query), (w_class,), scratch)
+    copies[3].wait()
+
+
+def self_part(cls_in, attn, query, w_class):
+    shapes = (
+        jax.ShapeDtypeStruct((16, 128), F32),
+        jax.ShapeDtypeStruct((1, D), F32),
+        jax.ShapeDtypeStruct((D, D), BF16),
+    )
+    scratch = (pltpu.VMEM((3, D, D), BF16), pltpu.SemaphoreType.DMA((4,)))
+    return call(self_kernel, "self_part", 2**30, shapes, (cls_in, attn, query), (w_class,), scratch)
 
 
 def last_kernel(parts_ref, self_ref, cls_ref, wo_ref, out_ref):
@@ -386,15 +430,16 @@
 
 
 def per_device(patches, cls_in, w_attn, w_out, w_class):
-    qkv = exchange(project(patches, w_attn))
-    turned, self_0 = ahead(cls_in, w_class)
+    qkv, turned, self_0, base, m = project(patches, w_attn, cls_in, w_class)
+    qkv = exchange(qkv)
     returned = exchange(attend(qkv))
+    turned, self_0, base, m = ahead(cls_in, turned, self_0, base, m, w_class)
     updated, part_0 = update(returned, patches, w_out, turned, w_class)
     parts_0 = exchange(part_0)
-    keys, values, w_o_0 = class_kv(updated, w_class)
-    cls_1, query_1, part_1 = middle(parts_0, self_0, cls_in, w_o_0, keys, values, w_class)
+    keys, values, m = class_kv(updated, w_class, m)
+    attn_0, query_1, part_1 = middle(parts_0, self_0, base, m, keys, values)
     parts_1 = exchange(part_1)
-    self_1, w_o_1 = self_part(cls_1, query_1, w_class)
+    self_1, cls_1, w_o_1 = self_part(cls_in, attn_0, query_1, w_class)
     return (updated, last(parts_1, self_1, cls_1, w_o_1))
 
 

time: 96.9 us -> 94.9 us (0.979)
  the two profiles are of different devices: /device:TPU:0 before, /device:TPU:1 now
where the time goes in v6:
time: 94.9 us; the launch traced here: 94.3 us
  Pallas kernels  41.8 us (44%)
  blocking collectives  23.5 us (25%)
  waiting for transfers between devices  14.2 us (15%)
  starting transfers between devices  11.2 us (12%)
  local copies, waits for them, and re-layouts  2.78 us (3%)
    all_to_all x1, blocking collectives, exchange(): return lax.all_to_all(blocks, 'patch', 0, 0)  23.5 us
    pallas_call x1, Pallas kernels, attend(): pl.pallas_call(attend_kernel, out_shape=jax.ShapeDtypeStruct((HEADS, HEAD...  16.8 us
    all_to_all x3, waiting for transfers between devices, exchange(): return lax.all_to_all(blocks, 'patch', 0, 0)  14.2 us
    pallas_call x5, Pallas kernels, call(): pl.pallas_call(kernel, out_shape=out_shape, in_specs=[RESIDENT] * len(res...  12.5 us
    pallas_call x1, Pallas kernels, project(): pl.pallas_call(project_kernel, out_shape=(jax.ShapeDtypeStruct((HEADS, 3...  12.3 us
    all_to_all x3, starting transfers between devices, exchange(): return lax.all_to_all(blocks, 'patch', 0, 0)  11.2 us
    unnamed x12, local copies, waits for them, and re-layouts  2.78 us
  transfers between devices with their start and end apart: 3, of which 3 were waited for; matrix products, arithmetic and copies ran while one was open for 0% of the time, Pallas kernels for 7%

profile of v6, /device:TPU:1, one launch (start us, length us, event | category | flops | bytes accessed | tf_op | source)
XLA Modules:
  0.0 94.3 jit_solution(15231365468808717936)
XLA Ops:
  0.6 0.0 copy-start.1
  0.6 1.0 %copy-done.1 = bf16[256,1024]{1,0:T(8,128)(2,1)S(1)} copy-done((bf16[256,1024]{1,0:T(8,128)(2,1)S(1)}, bf16[256,1024]{1,0:T(8,128)(2,1)}, u32[]{:S(2)}) %copy-start.1) | copy-done | bytes 524312
  1.7 0.0 copy-start.4
  1.7 0.7 copy-done.4
  2.4 12.3 %project.1 = (bf16[16,192,256]{2,1,0:T(8,128)(2,1)S(1)}, bf16[32,1024]{1,0:T(8,128)(2,1)S(1)}, f32[16,128]{1,0:T(8,128)S(1)}, f32[1,1024]{1,0:T(1,128)S(1)}, bf16[3,1024,1024]{2,1,0:T(8,128)(2,1)}) custom-call(bf16[256,1024]{1,0:T(8,128)(2,1)S(1)} %copy-done.1, bf16[3,1024,1024]{2,1,0:T(8,128)(2,1)} %w_hbm.5, f32[1,1024]{1,0:T(1,128)S(1)} %copy-done.4, ...), custom_call_target="tpu_custom_call" | custom-call | flops 1610612736 | bytes 8388608 | tf_op jit(solution)/shard_map/project/pallas_call | solution.py:120
  14.7 23.5 %all_to_all.20.qkv_ref = bf16[16,192,256]{2,1,0:T(8,128)(2,1)S(1)} all-to-all(bf16[16,192,256]{2,1,0:T(8,128)(2,1)S(1)} %get-tuple-element.22), channel_id=1, replica_groups=mesh['dp'=8,'patch'=16] {'patch'}, dimensions={0} | all-to-all | bytes 3145728 | tf_op jit(solution)/shard_map/all_to_all | solution.py:429
  38.2 0.0 copy-start.5
  38.2 16.8 %attend.1 = bf16[16,64,256]{2,1,0:T(8,128)(2,1)} custom-call(bf16[16,192,256]{2,1,0:T(8,128)(2,1)S(1)} %all_to_all.20.qkv_ref), custom_call_target="tpu_custom_call" | custom-call | flops 17179869184 | bytes 2097152 | tf_op jit(solution)/shard_map/attend/pallas_call | solution.py:193
  54.9 3.6 %all-to-all-start.1 = ((bf16[16,64,256]{2,1,0:T(8,128)(2,1)}), bf16[16,64,256]{2,1,0:T(8,128)(2,1)S(1)}, u32[]{:S(2)}, u32[]{:S(2)}) async-start(bf16[16,64,256]{2,1,0:T(8,128)(2,1)} %attend.1), calls=%async_computation.1 | async-start | bytes 1048576 | tf_op jit(solution)/shard_map/all_to_all | solution.py:429
  58.5 0.0 copy-done.5
  58.5 0.0 copy-start
  58.5 0.0 copy-start.2
  58.6 0.3 ahead.1
  58.8 8.6 %all-to-all-done.1.ret_ref = bf16[16,64,256]{2,1,0:T(8,128)(2,1)S(1)} async-done(((bf16[16,64,256]{2,1,0:T(8,128)(2,1)}), bf16[16,64,256]{2,1,0:T(8,128)(2,1)S(1)}, u32[]{:S(2)}, u32[]{:S(2)}) %all-to-all-start.1) | async-done | bytes 524320 | tf_op jit(solution)/shard_map/all_to_all | solution.py:429
  67.4 0.0 copy-done
  67.4 0.0 copy-done.2
  67.4 3.2 %update.1 = (bf16[256,1024]{1,0:T(8,128)(2,1)}, f32[16,16,128]{2,1,0:T(8,128)}) custom-call(bf16[16,64,256]{2,1,0:T(8,128)(2,1)S(1)} %all-to-all-done.1.ret_ref, bf16[256,1024]{1,0:T(8,128)(2,1)S(1)} %copy-done.2, bf16[32,1024]{1,0:T(8,128)(2,1)S(1)} %get-tuple-element.27.t_ref, bf16[1024,1024]{1,0:T(8,128)(2,1)S(1)} %copy-done, bf16[2,4,1024,1024]{3,2,1,0:T(8,128)(2,1)} %w_hbm.9), custom_call_target="tpu_custom_call" | custom-call | flops 1073741824 | bytes 1048576 | tf_op jit(solution)/shard_map/update/pallas_call | solution.py:39
  70.6 3.5 %all-to-all-start.2 = ((f32[16,16,128]{2,1,0:T(8,128)}), f32[16,16,128]{2,1,0:T(8,128)S(1)}, u32[]{:S(2)}, u32[]{:S(2)}) async-start(f32[16,16,128]{2,1,0:T(8,128)} %get-tuple-element.29), calls=%async_computation.2 | async-start | bytes 262144 | tf_op jit(solution)/shard_map/all_to_all | solution.py:429
  74.2 0.0 copy-start.3
  74.2 1.0 %copy-done.3 = bf16[256,1024]{1,0:T(8,128)(2,1)S(1)} copy-done((bf16[256,1024]{1,0:T(8,128)(2,1)S(1)}, bf16[256,1024]{1,0:T(8,128)(2,1)}, u32[]{:S(2)}) %copy-start.3) | copy-done | bytes 524312
  75.2 3.1 %class_kv.1 = (bf16[256,1024]{1,0:T(8,128)(2,1)S(1)}, bf16[256,1024]{1,0:T(8,128)(2,1)S(1)}, bf16[1024,1024]{1,0:T(8,128)(2,1)S(1)}) custom-call(bf16[256,1024]{1,0:T(8,128)(2,1)S(1)} %copy-done.3, bf16[2,4,1024,1024]{3,2,1,0:T(8,128)(2,1)} %w_hbm.9, bf16[3,1024,1024]{2,1,0:T(8,128)(2,1)} %get-tuple-element.32.m_hbm), custom_call_target="tpu_custom_call" | custom-call | flops 2147483648 | bytes 1048576 | tf_op jit(solution)/shard_map/class_kv/pallas_call | solution.py:39
  78.3 2.5 %all-to-all-done.2.parts_ref = f32[16,16,128]{2,1,0:T(8,128)S(1)} async-done(((f32[16,16,128]{2,1,0:T(8,128)}), f32[16,16,128]{2,1,0:T(8,128)S(1)}, u32[]{:S(2)}, u32[]{:S(2)}) %all-to-all-start.2) | async-done | bytes 131104 | tf_op jit(solution)/shard_map/all_to_all | solution.py:429
  80.8 1.7 %middle.1 = (f32[1,1024]{1,0:T(1,128)S(1)}, f32[1,1024]{1,0:T(1,128)S(1)}, f32[16,16,128]{2,1,0:T(8,128)}) custom-call(f32[16,16,128]{2,1,0:T(8,128)S(1)} %all-to-all-done.2.parts_ref, f32[16,128]{1,0:T(8,128)S(1)} %get-tuple-element.30.self_ref, f32[1,1024]{1,0:T(1,128)S(1)} %get-tuple-element.31.base_ref, bf16[1024,1024]{1,0:T(8,128)(2,1)S(1)} %get-tuple-element.33.m_ref, ...), custom_call_target="tpu_custom_call" | custom-call | flops 268435456 | bytes 1048576 | tf_op jit(solution)/shard_map/middle/pallas_call | solution.py:39
  82.5 4.1 %all-to-all-start.3 = ((f32[16,16,128]{2,1,0:T(8,128)}), f32[16,16,128]{2,1,0:T(8,128)S(1)}, u32[]{:S(2)}, u32[]{:S(2)}) async-start(f32[16,16,128]{2,1,0:T(8,128)} %get-tuple-element.36), calls=%async_computation.3 | async-start | bytes 262144 | tf_op jit(solution)/shard_map/all_to_all | solution.py:429
  86.6 3.6 %self_part.1 = (f32[16,128]{1,0:T(8,128)S(1)}, f32[1,1024]{1,0:T(1,128)S(1)}, bf16[1024,1024]{1,0:T(8,128)(2,1)S(1)}) custom-call(f32[1,1024]{1,0:T(1,128)S(1)} %copy-done.5, f32[1,1024]{1,0:T(1,128)S(1)} %get-tuple-element.37.attn_ref, f32[1,1024]{1,0:T(1,128)S(1)} %get-tuple-element.38.q_ref, bf16[2,4,1024,1024]{3,2,1,0:T(8,128)(2,1)} %w_hbm.9), custom_call_target="tpu_custom_call" | custom-call | flops 1073741824 | bytes 1048576 | tf_op jit(solution)/shard_map/self_part/pallas_call | solution.py:39
  90.2 3.1 %all-to-all-done.3.parts_ref = f32[16,16,128]{2,1,0:T(8,128)S(1)} async-done(((f32[16,16,128]{2,1,0:T(8,128)}), f32[16,16,128]{2,1,0:T(8,128)S(1)}, u32[]{:S(2)}, u32[]{:S(2)}) %all-to-all-start.3) | async-done | bytes 131104 | tf_op jit(solution)/shard_map/all_to_all | solution.py:429
  93.3 1.0 %last.1 = f32[1,1024]{1,0:T(1,128)} custom-call(f32[16,16,128]{2,1,0:T(8,128)S(1)} %all-to-all-done.3.parts_ref, f32[16,128]{1,0:T(8,128)S(1)} %get-tuple-element.39.self_ref, f32[1,1024]{1,0:T(1,128)S(1)} %get-tuple-element.40.cls_ref, bf16[1024,1024]{1,0:T(8,128)(2,1)S(1)} %get-tuple-element.41.wo_ref), custom_call_target="tpu_custom_call" | custom-call | flops 134217728 | bytes 1048576 | tf_op jit(solution)/shard_map/last/pallas_call | solution.py:39
Async XLA Ops:
  0.6 1.0 %copy-start.1 = (bf16[256,1024]{1,0:T(8,128)(2,1)S(1)}, bf16[256,1024]{1,0:T(8,128)(2,1)}, u32[]{:S(2)}) copy-start(bf16[256,1024]{1,0:T(8,128)(2,1)} %x_ref.3) | copy-start | bytes 1572868
  1.7 0.7 copy-start.4
  38.2 20.4 %copy-start.5 = (f32[1,1024]{1,0:T(1,128)S(1)}, f32[1,1024]{1,0:T(1,128)}, u32[]{:S(2)}) copy-start(f32[1,1024]{1,0:T(1,128)} %cls_ref.3) | copy-start | bytes 12292
  54.9 12.5 %all-to-all-start.1 = ((bf16[16,64,256]{2,1,0:T(8,128)(2,1)}), bf16[16,64,256]{2,1,0:T(8,128)(2,1)S(1)}, u32[]{:S(2)}, u32[]{:S(2)}) async-start(bf16[16,64,256]{2,1,0:T(8,128)(2,1)} %attend.1), calls=%async_computation.1 | async-start | bytes 1048576 | tf_op jit(solution)/shard_map/all_to_all | solution.py:429
  58.5 8.9 %copy-start = (bf16[1024,1024]{1,0:T(8,128)(2,1)S(1)}, bf16[1024,1024]{1,0:T(8,128)(2,1)}, u32[]{:S(2)}) copy-start(bf16[1024,1024]{1,0:T(8,128)(2,1)} %wo_ref.1) | copy-start | bytes 6291460
  58.5 8.9 %copy-start.2 = (bf16[256,1024]{1,0:T(8,128)(2,1)S(1)}, bf16[256,1024]{1,0:T(8,128)(2,1)}, u32[]{:S(2)}) copy-start(bf16[256,1024]{1,0:T(8,128)(2,1)} %x_ref.3) | copy-start | bytes 1572868
  70.6 10.2 %all-to-all-start.2 = ((f32[16,16,128]{2,1,0:T(8,128)}), f32[16,16,128]{2,1,0:T(8,128)S(1)}, u32[]{:S(2)}, u32[]{:S(2)}) async-start(f32[16,16,128]{2,1,0:T(8,128)} %get-tuple-element.29), calls=%async_computation.2 | async-start | bytes 262144 | tf_op jit(solution)/shard_map/all_to_all | solution.py:429
  74.2 1.0 %copy-start.3 = (bf16[256,1024]{1,0:T(8,128)(2,1)S(1)}, bf16[256,1024]{1,0:T(8,128)(2,1)}, u32[]{:S(2)}) copy-start(bf16[256,1024]{1,0:T(8,128)(2,1)} %get-tuple-element.20.upd_hbm) | copy-start | bytes 1572868
  82.5 10.8 %all-to-all-start.3 = ((f32[16,16,128]{2,1,0:T(8,128)}), f32[16,16,128]{2,1,0:T(8,128)S(1)}, u32[]{:S(2)}, u32[]{:S(2)}) async-start(f32[16,16,128]{2,1,0:T(8,128)} %get-tuple-element.36), calls=%async_computation.3 | async-start | bytes 262144 | tf_op jit(solution)/shard_map/all_to_all | solution.py:429

commit v7 on v6

--- a/solution.py
+++ b/solution.py
@@ -21,7 +21,7 @@
 VMEM_LIMIT = 14 * 2**20
 SMALL_LIMIT = 8 * 2**20
 LARGE_LIMIT = 46 * 2**20
-PROJECT_LIMIT = 50 * 2**20
+PROJECT_LIMIT = 62 * 2**20
 
 
 def dot(a, b, dims=NN):
@@ -85,21 +85,38 @@
     return lax.rem(lax.axis_index("dp"), 2) == 1
 
 
+PARTS = ((0, 0, 16), (1, 0, 16), (2, 0, 8), (2, 8, 8))
+
+
 def project_kernel(
-    x_ref, w_hbm, cls_hbm, class_hbm, out_ref, t_ref, self_ref, base_ref, m_hbm, w_s, m_s, cls_s, sems, sem
+    x_hbm, w_hbm, cls_hbm, class_hbm, out_hbm, t_ref, self_ref, base_ref, m_hbm,
+    w_s, m_s, cls_s, x_s, out_s, sems, sem, out_sems,
 ):
-    copies = start_copies([(w_hbm.at[k], w_s.at[k], sems.at[k]) for k in range(3)])
-    x = x_ref[...]
-    for kind in range(3):
-        copies[kind].wait()
-        y = dot(x, w_s[kind])
+    def weights(p):
+        kind, head, count = PARTS[p]
+        cols = slice(head * HEAD_DIM, (head + count) * HEAD_DIM)
+        return (w_hbm.at[kind, :, cols], w_s.at[kind, :, cols], sems.at[p])
+
+    x_copy, *copies = start_copies([(x_hbm, x_s, sem), weights(0)])
+    x_copy.wait()
+    copies += start_copies([weights(1)])
+    x = x_s[...]
+    outs = []
+    for p, (kind, head, count) in enumerate(PARTS):
+        copies[p].wait()
+        if p == 0:
+            copies += start_copies([weights(2), weights(3)])
+        y = dot(x, w_s[kind, :, head * HEAD_DIM : (head + count) * HEAD_DIM])
         if kind == 0:
             y = y * (0.125 * LOG2E)
         yt = y.astype(BF16).T
-        for h in range(HEADS):
-            out_ref[h, kind * HEAD_DIM : (kind + 1) * HEAD_DIM, :] = yt[
-                h * HEAD_DIM : (h + 1) * HEAD_DIM
-            ]
+        rows = slice(kind * HEAD_DIM, (kind + 1) * HEAD_DIM)
+        for h in range(count):
+            out_s[head + h, rows, :] = yt[h * HEAD_DIM : (h + 1) * HEAD_DIM]
+        part = slice(head, head + count)
+        outs += start_copies([(out_s.at[part, rows, :], out_hbm.at[part, rows, :], out_sems.at[p])])
+    for copy in outs:
+        copy.wait()
 
     @pl.when(second_core())
     def _():
@@ -120,14 +137,17 @@
     return pl.pallas_call(
         project_kernel,
         out_shape=(jax.ShapeDtypeStruct((HEADS, 3 * HEAD_DIM, ROWS), BF16), *AHEAD_SHAPES),
-        in_specs=[RESIDENT, ANYWHERE, ANYWHERE, ANYWHERE],
-        out_specs=(RESIDENT, RESIDENT, RESIDENT, RESIDENT, ANYWHERE),
+        in_specs=[ANYWHERE] * 4,
+        out_specs=(ANYWHERE, RESIDENT, RESIDENT, RESIDENT, ANYWHERE),
         scratch_shapes=[
             pltpu.VMEM((5, D, D), BF16),
             pltpu.VMEM((D, D), BF16),
             pltpu.VMEM((1, D), F32),
+            pltpu.VMEM((ROWS, D), BF16),
+            pltpu.VMEM((HEADS, 3 * HEAD_DIM, ROWS), BF16),
             pltpu.SemaphoreType.DMA((5,)),
             pltpu.SemaphoreType.DMA(()),
+            pltpu.SemaphoreType.DMA((len(PARTS),)),
         ],
         compiler_params=pltpu.CompilerParams(vmem_limit_bytes=PROJECT_LIMIT),
         cost_estimate=pl.CostEstimate(

time: 94.9 us -> 95.4 us (level)
  Pallas kernels: 41.8 us -> 44.6 us
  local copies, waits for them, and re-layouts: 2.78 us -> 1.06 us
    pallas_call x1, Pallas kernels: 12.3 us -> 15 us  [project(): pl.pallas_call(project_kernel, out_shape=(jax.ShapeDtypeStruct((HEADS, 3...]
    unnamed x12 -> x14, local copies, waits for them, and re-layouts: 2.78 us -> 1.06 us
where the time goes in v7:
time: 95.4 us; the launch traced here: 94.9 us
  Pallas kernels  44.6 us (47%)
  blocking collectives  23 us (24%)
  waiting for transfers between devices  14.2 us (15%)
  starting transfers between devices  11.2 us (12%)
  local copies, waits for them, and re-layouts  1.06 us (1%)
    all_to_all x1, blocking collectives, exchange(): return lax.all_to_all(blocks, 'patch', 0, 0)  23 us
    pallas_call x1, Pallas kernels, attend(): pl.pallas_call(attend_kernel, out_shape=jax.ShapeDtypeStruct((HEADS, HEAD...  16.8 us
    pallas_call x1, Pallas kernels, project(): pl.pallas_call(project_kernel, out_shape=(jax.ShapeDtypeStruct((HEADS, 3...  15 us
    all_to_all x3, waiting for transfers between devices, exchange(): return lax.all_to_all(blocks, 'patch', 0, 0)  14.2 us
    pallas_call x5, Pallas kernels, call(): pl.pallas_call(kernel, out_shape=out_shape, in_specs=[RESIDENT] * len(res...  12.5 us
    all_to_all x3, starting transfers between devices, exchange(): return lax.all_to_all(blocks, 'patch', 0, 0)  11.2 us
  transfers between devices with their start and end apart: 3, of which 3 were waited for; matrix products, arithmetic and copies ran while one was open for 0% of the time, Pallas kernels for 7%

profile of v7, /device:TPU:1, one launch (start us, length us, event | category | flops | bytes accessed | tf_op | source)
XLA Modules:
  0.0 94.9 jit_solution(13956739696916999087)
XLA Ops:
  0.6 15.0 %project.1 = (bf16[16,192,256]{2,1,0:T(8,128)(2,1)}, bf16[32,1024]{1,0:T(8,128)(2,1)}, f32[16,128]{1,0:T(8,128)}, f32[1,1024]{1,0:T(1,128)}, bf16[3,1024,1024]{2,1,0:T(8,128)(2,1)}) custom-call(bf16[256,1024]{1,0:T(8,128)(2,1)} %x_ref.1, bf16[3,1024,1024]{2,1,0:T(8,128)(2,1)} %w_hbm.5, f32[1,1024]{1,0:T(1,128)} %cls_ref.3, bf16[2,4,1024,1024]{3,2,1,0:T(8,128)(2,1)} %w_hbm.9), custom_call_target="tpu_custom_call" | custom-call | flops 1610612736 | bytes 8388608 | tf_op jit(solution)/shard_map/project/pallas_call | solution.py:137
  15.6 23.0 %all_to_all.20.qkv_ref = bf16[16,192,256]{2,1,0:T(8,128)(2,1)S(1)} all-to-all(bf16[16,192,256]{2,1,0:T(8,128)(2,1)} %get-tuple-element.22), channel_id=1, replica_groups=mesh['dp'=8,'patch'=16] {'patch'}, dimensions={0} | all-to-all | bytes 3145728 | tf_op jit(solution)/shard_map/all_to_all | solution.py:449
  38.7 0.0 copy-start.3
  38.7 0.0 copy-start.4
  38.7 0.0 copy-start.5
  38.7 0.0 copy-start.6
  38.7 16.8 %attend.1 = bf16[16,64,256]{2,1,0:T(8,128)(2,1)} custom-call(bf16[16,192,256]{2,1,0:T(8,128)(2,1)S(1)} %all_to_all.20.qkv_ref), custom_call_target="tpu_custom_call" | custom-call | flops 17179869184 | bytes 2097152 | tf_op jit(solution)/shard_map/attend/pallas_call | solution.py:213
  55.5 3.6 %all-to-all-start.1 = ((bf16[16,64,256]{2,1,0:T(8,128)(2,1)}), bf16[16,64,256]{2,1,0:T(8,128)(2,1)S(1)}, u32[]{:S(2)}, u32[]{:S(2)}) async-start(bf16[16,64,256]{2,1,0:T(8,128)(2,1)} %attend.1), calls=%async_computation.1 | async-start | bytes 1048576 | tf_op jit(solution)/shard_map/all_to_all | solution.py:449
  59.1 0.0 copy-done.3
  59.1 0.0 copy-done.4
  59.1 0.0 copy-done.5
  59.1 0.0 copy-done.6
  59.1 0.0 copy-start
  59.1 0.0 copy-start.1
  59.1 0.3 ahead.1
  59.4 8.6 %all-to-all-done.1.ret_ref = bf16[16,64,256]{2,1,0:T(8,128)(2,1)S(1)} async-done(((bf16[16,64,256]{2,1,0:T(8,128)(2,1)}), bf16[16,64,256]{2,1,0:T(8,128)(2,1)S(1)}, u32[]{:S(2)}, u32[]{:S(2)}) %all-to-all-start.1) | async-done | bytes 524320 | tf_op jit(solution)/shard_map/all_to_all | solution.py:449
  68.0 0.0 copy-done
  68.0 0.0 copy-done.1
  68.0 3.2 %update.1 = (bf16[256,1024]{1,0:T(8,128)(2,1)}, f32[16,16,128]{2,1,0:T(8,128)}) custom-call(bf16[16,64,256]{2,1,0:T(8,128)(2,1)S(1)} %all-to-all-done.1.ret_ref, bf16[256,1024]{1,0:T(8,128)(2,1)S(1)} %copy-done.1, bf16[32,1024]{1,0:T(8,128)(2,1)S(1)} %get-tuple-element.27.t_ref, bf16[1024,1024]{1,0:T(8,128)(2,1)S(1)} %copy-done, bf16[2,4,1024,1024]{3,2,1,0:T(8,128)(2,1)} %w_hbm.9), custom_call_target="tpu_custom_call" | custom-call | flops 1073741824 | bytes 1048576 | tf_op jit(solution)/shard_map/update/pallas_call | solution.py:39
  71.2 3.5 %all-to-all-start.2 = ((f32[16,16,128]{2,1,0:T(8,128)}), f32[16,16,128]{2,1,0:T(8,128)S(1)}, u32[]{:S(2)}, u32[]{:S(2)}) async-start(f32[16,16,128]{2,1,0:T(8,128)} %get-tuple-element.29), calls=%async_computation.2 | async-start | bytes 262144 | tf_op jit(solution)/shard_map/all_to_all | solution.py:449
  74.7 0.0 copy-start.2
  74.7 1.0 %copy-done.2 = bf16[256,1024]{1,0:T(8,128)(2,1)S(1)} copy-done((bf16[256,1024]{1,0:T(8,128)(2,1)S(1)}, bf16[256,1024]{1,0:T(8,128)(2,1)}, u32[]{:S(2)}) %copy-start.2) | copy-done | bytes 524312
  75.8 3.1 %class_kv.1 = (bf16[256,1024]{1,0:T(8,128)(2,1)S(1)}, bf16[256,1024]{1,0:T(8,128)(2,1)S(1)}, bf16[1024,1024]{1,0:T(8,128)(2,1)S(1)}) custom-call(bf16[256,1024]{1,0:T(8,128)(2,1)S(1)} %copy-done.2, bf16[2,4,1024,1024]{3,2,1,0:T(8,128)(2,1)} %w_hbm.9, bf16[3,1024,1024]{2,1,0:T(8,128)(2,1)} %get-tuple-element.32.m_hbm), custom_call_target="tpu_custom_call" | custom-call | flops 2147483648 | bytes 1048576 | tf_op jit(solution)/shard_map/class_kv/pallas_call | solution.py:39
  78.9 2.5 %all-to-all-done.2.parts_ref = f32[16,16,128]{2,1,0:T(8,128)S(1)} async-done(((f32[16,16,128]{2,1,0:T(8,128)}), f32[16,16,128]{2,1,0:T(8,128)S(1)}, u32[]{:S(2)}, u32[]{:S(2)}) %all-to-all-start.2) | async-done | bytes 131104 | tf_op jit(solution)/shard_map/all_to_all | solution.py:449
  81.4 1.7 %middle.1 = (f32[1,1024]{1,0:T(1,128)S(1)}, f32[1,1024]{1,0:T(1,128)S(1)}, f32[16,16,128]{2,1,0:T(8,128)}) custom-call(f32[16,16,128]{2,1,0:T(8,128)S(1)} %all-to-all-done.2.parts_ref, f32[16,128]{1,0:T(8,128)S(1)} %get-tuple-element.30.self_ref, f32[1,1024]{1,0:T(1,128)S(1)} %get-tuple-element.31.base_ref, bf16[1024,1024]{1,0:T(8,128)(2,1)S(1)} %get-tuple-element.33.m_ref, ...), custom_call_target="tpu_custom_call" | custom-call | flops 268435456 | bytes 1048576 | tf_op jit(solution)/shard_map/middle/pallas_call | solution.py:39
  83.0 4.1 %all-to-all-start.3 = ((f32[16,16,128]{2,1,0:T(8,128)}), f32[16,16,128]{2,1,0:T(8,128)S(1)}, u32[]{:S(2)}, u32[]{:S(2)}) async-start(f32[16,16,128]{2,1,0:T(8,128)} %get-tuple-element.36), calls=%async_computation.3 | async-start | bytes 262144 | tf_op jit(solution)/shard_map/all_to_all | solution.py:449
  87.2 3.6 %self_part.1 = (f32[16,128]{1,0:T(8,128)S(1)}, f32[1,1024]{1,0:T(1,128)S(1)}, bf16[1024,1024]{1,0:T(8,128)(2,1)S(1)}) custom-call(f32[1,1024]{1,0:T(1,128)S(1)} %copy-done.4, f32[1,1024]{1,0:T(1,128)S(1)} %get-tuple-element.37.attn_ref, f32[1,1024]{1,0:T(1,128)S(1)} %get-tuple-element.38.q_ref, bf16[2,4,1024,1024]{3,2,1,0:T(8,128)(2,1)} %w_hbm.9), custom_call_target="tpu_custom_call" | custom-call | flops 1073741824 | bytes 1048576 | tf_op jit(solution)/shard_map/self_part/pallas_call | solution.py:39
  90.7 3.1 %all-to-all-done.3.parts_ref = f32[16,16,128]{2,1,0:T(8,128)S(1)} async-done(((f32[16,16,128]{2,1,0:T(8,128)}), f32[16,16,128]{2,1,0:T(8,128)S(1)}, u32[]{:S(2)}, u32[]{:S(2)}) %all-to-all-start.3) | async-done | bytes 131104 | tf_op jit(solution)/shard_map/all_to_all | solution.py:449
  93.8 1.0 %last.1 = f32[1,1024]{1,0:T(1,128)} custom-call(f32[16,16,128]{2,1,0:T(8,128)S(1)} %all-to-all-done.3.parts_ref, f32[16,128]{1,0:T(8,128)S(1)} %get-tuple-element.39.self_ref, f32[1,1024]{1,0:T(1,128)S(1)} %get-tuple-element.40.cls_ref, bf16[1024,1024]{1,0:T(8,128)(2,1)S(1)} %get-tuple-element.41.wo_ref), custom_call_target="tpu_custom_call" | custom-call | flops 134217728 | bytes 1048576 | tf_op jit(solution)/shard_map/last/pallas_call | solution.py:39
Async XLA Ops:
  38.7 20.4 %copy-start.3 = (bf16[32,1024]{1,0:T(8,128)(2,1)S(1)}, bf16[32,1024]{1,0:T(8,128)(2,1)}, u32[]{:S(2)}) copy-start(bf16[32,1024]{1,0:T(8,128)(2,1)} %get-tuple-element.23.t_in) | copy-start | bytes 196612
  38.7 20.4 %copy-start.4 = (f32[1,1024]{1,0:T(1,128)S(1)}, f32[1,1024]{1,0:T(1,128)}, u32[]{:S(2)}) copy-start(f32[1,1024]{1,0:T(1,128)} %cls_ref.3) | copy-start | bytes 12292
  38.7 20.4 %copy-start.5 = (f32[16,128]{1,0:T(8,128)S(1)}, f32[16,128]{1,0:T(8,128)}, u32[]{:S(2)}) copy-start(f32[16,128]{1,0:T(8,128)} %get-tuple-element.24.self_in) | copy-start | bytes 24580
  38.7 20.4 %copy-start.6 = (f32[1,1024]{1,0:T(1,128)S(1)}, f32[1,1024]{1,0:T(1,128)}, u32[]{:S(2)}) copy-start(f32[1,1024]{1,0:T(1,128)} %get-tuple-element.25.base_in) | copy-start | bytes 12292
  55.5 12.5 %all-to-all-start.1 = ((bf16[16,64,256]{2,1,0:T(8,128)(2,1)}), bf16[16,64,256]{2,1,0:T(8,128)(2,1)S(1)}, u32[]{:S(2)}, u32[]{:S(2)}) async-start(bf16[16,64,256]{2,1,0:T(8,128)(2,1)} %attend.1), calls=%async_computation.1 | async-start | bytes 1048576 | tf_op jit(solution)/shard_map/all_to_all | solution.py:449
  59.1 8.9 %copy-start = (bf16[1024,1024]{1,0:T(8,128)(2,1)S(1)}, bf16[1024,1024]{1,0:T(8,128)(2,1)}, u32[]{:S(2)}) copy-start(bf16[1024,1024]{1,0:T(8,128)(2,1)} %wo_ref.1) | copy-start | bytes 6291460
  59.1 8.9 %copy-start.1 = (bf16[256,1024]{1,0:T(8,128)(2,1)S(1)}, bf16[256,1024]{1,0:T(8,128)(2,1)}, u32[]{:S(2)}) copy-start(bf16[256,1024]{1,0:T(8,128)(2,1)} %x_ref.1) | copy-start | bytes 1572868
  71.2 10.2 %all-to-all-start.2 = ((f32[16,16,128]{2,1,0:T(8,128)}), f32[16,16,128]{2,1,0:T(8,128)S(1)}, u32[]{:S(2)}, u32[]{:S(2)}) async-start(f32[16,16,128]{2,1,0:T(8,128)} %get-tuple-element.29), calls=%async_computation.2 | async-start | bytes 262144 | tf_op jit(solution)/shard_map/all_to_all | solution.py:449
  74.7 1.0 %copy-start.2 = (bf16[256,1024]{1,0:T(8,128)(2,1)S(1)}, bf16[256,1024]{1,0:T(8,128)(2,1)}, u32[]{:S(2)}) copy-start(bf16[256,1024]{1,0:T(8,128)(2,1)} %get-tuple-element.20.upd_hbm) | copy-start | bytes 1572868
  83.0 10.8 %all-to-all-start.3 = ((f32[16,16,128]{2,1,0:T(8,128)}), f32[16,16,128]{2,1,0:T(8,128)S(1)}, u32[]{:S(2)}, u32[]{:S(2)}) async-start(f32[16,16,128]{2,1,0:T(8,128)} %get-tuple-element.36), calls=%async_computation.3 | async-start | bytes 262144 | tf_op jit(solution)/shard_map/all_to_all | solution.py:449

commit v8 on v6

--- a/solution.py
+++ b/solution.py
@@ -88,10 +88,12 @@
 def project_kernel(
     x_ref, w_hbm, cls_hbm, class_hbm, out_ref, t_ref, self_ref, base_ref, m_hbm, w_s, m_s, cls_s, sems, sem
 ):
-    copies = start_copies([(w_hbm.at[k], w_s.at[k], sems.at[k]) for k in range(3)])
+    copies = start_copies([(w_hbm.at[k], w_s.at[k], sems.at[k]) for k in range(2)])
     x = x_ref[...]
     for kind in range(3):
         copies[kind].wait()
+        if kind == 0:
+            copies += start_copies([(w_hbm.at[2], w_s.at[2], sems.at[2])])
         y = dot(x, w_s[kind])
         if kind == 0:
             y = y * (0.125 * LOG2E)

time: 94.9 us -> 95 us (level)
  no operation moved by 1% of the time
where the time goes in v8:
time: 95 us; the launch traced here: 94.5 us
  Pallas kernels  42 us (44%)
  blocking collectives  23.5 us (25%)
  waiting for transfers between devices  14.2 us (15%)
  starting transfers between devices  11.2 us (12%)
  local copies, waits for them, and re-layouts  2.78 us (3%)
    all_to_all x1, blocking collectives, exchange(): return lax.all_to_all(blocks, 'patch', 0, 0)  23.5 us
    pallas_call x1, Pallas kernels, attend(): pl.pallas_call(attend_kernel, out_shape=jax.ShapeDtypeStruct((HEADS, HEAD...  16.7 us
    all_to_all x3, waiting for transfers between devices, exchange(): return lax.all_to_all(blocks, 'patch', 0, 0)  14.2 us
    pallas_call x5, Pallas kernels, call(): pl.pallas_call(kernel, out_shape=out_shape, in_specs=[RESIDENT] * len(res...  12.5 us
    pallas_call x1, Pallas kernels, project(): pl.pallas_call(project_kernel, out_shape=(jax.ShapeDtypeStruct((HEADS, 3...  12.5 us
    all_to_all x3, starting transfers between devices, exchange(): return lax.all_to_all(blocks, 'patch', 0, 0)  11.2 us
    unnamed x12, local copies, waits for them, and re-layouts  2.78 us
  transfers between devices with their start and end apart: 3, of which 3 were waited for; matrix products, arithmetic and copies ran while one was open for 0% of the time, Pallas kernels for 7%

profile of v8, /device:TPU:1, one launch (start us, length us, event | category | flops | bytes accessed | tf_op | source)
XLA Modules:
  0.0 94.5 jit_solution(4334380324830593355)
XLA Ops:
  0.6 0.0 copy-start.1
  0.6 1.0 %copy-done.1 = bf16[256,1024]{1,0:T(8,128)(2,1)S(1)} copy-done((bf16[256,1024]{1,0:T(8,128)(2,1)S(1)}, bf16[256,1024]{1,0:T(8,128)(2,1)}, u32[]{:S(2)}) %copy-start.1) | copy-done | bytes 524312
  1.7 0.0 copy-start.4
  1.7 0.7 copy-done.4
  2.4 12.5 %project.1 = (bf16[16,192,256]{2,1,0:T(8,128)(2,1)S(1)}, bf16[32,1024]{1,0:T(8,128)(2,1)S(1)}, f32[16,128]{1,0:T(8,128)S(1)}, f32[1,1024]{1,0:T(1,128)S(1)}, bf16[3,1024,1024]{2,1,0:T(8,128)(2,1)}) custom-call(bf16[256,1024]{1,0:T(8,128)(2,1)S(1)} %copy-done.1, bf16[3,1024,1024]{2,1,0:T(8,128)(2,1)} %w_hbm.5, f32[1,1024]{1,0:T(1,128)S(1)} %copy-done.4, ...), custom_call_target="tpu_custom_call" | custom-call | flops 1610612736 | bytes 8388608 | tf_op jit(solution)/shard_map/project/pallas_call | solution.py:122
  14.8 23.5 %all_to_all.20.qkv_ref = bf16[16,192,256]{2,1,0:T(8,128)(2,1)S(1)} all-to-all(bf16[16,192,256]{2,1,0:T(8,128)(2,1)S(1)} %get-tuple-element.22), channel_id=1, replica_groups=mesh['dp'=8,'patch'=16] {'patch'}, dimensions={0} | all-to-all | bytes 3145728 | tf_op jit(solution)/shard_map/all_to_all | solution.py:431
  38.3 0.0 copy-start.5
  38.3 16.7 %attend.1 = bf16[16,64,256]{2,1,0:T(8,128)(2,1)} custom-call(bf16[16,192,256]{2,1,0:T(8,128)(2,1)S(1)} %all_to_all.20.qkv_ref), custom_call_target="tpu_custom_call" | custom-call | flops 17179869184 | bytes 2097152 | tf_op jit(solution)/shard_map/attend/pallas_call | solution.py:195
  55.1 3.6 %all-to-all-start.1 = ((bf16[16,64,256]{2,1,0:T(8,128)(2,1)}), bf16[16,64,256]{2,1,0:T(8,128)(2,1)S(1)}, u32[]{:S(2)}, u32[]{:S(2)}) async-start(bf16[16,64,256]{2,1,0:T(8,128)(2,1)} %attend.1), calls=%async_computation.1 | async-start | bytes 1048576 | tf_op jit(solution)/shard_map/all_to_all | solution.py:431
  58.7 0.0 copy-done.5
  58.7 0.0 copy-start
  58.7 0.0 copy-start.2
  58.7 0.3 ahead.1
  59.0 8.6 %all-to-all-done.1.ret_ref = bf16[16,64,256]{2,1,0:T(8,128)(2,1)S(1)} async-done(((bf16[16,64,256]{2,1,0:T(8,128)(2,1)}), bf16[16,64,256]{2,1,0:T(8,128)(2,1)S(1)}, u32[]{:S(2)}, u32[]{:S(2)}) %all-to-all-start.1) | async-done | bytes 524320 | tf_op jit(solution)/shard_map/all_to_all | solution.py:431
  67.6 0.0 copy-done
  67.6 0.0 copy-done.2
  67.6 3.2 %update.1 = (bf16[256,1024]{1,0:T(8,128)(2,1)}, f32[16,16,128]{2,1,0:T(8,128)}) custom-call(bf16[16,64,256]{2,1,0:T(8,128)(2,1)S(1)} %all-to-all-done.1.ret_ref, bf16[256,1024]{1,0:T(8,128)(2,1)S(1)} %copy-done.2, bf16[32,1024]{1,0:T(8,128)(2,1)S(1)} %get-tuple-element.27.t_ref, bf16[1024,1024]{1,0:T(8,128)(2,1)S(1)} %copy-done, bf16[2,4,1024,1024]{3,2,1,0:T(8,128)(2,1)} %w_hbm.9), custom_call_target="tpu_custom_call" | custom-call | flops 1073741824 | bytes 1048576 | tf_op jit(solution)/shard_map/update/pallas_call | solution.py:39
  70.8 3.5 %all-to-all-start.2 = ((f32[16,16,128]{2,1,0:T(8,128)}), f32[16,16,128]{2,1,0:T(8,128)S(1)}, u32[]{:S(2)}, u32[]{:S(2)}) async-start(f32[16,16,128]{2,1,0:T(8,128)} %get-tuple-element.29), calls=%async_computation.2 | async-start | bytes 262144 | tf_op jit(solution)/shard_map/all_to_all | solution.py:431
  74.3 0.0 copy-start.3
  74.4 1.0 %copy-done.3 = bf16[256,1024]{1,0:T(8,128)(2,1)S(1)} copy-done((bf16[256,1024]{1,0:T(8,128)(2,1)S(1)}, bf16[256,1024]{1,0:T(8,128)(2,1)}, u32[]{:S(2)}) %copy-start.3) | copy-done | bytes 524312
  75.4 3.1 %class_kv.1 = (bf16[256,1024]{1,0:T(8,128)(2,1)S(1)}, bf16[256,1024]{1,0:T(8,128)(2,1)S(1)}, bf16[1024,1024]{1,0:T(8,128)(2,1)S(1)}) custom-call(bf16[256,1024]{1,0:T(8,128)(2,1)S(1)} %copy-done.3, bf16[2,4,1024,1024]{3,2,1,0:T(8,128)(2,1)} %w_hbm.9, bf16[3,1024,1024]{2,1,0:T(8,128)(2,1)} %get-tuple-element.32.m_hbm), custom_call_target="tpu_custom_call" | custom-call | flops 2147483648 | bytes 1048576 | tf_op jit(solution)/shard_map/class_kv/pallas_call | solution.py:39
  78.5 2.5 %all-to-all-done.2.parts_ref = f32[16,16,128]{2,1,0:T(8,128)S(1)} async-done(((f32[16,16,128]{2,1,0:T(8,128)}), f32[16,16,128]{2,1,0:T(8,128)S(1)}, u32[]{:S(2)}, u32[]{:S(2)}) %all-to-all-start.2) | async-done | bytes 131104 | tf_op jit(solution)/shard_map/all_to_all | solution.py:431
  81.0 1.7 %middle.1 = (f32[1,1024]{1,0:T(1,128)S(1)}, f32[1,1024]{1,0:T(1,128)S(1)}, f32[16,16,128]{2,1,0:T(8,128)}) custom-call(f32[16,16,128]{2,1,0:T(8,128)S(1)} %all-to-all-done.2.parts_ref, f32[16,128]{1,0:T(8,128)S(1)} %get-tuple-element.30.self_ref, f32[1,1024]{1,0:T(1,128)S(1)} %get-tuple-element.31.base_ref, bf16[1024,1024]{1,0:T(8,128)(2,1)S(1)} %get-tuple-element.33.m_ref, ...), custom_call_target="tpu_custom_call" | custom-call | flops 268435456 | bytes 1048576 | tf_op jit(solution)/shard_map/middle/pallas_call | solution.py:39
  82.6 4.1 %all-to-all-start.3 = ((f32[16,16,128]{2,1,0:T(8,128)}), f32[16,16,128]{2,1,0:T(8,128)S(1)}, u32[]{:S(2)}, u32[]{:S(2)}) async-start(f32[16,16,128]{2,1,0:T(8,128)} %get-tuple-element.36), calls=%async_computation.3 | async-start | bytes 262144 | tf_op jit(solution)/shard_map/all_to_all | solution.py:431
  86.7 3.6 %self_part.1 = (f32[16,128]{1,0:T(8,128)S(1)}, f32[1,1024]{1,0:T(1,128)S(1)}, bf16[1024,1024]{1,0:T(8,128)(2,1)S(1)}) custom-call(f32[1,1024]{1,0:T(1,128)S(1)} %copy-done.5, f32[1,1024]{1,0:T(1,128)S(1)} %get-tuple-element.37.attn_ref, f32[1,1024]{1,0:T(1,128)S(1)} %get-tuple-element.38.q_ref, bf16[2,4,1024,1024]{3,2,1,0:T(8,128)(2,1)} %w_hbm.9), custom_call_target="tpu_custom_call" | custom-call | flops 1073741824 | bytes 1048576 | tf_op jit(solution)/shard_map/self_part/pallas_call | solution.py:39
  90.3 3.1 %all-to-all-done.3.parts_ref = f32[16,16,128]{2,1,0:T(8,128)S(1)} async-done(((f32[16,16,128]{2,1,0:T(8,128)}), f32[16,16,128]{2,1,0:T(8,128)S(1)}, u32[]{:S(2)}, u32[]{:S(2)}) %all-to-all-start.3) | async-done | bytes 131104 | tf_op jit(solution)/shard_map/all_to_all | solution.py:431
  93.4 1.0 %last.1 = f32[1,1024]{1,0:T(1,128)} custom-call(f32[16,16,128]{2,1,0:T(8,128)S(1)} %all-to-all-done.3.parts_ref, f32[16,128]{1,0:T(8,128)S(1)} %get-tuple-element.39.self_ref, f32[1,1024]{1,0:T(1,128)S(1)} %get-tuple-element.40.cls_ref, bf16[1024,1024]{1,0:T(8,128)(2,1)S(1)} %get-tuple-element.41.wo_ref), custom_call_target="tpu_custom_call" | custom-call | flops 134217728 | bytes 1048576 | tf_op jit(solution)/shard_map/last/pallas_call | solution.py:39
Async XLA Ops:
  0.6 1.0 %copy-start.1 = (bf16[256,1024]{1,0:T(8,128)(2,1)S(1)}, bf16[256,1024]{1,0:T(8,128)(2,1)}, u32[]{:S(2)}) copy-start(bf16[256,1024]{1,0:T(8,128)(2,1)} %x_ref.3) | copy-start | bytes 1572868
  1.7 0.7 copy-start.4
  38.3 20.4 %copy-start.5 = (f32[1,1024]{1,0:T(1,128)S(1)}, f32[1,1024]{1,0:T(1,128)}, u32[]{:S(2)}) copy-start(f32[1,1024]{1,0:T(1,128)} %cls_ref.3) | copy-start | bytes 12292
  55.1 12.5 %all-to-all-start.1 = ((bf16[16,64,256]{2,1,0:T(8,128)(2,1)}), bf16[16,64,256]{2,1,0:T(8,128)(2,1)S(1)}, u32[]{:S(2)}, u32[]{:S(2)}) async-start(bf16[16,64,256]{2,1,0:T(8,128)(2,1)} %attend.1), calls=%async_computation.1 | async-start | bytes 1048576 | tf_op jit(solution)/shard_map/all_to_all | solution.py:431
  58.7 8.9 %copy-start = (bf16[1024,1024]{1,0:T(8,128)(2,1)S(1)}, bf16[1024,1024]{1,0:T(8,128)(2,1)}, u32[]{:S(2)}) copy-start(bf16[1024,1024]{1,0:T(8,128)(2,1)} %wo_ref.1) | copy-start | bytes 6291460
  58.7 8.9 %copy-start.2 = (bf16[256,1024]{1,0:T(8,128)(2,1)S(1)}, bf16[256,1024]{1,0:T(8,128)(2,1)}, u32[]{:S(2)}) copy-start(bf16[256,1024]{1,0:T(8,128)(2,1)} %x_ref.3) | copy-start | bytes 1572868
  70.8 10.2 %all-to-all-start.2 = ((f32[16,16,128]{2,1,0:T(8,128)}), f32[16,16,128]{2,1,0:T(8,128)S(1)}, u32[]{:S(2)}, u32[]{:S(2)}) async-start(f32[16,16,128]{2,1,0:T(8,128)} %get-tuple-element.29), calls=%async_computation.2 | async-start | bytes 262144 | tf_op jit(solution)/shard_map/all_to_all | solution.py:431
  74.3 1.0 %copy-start.3 = (bf16[256,1024]{1,0:T(8,128)(2,1)S(1)}, bf16[256,1024]{1,0:T(8,128)(2,1)}, u32[]{:S(2)}) copy-start(bf16[256,1024]{1,0:T(8,128)(2,1)} %get-tuple-element.20.upd_hbm) | copy-start | bytes 1572868
  82.6 10.8 %all-to-all-start.3 = ((f32[16,16,128]{2,1,0:T(8,128)}), f32[16,16,128]{2,1,0:T(8,128)S(1)}, u32[]{:S(2)}, u32[]{:S(2)}) async-start(f32[16,16,128]{2,1,0:T(8,128)} %get-tuple-element.36), calls=%async_computation.3 | async-start | bytes 262144 | tf_op jit(solution)/shard_map/all_to_all | solution.py:431
